TPU v7x, 32 devices: a whole 2x2x4 slice. The times are simulated.
32 devices in a mesh: row: 4 (over x, core), col: 8 (over z, y).
Axes of the slice: x: 2, y: 2, z: 4, core: 2. Of those that a mesh axis runs over, the one named last changes fastest.
Arguments:
- kernel: float32 [16384, 16384], P('row', 'col'), may hold values from 0 to 20, as said below
Outputs:
- factored: float32 [16384, 16384], P('row', 'col')
Inputs may be any that keep to these rules, and one draw needn't show every extreme that they name: `kernel`: in logical order K is symmetric and positive definite.
All inputs are finite; a program needn't handle non-finite values.
Results may differ from a plain program's by a relative error of at most 0.0003.
Values sent between devices are 32-bit elements; how exact they have to be, the bound alone decides.
No kernel may reach another device: no remote copies, remote signals or barrier semaphores. Data moves between devices by JAX's collectives and lax.ppermute only.
A program may use at most 192 MiB of HBM per device.

v0:
```python
import jax
import jax.numpy as jnp
from jax import lax
from jax.sharding import PartitionSpec as P

NB = 512


def from_root(value, axis, source):
    kept = jnp.where(lax.axis_index(axis) == source, value, 0).astype(value.dtype)
    return lax.psum(kept, axis)


def make_panel(corner, column, row_global, section_index):
    factor = jnp.linalg.cholesky(corner)
    solved = jax.scipy.linalg.solve_triangular(factor, column.T, lower=True).T
    tiled = jnp.tile(factor, (column.shape[0] // NB, 1))
    chosen = jnp.where((row_global == section_index)[:, None], tiled, jnp.zeros_like(solved))
    return jnp.where((row_global > section_index)[:, None], solved, chosen)


def on_device(kernel):
    rows_axis = lax.axis_size("row")
    cols_axis = lax.axis_size("col")
    local_rows = kernel.shape[0]
    col_blocks = kernel.shape[1] // NB
    row_global = jnp.repeat(jnp.arange(local_rows // NB) * rows_axis + lax.axis_index("row"), NB)
    col_global = jnp.repeat(jnp.arange(col_blocks) * cols_axis + lax.axis_index("col"), NB)
    matrix = kernel
    home_row = 0 % rows_axis
    row_slot = 0 // rows_axis
    home_col = 0 % cols_axis
    col_slot = 0 // cols_axis
    corner = matrix[row_slot * NB : (row_slot + 1) * NB, col_slot * NB : (col_slot + 1) * NB]
    column = matrix[:, col_slot * NB : (col_slot + 1) * NB]
    corner = from_root(corner, ("row", "col"), home_row * cols_axis + home_col)
    column = from_root(column, "col", home_col)
    panel_block = make_panel(corner, column, row_global, 0)
    trailing = jnp.where((row_global > 0)[:, None], panel_block, jnp.zeros_like(panel_block))
    pieces = []
    for block_slot in range(col_blocks):
        col_target = block_slot * cols_axis + lax.axis_index("col")
        source_row = col_target % rows_axis
        source_slot = col_target // rows_axis
        piece = lax.dynamic_slice_in_dim(trailing, source_slot * NB, NB, 0)
        pieces.append(from_root(piece, "row", source_row))
    across = jnp.concatenate(pieces, 0)
    update = lax.dot_general(
        trailing, across, (((1,), (1,)), ((), ())), precision=lax.Precision.HIGHEST
    )
    matrix = matrix - update
    matrix = jnp.where((col_global == 0)[None, :], jnp.tile(panel_block, (1, col_blocks)), matrix)
    upper_mask = (row_global == 0)[:, None] & (col_global > 0)[None, :]
    matrix = jnp.where(upper_mask, jnp.zeros_like(matrix), matrix)
    return matrix


def solution(mesh):
    in_specs = (P("row", "col"),)
    out_specs = P("row", "col")
    return jax.shard_map(
        on_device, mesh=mesh, in_specs=in_specs, out_specs=out_specs, check_vma=False
    )
```

profile of v0, /device:TPU:0, one launch (start us, length us, event | category | flops | bytes accessed | tf_op | source)
XLA Modules:
  0.0 670.6 jit_solution(8196646630702163790)
XLA Ops:
  6.5 1.3 slice.120
  8.2 1.1 broadcast_select_fusion.1
  9.4 7.8 %slice.121 = f32[4096,512]{1,0:T(8,128)} slice(f32[4096,2048]{1,0:T(8,128)} %param.1), slice={[0:4096], [0:512]} | slice | bytes 16777216 | tf_op jit(solution)/shard_map/slice | solution.py:35
  17.1 9.0 %copy.18 = f32[4096,512]{0,1:T(8,128)} copy(f32[4096,512]{1,0:T(8,128)} %slice.121) | data formatting | bytes 16777216
  26.1 7.7 %select_bitcast_fusion = f32[512,4096]{1,0:T(8,128)} fusion(f32[4096,512]{0,1:T(8,128)} %copy.18, pred[]{:T(512)S(6)} %eq.51), kind=kLoop, calls=%fused_computation.5 | loop fusion | flops 2097152 | bytes 16777216 | tf_op jit(solution)/shard_map/transpose | solution.py:16
  34.4 110.7 %all-reduce.6.cloned.1.call-done = f32[512,512]{0,1:T(8,128)} async-done(((f32[512,512]{0,1:T(8,128)}), f32[512,512]{0,1:T(8,128)}) %all-reduce.6.cloned.1.call-update) | async-done | bytes 1048592 | tf_op jit(solution)/shard_map/psum | solution.py:11
  145.1 1.6 copy.3
  146.6 1.4 fusion.22
  148.1 11.7 %cholesky.103 = f32[128,128]{1,0:T(8,128)S(1)} custom-call(f32[128,128]{1,0:T(8,128)S(1)} %cholesky.263), custom_call_target="Cholesky" | custom-call | tf_op jit(solution)/shard_map/jit(cholesky)/cholesky | solution.py:15
  159.9 9.8 %custom-call.31 = f32[1,128,128]{1,2,0:T(8,128)S(1)} custom-call(f32[1,128,128]{2,1,0:T(8,128)S(1)} %get-tuple-element.44), custom_call_target="InvertDiagBlocksLowerTriangular" | custom-call | tf_op jit(solution)/shard_map/jit(cholesky)/cholesky | solution.py:15
  170.6 11.7 %cholesky.215 = f32[128,128]{1,0:T(8,128)S(1)} custom-call(f32[128,128]{1,0:T(8,128)S(1)} %cholesky.267), custom_call_target="Cholesky" | custom-call | tf_op jit(solution)/shard_map/jit(cholesky)/cholesky | solution.py:15
  182.4 10.2 %custom-call.32 = f32[1,128,128]{1,2,0:T(8,128)S(1)} custom-call(f32[1,128,128]{2,1,0:T(8,128)S(1)} %get-tuple-element.42), custom_call_target="InvertDiagBlocksLowerTriangular" | custom-call | tf_op jit(solution)/shard_map/jit(cholesky)/cholesky | solution.py:15
  193.1 0.6 convolution_subtract_fusion.3
  193.7 11.7 %cholesky.236 = f32[128,128]{1,0:T(8,128)S(1)} custom-call(f32[128,128]{1,0:T(8,128)S(1)} %cholesky.272), custom_call_target="Cholesky" | custom-call | tf_op jit(solution)/shard_map/jit(cholesky)/cholesky | solution.py:15
  205.6 9.8 %custom-call.33 = f32[1,128,128]{1,2,0:T(8,128)S(1)} custom-call(f32[1,128,128]{2,1,0:T(8,128)S(1)} %get-tuple-element.40), custom_call_target="InvertDiagBlocksLowerTriangular" | custom-call | tf_op jit(solution)/shard_map/jit(cholesky)/cholesky | solution.py:15
  215.7 0.5 convolution_subtract_fusion.4
  216.2 11.9 %cholesky.253 = f32[128,128]{1,0:T(8,128)S(1)} custom-call(f32[128,128]{1,0:T(8,128)S(1)} %convolution_subtract_fusion.4), custom_call_target="Cholesky" | custom-call | tf_op jit(solution)/shard_map/jit(cholesky)/cholesky | solution.py:15
  228.1 0.6 compare_reduce_fusion.2
  230.0 0.6 compare_reduce_fusion.1
  231.3 0.6 compare_reduce_fusion
  232.9 8.1 %while.1 = (s32[]{:T(128)}, f32[512,512]{0,1:T(8,128)S(1)}, s32[4,2]{0,1:T(2,128)S(1)}, f32[4,128,128]{2,1,0:T(8,128)S(1)}, s32[]{:T(128)}) while((s32[]{:T(128)}, f32[512,512]{0,1:T(8,128)S(1)}, s32[4,2]{0,1:T(2,128)S(1)}, f32[4,128,128]{2,1,0:T(8,128)S(1)}, s32[]{:T(128)}) %tuple.31), condition=%wide.while_cond, body=%wide.while_body.sunk | while | flops 2 | bytes 393329 | solution.py:16
  233.0 0.5 fusion.60
  233.5 1.3 dynamic-slice.7
  235.0 0.5 fusion.60
  235.5 1.3 dynamic-slice.7
  237.1 0.5 fusion.60
  237.6 1.3 dynamic-slice.7
  239.1 0.5 fusion.60
  239.6 1.3 dynamic-slice.7
  241.0 39.3 %custom-call.34 = f32[4,128,128]{1,2,0:T(8,128)S(1)} custom-call(f32[4,128,128]{2,1,0:T(8,128)S(1)} %get-tuple-element.12), custom_call_target="InvertDiagBlocksLowerTriangular" | custom-call | tf_op jit(solution)/shard_map/jit(_solve_triangular)/triangular_solve | solution.py:16
  280.4 1.1 tile.8
  281.4 11.7 %copy.23 = f32[64,8,8,512]{3,1,2,0:T(8,128)} copy(f32[64,8,8,512]{3,2,1,0:T(8,128)S(1)} %bitcast.76) | data formatting | bytes 16777216
  293.1 125.9 %all-reduce.8.cloned.1.call-done = f32[512,4096]{1,0:T(8,128)} async-done(((f32[512,4096]{1,0:T(8,128)}), f32[512,4096]{1,0:T(8,128)}) %all-reduce.8.cloned.1.call-update) | async-done | bytes 8388624 | tf_op jit(solution)/shard_map/psum | solution.py:11
  419.0 3.5 fusion.20
  422.5 4.8 convolution_subtract_fusion.1
  427.3 2.0 fusion.35
  429.3 2.4 convolution_subtract_fusion
  431.7 1.9 fusion.33
  433.7 4.0 fusion.7
  437.7 3.3 fusion.32
  441.0 9.4 %broadcast_select_fusion = (f32[4096,512]{0,1:T(8,128)S(1)}, f32[4096,512]{0,1:T(8,128)}) fusion(pred[4096]{0:T(1024)(128)(4,1)S(1)} %bitcast.81, f32[4096,512]{0,1:T(8,128)} %bitcast.75, pred[4096]{0:T(1024)(128)(4,1)S(1)} %bitcast.77, f32[128,4096]{1,0:T(8,128)} %fusion.32, f32[128,4096]{1,0:T(8,128)} %copy-done.3, f32[128,4096]{1,0:T(8,128)} %copy-done.2, ...), kind=kLoop, calls=%fused_computation.25 | loop fusion | flops 12582912 | bytes 33562624 | tf_op jit(solution)/shard_map/jit(_where)/select_n | solution.py:39
  450.4 2.5 dynamic-slice_select_fusion.3
  452.9 1.9 copy-done
  455.1 9.0 %copy.13 = f32[4096,512]{1,0:T(8,128)} copy(f32[4096,512]{0,1:T(8,128)} %get-tuple-element.30) | data formatting | bytes 16777216 | tf_op jit(solution)/shard_map/jit(_where)/select_n | solution.py:19
  464.1 13.8 %tile.20 = f32[4096,4,512]{2,1,0:T(4,128)} broadcast(f32[4096,512]{1,0:T(8,128)} %copy.13), dimensions={0,2} | broadcast | bytes 41943040 | tf_op jit(solution)/shard_map/tile | solution.py:52
  477.9 30.1 %copy.24 = f32[512,8,4,512]{3,1,2,0:T(8,128)} copy(f32[512,8,4,512]{3,2,1,0:T(4,128)} %bitcast.74) | data formatting | bytes 67108864
  508.0 32.1 %all-reduce.10.cloned.1.call-done = (f32[512,512]{0,1:T(8,128)}, f32[512,512]{0,1:T(8,128)}, f32[512,512]{0,1:T(8,128)}, f32[512,512]{0,1:T(8,128)}) async-done(((f32[512,512]{0,1:T(8,128)}, f32[512,512]{0,1:T(8,128)}, f32[512,512]{0,1:T(8,128)}, f32[512,512]{0,1:T(8,128)}), (f32[512,512]{0,1:T(8,128)}, f32[512,512]{0,1:T(8,128)}, f32[512,512]{0,1:T(8,128)}, ...) | async-done | bytes 4194320 | tf_op jit(solution)/shard_map/psum | solution.py:11
  540.1 123.8 %select_select_fusion = f32[4096,2048]{1,0:T(8,128)} fusion(f32[4096,2048]{1,0:T(8,128)} %bitcast.73, f32[4096,2048]{1,0:T(8,128)} %param.1, pred[2048]{0:T(1024)(128)(4,1)S(1)} %bitcast.79, pred[2048]{0:T(1024)(128)(4,1)S(1)} %bitcast.80, pred[4096]{0:T(1024)(128)(4,1)S(1)} %bitcast.78, f32[4096,512]{0,1:T(8,128)} %copy-done, ...), kind=kOutput, calls=%fused_computation.2 | convolution fusion | flops 51576307712 | bytes 113254400 | tf_op jit(solution)/shard_map/dot_general | solution.py:48
  (63 shorter events, 4.0 us)
Async XLA Ops:
  6.5 138.5 %all-reduce.6.cloned.1.call-start = ((), (), s32[]{:S(2)}) async-start(), calls=%async_computation | async-start | bytes 2097152 | tf_op jit(solution)/shard_map/psum | solution.py:11
  9.3 409.6 %all-reduce.8.cloned.1.call-start = ((), (), s32[]{:S(2)}) async-start(), calls=%async_computation.1 | async-start | bytes 16777216 | tf_op jit(solution)/shard_map/psum | solution.py:11
  33.8 506.3 %all-reduce.10.cloned.1.call-start = ((), (), s32[]{:S(2)}) async-start(), calls=%async_computation.2 | async-start | bytes 8388608 | tf_op jit(solution)/shard_map/psum | solution.py:11
  422.5 11.2 %copy-start.1 = (f32[128,4096]{1,0:T(8,128)}, f32[128,4096]{1,0:T(8,128)S(1)}, u32[]{:S(2)}) copy-start(f32[128,4096]{1,0:T(8,128)S(1)} %fusion.20) | copy-start | bytes 6291460
  422.5 6.8 %copy-start.4 = (f32[512,4096]{1,0:T(8,128)S(1)}, f32[512,4096]{1,0:T(8,128)}, u32[]{:S(2)}) copy-start(f32[512,4096]{1,0:T(8,128)} %all-reduce.8.cloned.1.call-done) | copy-start | bytes 25165828
  429.3 4.4 copy-start.2
  433.7 4.0 copy-start.3
  450.4 4.4 copy-start
Sparse Core Ops, SparseCore 0:
  12.5 132.4 all-reduce.5
  149.4 269.4 all-reduce.7
  455.0 85.0 all-reduce.9
where the time goes:
time: 674 us; the launch traced here: 671 us
  waiting for transfers between devices  269 us (40%)
  matrix products  148 us (22%)
  other arithmetic  141 us (21%)
  local copies, waits for them, and re-layouts  96.5 us (14%)
  between operations  16.3 us (2%)
    psum x3, waiting for transfers between devices, from_root(): return lax.psum(kept, axis)  269 us
    dot_general x1, matrix products, on_device(): lax.dot_general(trailing, across, (((1,), (1,)), ((), ())), precision=lax...  124 us
    another operation x14, other arithmetic, make_panel(): factor = jnp.linalg.cholesky(corner)  78.9 us
    unnamed x22, local copies, waits for them, and re-layouts  53.3 us
    another operation x3, other arithmetic, make_panel(): solved = jax.scipy.linalg.solve_triangular(factor, column.T, lower=True).T  39.6 us
    another operation x7, matrix products, make_panel(): solved = jax.scipy.linalg.solve_triangular(factor, column.T, lower=True).T  21.9 us
    another operation x1, local copies, waits for them, and re-layouts, on_device(): jnp.tile(panel_block, (1, col_blocks))  13.8 us
  transfers between devices with their start and end apart: 3, of which 3 were waited for; matrix products, arithmetic and copies ran while one was open for 33% of the time, Pallas kernels for 0%

commit v1 on v0

v1 whole, which is shorter than its diff:
```python
import functools

import jax
import jax.numpy as jnp
from jax import lax
from jax.experimental import pallas as pl
from jax.experimental.pallas import tpu as pltpu
from jax.sharding import PartitionSpec as P

NB = 512
SUB = 128
LANES = 8
VMEM_BYTES = 60 * 1024 * 1024
LOWER = [(i, j) for i in range(NB // SUB) for j in range(i + 1)]
EXACT = lax.Precision.HIGHEST


def dot_nt(a, b):
    return lax.dot_general(
        a, b, (((1,), (1,)), ((), ())), precision=EXACT, preferred_element_type=jnp.float32
    )


def dot_nn(a, b):
    return lax.dot_general(
        a, b, (((1,), (0,)), ((), ())), precision=EXACT, preferred_element_type=jnp.float32
    )


def split(value):
    high = value.astype(jnp.bfloat16)
    low = (value - high.astype(jnp.float32)).astype(jnp.bfloat16)
    return high, low


def small_cholesky(block):
    groups = SUB // LANES
    lane = lax.broadcasted_iota(jnp.int32, (LANES, SUB), 1)
    sub = lax.broadcasted_iota(jnp.int32, (LANES, SUB), 0)
    left = [block[g * LANES : (g + 1) * LANES] for g in range(groups)]
    right = [jnp.where(lane == sub + g * LANES, 1.0, 0.0) for g in range(groups)]
    for i in range(0, SUB, 2):
        g0, o = divmod(i, LANES)
        head = left[g0]
        row0, row1 = head[o : o + 1], head[o + 1 : o + 2]
        side0, side1 = right[g0][o : o + 1], right[g0][o + 1 : o + 2]
        inv0 = 1.0 / row0[:, i : i + 1]
        ratio = row0[:, i + 1 : i + 2] * inv0
        pivot1 = row1[:, i + 1 : i + 2] - row0[:, i + 1 : i + 2] * ratio
        inv1 = 1.0 / pivot1
        row1 = row1 - ratio * row0
        side1 = side1 - ratio * side0
        row0s, side0s = row0 * inv0, side0 * inv0
        row1s, side1s = row1 * inv1, side1 * inv1
        for g in range(g0, groups):
            col0 = left[g][:, i : i + 1]
            col1 = left[g][:, i + 1 : i + 2] - col0 * ratio
            if g == g0:
                if o + 2 < LANES:
                    below = sub > o + 1
                    new_left = left[g] - jnp.where(below, col0, 0.0) * row0s - jnp.where(below, col1, 0.0) * row1s
                    new_right = right[g] - jnp.where(below, col0, 0.0) * side0s - jnp.where(below, col1, 0.0) * side1s
                else:
                    new_left, new_right = left[g], right[g]
                left[g] = jnp.where(sub == o + 1, row1, new_left)
                right[g] = jnp.where(sub == o + 1, side1, new_right)
            else:
                left[g] = left[g] - col0 * row0s - col1 * row1s
                right[g] = right[g] - col0 * side0s - col1 * side1s
    upper, inverse = [], []
    for g in range(groups):
        row = sub + g * LANES
        pivot = jnp.sum(jnp.where(lane == row, left[g], 0.0), axis=1, keepdims=True)
        scale = lax.rsqrt(pivot)
        upper.append(jnp.where(lane >= row, left[g] * scale, 0.0))
        inverse.append(jnp.where(lane <= row, right[g] * scale, 0.0))
    return jnp.concatenate(upper, 0), jnp.concatenate(inverse, 0)


def factor_kernel(first_ref, second_ref, factor_ref, inv_ref, inv_t_ref, work):
    half = first_ref.shape[0]
    count = NB // SUB
    factor_ref[...] = jnp.zeros_like(factor_ref)
    inv_ref[...] = jnp.zeros_like(inv_ref)
    inv_t_ref[...] = jnp.zeros_like(inv_t_ref)
    for n, (i, j) in enumerate(LOWER):
        value = first_ref[n] if n < half else second_ref[n - half]
        work[i * SUB : (i + 1) * SUB, j * SUB : (j + 1) * SUB] = value
    for k in range(count):
        a, b = k * SUB, (k + 1) * SUB
        upper, inverse = small_cholesky(work[a:b, a:b])
        factor_ref[a:b, a:b] = upper.T
        inverse_t = inverse.T
        inv_ref[a:b, a:b] = inverse
        inv_t_ref[a:b, a:b] = inverse_t
        if k + 1 < count:
            panel = dot_nn(work[b:, a:b], inverse_t)
            factor_ref[b:, a:b] = panel
            for j in range(k + 1, count):
                c, d = j * SUB, (j + 1) * SUB
                work[c:, c:d] -= dot_nt(panel[c - b :], panel[c - b : d - b])
        if k:
            partial = dot_nt(inv_t_ref[:a, :a], factor_ref[a:b, :a])
            part = -dot_nn(partial, inverse_t)
            inv_t_ref[:a, a:b] = part
            inv_ref[a:b, :a] = part.T


def factorize(first, second):
    square = jax.ShapeDtypeStruct((NB, NB), jnp.float32)
    return pl.pallas_call(
        factor_kernel,
        out_shape=(square, square, square),
        in_specs=[pl.BlockSpec(memory_space=pltpu.VMEM)] * 2,
        out_specs=(pl.BlockSpec(memory_space=pltpu.VMEM),) * 3,
        scratch_shapes=[pltpu.VMEM((NB, NB), jnp.float32)],
        compiler_params=pltpu.CompilerParams(vmem_limit_bytes=VMEM_BYTES),
        cost_estimate=pl.CostEstimate(flops=2 * NB**3, bytes_accessed=6 * NB * NB * 4, transcendentals=0),
        name="factor_corner",
    )(first, second)


def across_kernel(inv_ref, rows_ref, out_ref):
    value = dot_nn(inv_ref[...], rows_ref[...])
    high, low = split(value)
    out_ref[:NB] = high
    out_ref[NB : 2 * NB] = high
    out_ref[2 * NB :] = low


def solve_across(inv, rows):
    width = rows.shape[1]
    return pl.pallas_call(
        across_kernel,
        grid=(width // NB,),
        out_shape=jax.ShapeDtypeStruct((3 * NB, width), jnp.bfloat16),
        in_specs=[
            pl.BlockSpec((NB, NB), lambda i: (0, 0)),
            pl.BlockSpec((NB, NB), lambda i: (0, i)),
        ],
        out_specs=pl.BlockSpec((3 * NB, NB), lambda i: (0, i)),
        compiler_params=pltpu.CompilerParams(vmem_limit_bytes=VMEM_BYTES),
        cost_estimate=pl.CostEstimate(
            flops=2 * NB * NB * width, bytes_accessed=10 * NB * width, transcendentals=0
        ),
        name="solve_across",
    )(inv, rows)


def update_kernel(count, tile, info, *refs):
    chunks = refs[:count]
    inv_t_ref, factor_ref, across_ref, matrix_ref = refs[count : count + 4]
    out_ref, panel, panel3 = refs[-3:]
    i, j = pl.program_id(0), pl.program_id(1)
    first_row = jnp.logical_and(info[count] == 0, info[i] == 0)
    first_col = jnp.logical_and(info[count + 1] == 0, j == 0)

    @pl.when(j == 0)
    def _():
        for n in range(count):

            @pl.when(i == n)
            def _():
                panel[...] = dot_nn(chunks[n][...], inv_t_ref[...])

        high, low = split(panel[...])
        panel3[:, :NB] = high
        panel3[:, NB : 2 * NB] = low
        panel3[:, 2 * NB :] = high

        @pl.when(first_row)
        def _():
            panel[...] = factor_ref[...]

    @pl.when(first_row)
    def _():
        out_ref[...] = jnp.zeros_like(out_ref)

    @pl.when(jnp.logical_not(first_row))
    def _():
        columns = pl.ds(pl.multiple_of(j * tile, tile), tile)
        product = jnp.dot(panel3[...], across_ref[:, columns], preferred_element_type=jnp.float32)
        out_ref[...] = matrix_ref[...] - product

    @pl.when(first_col)
    def _():
        out_ref[:, :NB] = panel[...]


def update(info, chunks, inv_t, factor, across, matrix, base):
    count = len(chunks)
    rows, width = matrix.shape
    tile = 2 * NB if width % (2 * NB) == 0 else NB
    whole = lambda i, j, info: (0, 0)
    moving = lambda i, j, info: (info[i], j)
    square = pl.BlockSpec((NB, NB), whole)
    in_specs = [square] * (count + 2) + [
        pl.BlockSpec((3 * NB, width), whole),
        pl.BlockSpec((NB, tile), moving),
    ]
    operands = [info, *chunks, inv_t, factor, across, matrix]
    aliases = {}
    if base is not None:
        in_specs.append(pl.BlockSpec(memory_space=pl.ANY))
        operands.append(base)
        aliases = {len(operands) - 1: 0}
    return pl.pallas_call(
        functools.partial(update_kernel, count, tile),
        grid_spec=pltpu.PrefetchScalarGridSpec(
            num_scalar_prefetch=1,
            grid=(count, width // tile),
            in_specs=in_specs,
            out_specs=pl.BlockSpec((NB, tile), moving),
            scratch_shapes=[
                pltpu.VMEM((NB, NB), jnp.float32),
                pltpu.VMEM((NB, 3 * NB), jnp.bfloat16),
            ],
        ),
        out_shape=jax.ShapeDtypeStruct(matrix.shape, jnp.float32),
        input_output_aliases=aliases,
        compiler_params=pltpu.CompilerParams(vmem_limit_bytes=VMEM_BYTES),
        cost_estimate=pl.CostEstimate(
            flops=6 * count * NB * NB * (width + 2 * NB),
            bytes_accessed=8 * count * NB * width,
            transcendentals=0,
        ),
        name="update_rows",
    )(*operands)


def spread(value, axes, index, order):
    reached = [0]
    for bit in order:
        pairs = [(n, n | bit) for n in reached]
        came = lax.ppermute(value, axes, pairs)
        done = sum(order[: order.index(bit)])
        value = jnp.where((index & ~done) == bit, came, value)
        reached = reached + [n | bit for n in reached]
    return value


def bits_of(size):
    return [1 << n for n in range(size.bit_length() - 1)]


def spread_corner(matrix, p, q, rows_axis, cols_axis):
    corner = matrix[:NB, :NB]
    pieces = jnp.stack(
        [corner[i * SUB : (i + 1) * SUB, j * SUB : (j + 1) * SUB] for i, j in LOWER]
    )
    half = len(LOWER) // 2
    low_bits = bits_of(cols_axis)
    high_bits = [cols_axis * b for b in bits_of(rows_axis)]
    core, across = high_bits[:1], high_bits[1:]
    one = across[::-1] + low_bits[:1] + low_bits[:0:-1] + core
    two = low_bits[:0:-1] + low_bits[:1] + across[::-1] + core
    index = p * cols_axis + q
    axes = ("row", "col")
    return (
        spread(pieces[:half], axes, index, one),
        spread(pieces[half:], axes, index, two),
    )


def ring_positions(cols_axis):
    half = cols_axis // 2
    return [2 * n for n in range(half)] + [2 * n + 1 for n in reversed(range(half))]


def gather_rows(matrix, p, q, rows_axis, cols_axis):
    groups = cols_axis // rows_axis
    came = None
    for t in range(rows_axis):
        block = matrix[:NB, t * NB : (t + 1) * NB].T
        pairs = []
        for r in range(cols_axis):
            h, target = divmod(r, rows_axis)
            pairs.append((r, target * cols_axis + h * rows_axis + (target ^ t)))
        piece = lax.ppermute(block, ("row", "col"), pairs)
        came = piece if came is None else came + piece
    ring = ring_positions(cols_axis)
    table = jnp.array(ring, jnp.int32)
    position = jnp.array([ring.index(n) for n in range(cols_axis)], jnp.int32)[q]

    def slot(shift):
        source = table[(position + shift) % cols_axis]
        h = source // rows_axis
        return groups * ((source % rows_axis) ^ p) + h

    up = [(ring[n], ring[(n + 1) % cols_axis]) for n in range(cols_axis)]
    down = [(b, a) for a, b in up]
    found = [(slot(0), came)]
    going, coming = came, came
    for step in range(1, cols_axis // 2):
        going = lax.ppermute(going, "col", up)
        coming = lax.ppermute(coming, "col", down)
        found.append((slot(-step), going))
        found.append((slot(step), coming))
    top = lax.ppermute(going[: NB // 2], "col", up)
    bottom = lax.ppermute(coming[NB // 2 :], "col", down)
    found.append((slot(cols_axis // 2), jnp.concatenate([top, bottom], 0)))
    return found


def from_root(value, axis, source):
    kept = jnp.where(lax.axis_index(axis) == source, value, 0).astype(value.dtype)
    return lax.psum(kept, axis)


def on_device(matrix):
    rows_axis = lax.axis_size("row")
    cols_axis = lax.axis_size("col")
    p, q = lax.axis_index("row"), lax.axis_index("col")
    row_blocks = matrix.shape[0] // NB
    col_blocks = matrix.shape[1] // NB
    first, second = spread_corner(matrix, p, q, rows_axis, cols_axis)
    if row_blocks == cols_axis and col_blocks == rows_axis:
        found = gather_rows(matrix, p, q, rows_axis, cols_axis)
    else:
        column = from_root(matrix[:, :NB], "col", 0)
        found = [(jnp.int32(s), column[s * NB : (s + 1) * NB]) for s in range(row_blocks)]
    above = spread(matrix[:NB], "row", p, bits_of(rows_axis)[::-1])
    factor, inv, inv_t = factorize(first, second)
    across = solve_across(inv, above)
    early = max(1, len(found) - 3)
    out = None
    for part in (found[:early], found[early:]):
        if part:
            info = jnp.stack([s for s, _ in part] + [p, q]).astype(jnp.int32)
            out = update(info, [c for _, c in part], inv_t, factor, across, matrix, out)
    return out


def solution(mesh):
    in_specs = (P("row", "col"),)
    out_specs = P("row", "col")
    return jax.shard_map(
        on_device, mesh=mesh, in_specs=in_specs, out_specs=out_specs, check_vma=False
    )
```

time: 674 us -> 364 us (0.54)
  the two profiles are of different devices: /device:TPU:0 before, /device:TPU:26 now
where the time goes in v1:
time: 364 us; the launch traced here: 357 us
  Pallas kernels  153 us (42%)
  waiting for transfers between devices  88.7 us (24%)
  starting transfers between devices  41.4 us (11%)
  between operations  27.5 us (8%)
  local copies, waits for them, and re-layouts  26.2 us (7%)
  other arithmetic  20.9 us (6%)
    pallas_call x1, Pallas kernels, factorize(): pl.pallas_call(factor_kernel, out_shape=(square, square, square), in_spec...  79.2 us
    pallas_call x2, Pallas kernels, update(): pl.pallas_call(functools.partial(update_kernel, count, tile), grid_spec=p...  63.1 us
    ppermute x4, waiting for transfers between devices, gather_rows(): piece = lax.ppermute(block, ('row', 'col'), pairs)  43.4 us
    ppermute x3, waiting for transfers between devices, gather_rows(): coming = lax.ppermute(coming, 'col', down)  24.8 us
    ppermute x12, waiting for transfers between devices, spread(): came = lax.ppermute(value, axes, pairs)  20.4 us
    ppermute x3, starting transfers between devices, gather_rows(): going = lax.ppermute(going, 'col', up)  17.2 us
    select_n x12, other arithmetic, spread(): value = jnp.where(index & ~done == bit, came, value)  16.6 us
    ppermute x12, starting transfers between devices, spread(): came = lax.ppermute(value, axes, pairs)  16.2 us
  transfers between devices with their start and end apart: 24, of which 5 were waited for; matrix products, arithmetic and copies ran while one was open for 10% of the time, Pallas kernels for 22%

profile of v1, /device:TPU:26, one launch (start us, length us, event | category | flops | bytes accessed | tf_op | source)
XLA Modules:
  0.0 357.4 jit_solution(12770796844441784184)
XLA Ops:
  0.0 4.7 %slice.82 = f32[512,2048]{1,0:T(8,128)} slice(f32[4096,2048]{1,0:T(8,128)} %refs_6_.1), slice={[0:512], [0:2048]} | slice | bytes 8388608 | tf_op jit(solution)/shard_map/slice | solution.py:322
  4.7 1.3 collective-permute-start.22
  6.0 3.7 %fusion = (f32[512,512]{1,0:T(8,128)S(1)}, f32[512,512]{1,0:T(8,128)S(1)}, f32[512,512]{1,0:T(8,128)S(1)}, f32[512,512]{1,0:T(8,128)}) fusion(f32[4096,2048]{1,0:T(8,128)} %refs_6_.1), kind=kLoop, calls=%fused_computation.24 | loop fusion | bytes 8388608 | tf_op jit(solution)/shard_map/slice | solution.py:274
  9.6 2.6 copy.12
  12.2 1.7 collective-permute-start.3
  13.9 1.4 copy.9
  15.3 1.3 collective-permute-start
  16.5 1.4 copy.11
  18.0 0.7 collective-permute-start.2
  18.7 1.3 copy.10
  20.0 1.6 collective-permute-start.1
  21.6 1.5 bitcast_dynamic-update-slice_fusion.4
  23.1 43.4 %collective-permute-done = f32[512,512]{1,0:T(8,128)S(1)} collective-permute-done((f32[512,512]{1,0:T(8,128)}, f32[512,512]{1,0:T(8,128)S(1)}, u32[]{:S(2)}, u32[]{:S(2)}) %collective-permute-start) | collective-permute-done | bytes 1048608 | tf_op jit(solution)/shard_map/ppermute | solution.py:279
  66.5 2.0 add_add_fusion.refs_0_
  68.6 12.8 %collective-permute-start.4 = (f32[512,512]{1,0:T(8,128)S(1)}, f32[512,512]{1,0:T(8,128)}, u32[]{:S(2)}, u32[]{:S(2)}) collective-permute-start(f32[512,512]{1,0:T(8,128)S(1)} %add_add_fusion.refs_0_), channel_id=1, source_target_pairs={{0,2},{2,4},{4,6},{6,7},{7,5},{5,3},{3,1},{1,0},{8,10},{10,12},{12... | collective-permute-start | bytes 3145736 | tf_op jit(solution)/shard_map/ppermute | solution.py:295
  81.5 6.6 %broadcast_select_fusion = f32[512,2048]{1,0:T(8,128)} fusion(f32[512,2048]{1,0:T(8,128)} %collective-permute-done.22, pred[]{:T(512)S(6)} %eq.61, f32[4096,2048]{1,0:T(8,128)} %refs_6_.1), kind=kLoop, calls=%fused_computation | loop fusion | flops 1048576 | bytes 12582913 | tf_op jit(solution)/shard_map/jit(_where)/select_n | solution.py:237
  88.1 3.4 collective-permute-start.23
  91.5 1.5 bitcast_dynamic-update-slice_fusion.3
  93.0 1.5 bitcast_dynamic-update-slice_fusion.2
  94.5 1.5 bitcast_dynamic-update-slice_fusion.1
  96.0 1.5 bitcast_dynamic-update-slice_fusion
  98.9 6.4 %collective-permute-done.7.refs_2_ = f32[512,512]{1,0:T(8,128)} collective-permute-done((f32[512,512]{1,0:T(8,128)S(1)}, f32[512,512]{1,0:T(8,128)}, u32[]{:S(2)}, u32[]{:S(2)}) %collective-permute-start.7) | collective-permute-done | bytes 1048608 | tf_op jit(solution)/shard_map/ppermute | solution.py:296
  105.3 2.3 collective-permute-start.5
  107.7 0.7 collective-permute-start.18
  108.3 1.0 broadcast_select_fusion.6
  109.4 0.7 collective-permute-start.13
  110.9 1.4 collective-permute-start.14
  112.3 18.5 %collective-permute-done.8.refs_4_ = f32[512,512]{1,0:T(8,128)} collective-permute-done((f32[512,512]{1,0:T(8,128)}, f32[512,512]{1,0:T(8,128)}, u32[]{:S(2)}, u32[]{:S(2)}) %collective-permute-start.8) | collective-permute-done | bytes 1048608 | tf_op jit(solution)/shard_map/ppermute | solution.py:296
  131.1 2.0 collective-permute-start.6
  133.1 1.3 collective-permute-start.20
  134.5 1.3 collective-permute-start.15
  135.8 6.4 %collective-permute-done.20 = f32[5,128,128]{2,1,0:T(8,128)} collective-permute-done((f32[5,128,128]{2,1,0:T(8,128)S(1)}, f32[5,128,128]{2,1,0:T(8,128)}, u32[]{:S(2)}, u32[]{:S(2)}) %collective-permute-start.20) | collective-permute-done | bytes 327712 | tf_op jit(solution)/shard_map/ppermute | solution.py:235
  142.2 1.0 broadcast_select_fusion.5
  143.2 2.0 collective-permute-start.21
  145.2 14.0 %collective-permute-done.15 = f32[5,128,128]{2,1,0:T(8,128)} collective-permute-done((f32[5,128,128]{2,1,0:T(8,128)S(1)}, f32[5,128,128]{2,1,0:T(8,128)}, u32[]{:S(2)}, u32[]{:S(2)}) %collective-permute-start.15) | collective-permute-done | bytes 327712 | tf_op jit(solution)/shard_map/ppermute | solution.py:235
  159.3 1.0 broadcast_select_fusion.9
  160.3 2.0 collective-permute-start.16
  169.4 0.7 fusion.1
  190.7 1.1 slice.83
  191.8 2.3 collective-permute-start.10
  195.3 0.8 broadcast_select_fusion.10.second_ref
  196.1 0.8 broadcast_select_fusion.11.first_ref
  196.9 79.2 %factor_corner.1 = (f32[512,512]{1,0:T(8,128)}, f32[512,512]{1,0:T(8,128)}, f32[512,512]{1,0:T(8,128)}) custom-call(f32[5,128,128]{2,1,0:T(8,128)} %broadcast_select_fusion.11.first_ref, f32[5,128,128]{2,1,0:T(8,128)} %broadcast_select_fusion.10.second_ref), custom_call_target="tpu_custom_call" | custom-call | flops 268435456 | bytes 6291456 | tf_op jit(solution)/shard_map/factor_corner/pallas_call | solution.py:111
  276.1 2.3 pad_maximum_fusion.refs_2_
  278.3 5.3 %broadcast_select_fusion.1.rows_ref = f32[512,2048]{1,0:T(8,128)} fusion(f32[512,2048]{1,0:T(8,128)} %collective-permute-done.23, f32[512,2048]{1,0:T(8,128)} %broadcast_select_fusion, pred[]{:T(512)S(6)} %eq.60), kind=kLoop, calls=%fused_computation.1 | loop fusion | flops 1048576 | bytes 12582913 | tf_op jit(solution)/shard_map/jit(_where)/select_n | solution.py:237
  283.6 10.4 %solve_across.1.refs_7_.refs_5_ = bf16[1536,2048]{1,0:T(8,128)(2,1)} custom-call(f32[512,512]{1,0:T(8,128)} %get-tuple-element.10.inv_ref, f32[512,2048]{1,0:T(8,128)} %broadcast_select_fusion.1.rows_ref), custom_call_target="tpu_custom_call" | custom-call | flops 1073741824 | bytes 10485760 | tf_op jit(solution)/shard_map/solve_across/pallas_call | solution.py:133
  294.0 37.9 %update_rows.2.refs_7_ = f32[4096,2048]{1,0:T(8,128)} custom-call(s32[7]{0:T(128)} %stack.96.info, f32[512,512]{1,0:T(8,128)} %copy-done.2, f32[512,512]{1,0:T(8,128)} %collective-permute-done.4.refs_1_, f32[512,512]{1,0:T(8,128)} %collective-permute-done.7.refs_2_, f32[512,512]{1,0:T(8,128)} %collective-permute-done.5.refs_3_, ...), custom_call_target="tpu_custom_call" | custom-call | flops 24159191040 | bytes 41943040 | tf_op jit(solution)/shard_map/update_rows/pallas_call | solution.py:207
  331.9 25.2 %update_rows.3 = f32[4096,2048]{1,0:T(8,128)} custom-call(s32[5]{0:T(128)} %stack.78.info, f32[512,512]{1,0:T(8,128)} %copy-done.1, f32[512,512]{1,0:T(8,128)} %copy-done, f32[512,512]{1,0:T(8,128)} %pad_maximum_fusion.refs_2_, f32[512,512]{1,0:T(8,128)} %get-tuple-element.8.refs_5_.refs_3_, ...), custom_call_target="tpu_custom_call", output_to_operand_aliasing={{}: (8, {})} | custom-call | flops 14495514624 | bytes 25165824 | tf_op jit(solution)/shard_map/update_rows/pallas_call | solution.py:207
  (45 shorter events, 4.6 us)
Async XLA Ops:
  4.7 76.8 %collective-permute-start.22 = (f32[512,2048]{1,0:T(8,128)}, f32[512,2048]{1,0:T(8,128)}, u32[]{:S(2)}, u32[]{:S(2)}) collective-permute-start(f32[512,2048]{1,0:T(8,128)} %slice.82), channel_id=1, source_target_pairs={{0,16},{1,17},{2,18},{3,19},{4,20},{5,21},{6,22},{7,23}} | collective-permute-start | bytes 12582920 | tf_op jit(solution)/shard_map/ppermute | solution.py:235
  12.2 10.9 %collective-permute-start.3 = (f32[512,512]{1,0:T(8,128)}, f32[512,512]{1,0:T(8,128)}, u32[]{:S(2)}, u32[]{:S(2)}) collective-permute-start(f32[512,512]{1,0:T(8,128)} %bitcast.43), channel_id=1, source_target_pairs={{0,3},{1,10},{2,17},{3,24},{4,7},{5,14},{6,21},{7,28}} | collective-permute-start | bytes 3145736 | tf_op jit(solution)/shard_map/ppermute | solution.py:279
  15.3 51.3 %collective-permute-start = (f32[512,512]{1,0:T(8,128)}, f32[512,512]{1,0:T(8,128)S(1)}, u32[]{:S(2)}, u32[]{:S(2)}) collective-permute-start(f32[512,512]{1,0:T(8,128)} %bitcast.44), channel_id=1, source_target_pairs={{0,0},{1,9},{2,18},{3,27},{4,4},{5,13},{6,22},{7,31}} | collective-permute-start | bytes 3145736 | tf_op jit(solution)/shard_map/ppermute | solution.py:279
  18.0 48.6 %collective-permute-start.2 = (f32[512,512]{1,0:T(8,128)}, f32[512,512]{1,0:T(8,128)S(1)}, u32[]{:S(2)}, u32[]{:S(2)}) collective-permute-start(f32[512,512]{1,0:T(8,128)} %bitcast.45), channel_id=1, source_target_pairs={{0,2},{1,11},{2,16},{3,25},{4,6},{5,15},{6,20},{7,29}} | collective-permute-start | bytes 3145736 | tf_op jit(solution)/shard_map/ppermute | solution.py:279
  20.0 46.5 %collective-permute-start.1 = (f32[512,512]{1,0:T(8,128)}, f32[512,512]{1,0:T(8,128)}, u32[]{:S(2)}, u32[]{:S(2)}) collective-permute-start(f32[512,512]{1,0:T(8,128)} %bitcast.46), channel_id=1, source_target_pairs={{0,1},{1,8},{2,19},{3,26},{4,5},{5,12},{6,23},{7,30}} | collective-permute-start | bytes 3145736 | tf_op jit(solution)/shard_map/ppermute | solution.py:279
  68.6 19.5 %copy-start.2 = (f32[512,512]{1,0:T(8,128)}, f32[512,512]{1,0:T(8,128)S(1)}, u32[]{:S(2)}) copy-start(f32[512,512]{1,0:T(8,128)S(1)} %add_add_fusion.refs_0_) | copy-start | bytes 3145732
  68.6 36.7 %collective-permute-start.7 = (f32[512,512]{1,0:T(8,128)S(1)}, f32[512,512]{1,0:T(8,128)}, u32[]{:S(2)}, u32[]{:S(2)}) collective-permute-start(f32[512,512]{1,0:T(8,128)S(1)} %add_add_fusion.refs_0_), channel_id=1, source_target_pairs={{2,0},{4,2},{6,4},{7,6},{5,7},{3,5},{1,3},{0,1},{10,8},{12,10},{14... | collective-permute-start | bytes 3145736 | tf_op jit(solution)/shard_map/ppermute | solution.py:296
  68.6 36.6 %collective-permute-start.4 = (f32[512,512]{1,0:T(8,128)S(1)}, f32[512,512]{1,0:T(8,128)}, u32[]{:S(2)}, u32[]{:S(2)}) collective-permute-start(f32[512,512]{1,0:T(8,128)S(1)} %add_add_fusion.refs_0_), channel_id=1, source_target_pairs={{0,2},{2,4},{4,6},{6,7},{7,5},{5,3},{3,1},{1,0},{8,10},{10,12},{12... | collective-permute-start | bytes 3145736 | tf_op jit(solution)/shard_map/ppermute | solution.py:295
  88.1 74.2 %copy-start.4 = (s32[8]{0:T(128)S(1)}, s32[8]{0:T(128)}, u32[]{:S(2)}) copy-start(s32[8]{0:T(128)} %constant.179.clone) | copy-start | bytes 100
  88.1 81.3 %copy-start.3 = (s32[8]{0:T(128)S(1)}, s32[8]{0:T(128)}, u32[]{:S(2)}) copy-start(s32[8]{0:T(128)} %constant.178.clone) | copy-start | bytes 100
  88.1 190.2 %collective-permute-start.23 = (f32[512,2048]{1,0:T(8,128)}, f32[512,2048]{1,0:T(8,128)}, u32[]{:S(2)}, u32[]{:S(2)}) collective-permute-start(f32[512,2048]{1,0:T(8,128)} %broadcast_select_fusion), channel_id=1, source_target_pairs={{0,8},{16,24},{1,9},{17,25},{2,10},{18,26},{3,11},{19,27},{4,12},{... | collective-permute-start | bytes 12582920 | tf_op jit(solution)/shard_map/ppermute | solution.py:235
  97.5 10.1 %collective-permute-start.17 = (f32[5,128,128]{2,1,0:T(8,128)S(1)}, f32[5,128,128]{2,1,0:T(8,128)S(1)}, u32[]{:S(2)}, u32[]{:S(2)}) collective-permute-start(f32[5,128,128]{2,1,0:T(8,128)S(1)} %get-tuple-element.11), channel_id=1, source_target_pairs={{0,4}} | collective-permute-start | bytes 983048 | tf_op jit(solution)/shard_map/ppermute | solution.py:235
  98.2 10.1 %collective-permute-start.12 = (f32[5,128,128]{2,1,0:T(8,128)}, f32[5,128,128]{2,1,0:T(8,128)S(1)}, u32[]{:S(2)}, u32[]{:S(2)}) collective-permute-start(f32[5,128,128]{2,1,0:T(8,128)} %get-tuple-element.12), channel_id=1, source_target_pairs={{0,16}} | collective-permute-start | bytes 983048 | tf_op jit(solution)/shard_map/ppermute | solution.py:235
  105.3 25.5 %collective-permute-start.8 = (f32[512,512]{1,0:T(8,128)}, f32[512,512]{1,0:T(8,128)}, u32[]{:S(2)}, u32[]{:S(2)}) collective-permute-start(f32[512,512]{1,0:T(8,128)} %collective-permute-done.7.refs_2_), channel_id=1, source_target_pairs={{2,0},{4,2},{6,4},{7,6},{5,7},{3,5},{1,3},{0,1},{10,8},{12,10},{14... | collective-permute-start | bytes 3145736 | tf_op jit(solution)/shard_map/ppermute | solution.py:296
  105.3 25.8 %collective-permute-start.5 = (f32[512,512]{1,0:T(8,128)}, f32[512,512]{1,0:T(8,128)}, u32[]{:S(2)}, u32[]{:S(2)}) collective-permute-start(f32[512,512]{1,0:T(8,128)} %collective-permute-done.4.refs_1_), channel_id=1, source_target_pairs={{0,2},{2,4},{4,6},{6,7},{7,5},{5,3},{3,1},{1,0},{8,10},{10,12},{12... | collective-permute-start | bytes 3145736 | tf_op jit(solution)/shard_map/ppermute | solution.py:295
  107.7 2.4 collective-permute-start.18
  109.4 1.4 collective-permute-start.13
  110.1 23.0 %collective-permute-start.19 = (f32[5,128,128]{2,1,0:T(8,128)S(1)}, f32[5,128,128]{2,1,0:T(8,128)S(1)}, u32[]{:S(2)}, u32[]{:S(2)}) collective-permute-start(f32[5,128,128]{2,1,0:T(8,128)S(1)} %broadcast_select_fusion.3), channel_id=1, source_target_pairs={{0,1},{4,5},{2,3},{6,7}} | collective-permute-start | bytes 983048 | tf_op jit(solution)/shard_map/ppermute | solution.py:235
  110.9 23.6 %collective-permute-start.14 = (f32[5,128,128]{2,1,0:T(8,128)S(1)}, f32[5,128,128]{2,1,0:T(8,128)}, u32[]{:S(2)}, u32[]{:S(2)}) collective-permute-start(f32[5,128,128]{2,1,0:T(8,128)S(1)} %broadcast_select_fusion.7), channel_id=1, source_target_pairs={{0,4},{16,20},{1,5},{17,21}} | collective-permute-start | bytes 983048 | tf_op jit(solution)/shard_map/ppermute | solution.py:235
  130.8 59.8 %collective-permute-start.9 = (f32[512,512]{1,0:T(8,128)}, f32[512,512]{1,0:T(8,128)S(1)}, u32[]{:S(2)}, u32[]{:S(2)}) collective-permute-start(f32[512,512]{1,0:T(8,128)} %collective-permute-done.8.refs_4_), channel_id=1, source_target_pairs={{2,0},{4,2},{6,4},{7,6},{5,7},{3,5},{1,3},{0,1},{10,8},{12,10},{14... | collective-permute-start | bytes 3145736 | tf_op jit(solution)/shard_map/ppermute | solution.py:296
  131.1 59.7 %collective-permute-start.6 = (f32[512,512]{1,0:T(8,128)}, f32[512,512]{1,0:T(8,128)S(1)}, u32[]{:S(2)}, u32[]{:S(2)}) collective-permute-start(f32[512,512]{1,0:T(8,128)} %collective-permute-done.5.refs_3_), channel_id=1, source_target_pairs={{0,2},{2,4},{4,6},{6,7},{7,5},{5,3},{3,1},{1,0},{8,10},{10,12},{12... | collective-permute-start | bytes 3145736 | tf_op jit(solution)/shard_map/ppermute | solution.py:295
  133.1 9.1 %collective-permute-start.20 = (f32[5,128,128]{2,1,0:T(8,128)S(1)}, f32[5,128,128]{2,1,0:T(8,128)}, u32[]{:S(2)}, u32[]{:S(2)}) collective-permute-start(f32[5,128,128]{2,1,0:T(8,128)S(1)} %broadcast_select_fusion.4), channel_id=1, source_target_pairs={{0,16},{4,20},{2,18},{6,22},{1,17},{5,21},{3,19},{7,23}} | collective-permute-start | bytes 983048 | tf_op jit(solution)/shard_map/ppermute | solution.py:235
  134.5 24.8 %collective-permute-start.15 = (f32[5,128,128]{2,1,0:T(8,128)S(1)}, f32[5,128,128]{2,1,0:T(8,128)}, u32[]{:S(2)}, u32[]{:S(2)}) collective-permute-start(f32[5,128,128]{2,1,0:T(8,128)S(1)} %broadcast_select_fusion.8), channel_id=1, source_target_pairs={{0,2},{16,18},{1,3},{17,19},{4,6},{20,22},{5,7},{21,23}} | collective-permute-start | bytes 983048 | tf_op jit(solution)/shard_map/ppermute | solution.py:235
  143.2 52.1 %collective-permute-start.21 = (f32[5,128,128]{2,1,0:T(8,128)S(1)}, f32[5,128,128]{2,1,0:T(8,128)}, u32[]{:S(2)}, u32[]{:S(2)}) collective-permute-start(f32[5,128,128]{2,1,0:T(8,128)S(1)} %broadcast_select_fusion.5), channel_id=1, source_target_pairs={{0,8},{4,12},{2,10},{6,14},{1,9},{5,13},{3,11},{7,15},{16,24},{20,... | collective-permute-start | bytes 983048 | tf_op jit(solution)/shard_map/ppermute | solution.py:235
  160.3 35.8 %collective-permute-start.16 = (f32[5,128,128]{2,1,0:T(8,128)S(1)}, f32[5,128,128]{2,1,0:T(8,128)}, u32[]{:S(2)}, u32[]{:S(2)}) collective-permute-start(f32[5,128,128]{2,1,0:T(8,128)S(1)} %broadcast_select_fusion.9), channel_id=1, source_target_pairs={{0,8},{16,24},{1,9},{17,25},{4,12},{20,28},{5,13},{21,29},{2,10},{... | collective-permute-start | bytes 983048 | tf_op jit(solution)/shard_map/ppermute | solution.py:235
  190.6 93.0 %copy-start = (f32[512,512]{1,0:T(8,128)}, f32[512,512]{1,0:T(8,128)S(1)}, u32[]{:S(2)}) copy-start(f32[512,512]{1,0:T(8,128)S(1)} %collective-permute-done.9.refs_1_) | copy-start | bytes 3145732
  190.7 85.4 %collective-permute-start.11 = (f32[256,512]{1,0:T(8,128)S(1)}, f32[256,512]{1,0:T(8,128)}, u32[]{:S(2)}, u32[]{:S(2)}) collective-permute-start(f32[256,512]{1,0:T(8,128)S(1)} %slice.84), channel_id=1, source_target_pairs={{2,0},{4,2},{6,4},{7,6},{5,7},{3,5},{1,3},{0,1},{10,8},{12,10},{14... | collective-permute-start | bytes 1572872 | tf_op jit(solution)/shard_map/ppermute | solution.py:300
  190.7 92.9 %copy-start.1 = (f32[512,512]{1,0:T(8,128)}, f32[512,512]{1,0:T(8,128)S(1)}, u32[]{:S(2)}) copy-start(f32[512,512]{1,0:T(8,128)S(1)} %collective-permute-done.6.refs_0_) | copy-start | bytes 3145732
  191.8 84.2 %collective-permute-start.10 = (f32[256,512]{1,0:T(8,128)}, f32[256,512]{1,0:T(8,128)}, u32[]{:S(2)}, u32[]{:S(2)}) collective-permute-start(f32[256,512]{1,0:T(8,128)} %slice.83), channel_id=1, source_target_pairs={{0,2},{2,4},{4,6},{6,7},{7,5},{5,3},{3,1},{1,0},{8,10},{10,12},{12... | collective-permute-start | bytes 1572872 | tf_op jit(solution)/shard_map/ppermute | solution.py:299

commit v2 on v0

v2 whole, which is shorter than its diff:
```python
import functools

import jax
import jax.numpy as jnp
import numpy as np
from jax import lax
from jax.experimental import pallas as pl
from jax.experimental.pallas import tpu as pltpu
from jax.sharding import PartitionSpec as P

NB = 512
SUB = 128
LANES = 8
COUNT = NB // SUB
VMEM_BYTES = 60 * 1024 * 1024
LOWER = [(i, j) for i in range(COUNT) for j in range(i + 1)]
HALF = len(LOWER) // 2
EXACT = lax.Precision.HIGHEST
PARAMS = pltpu.CompilerParams(vmem_limit_bytes=VMEM_BYTES)
SQUARE = jax.ShapeDtypeStruct((NB, NB), jnp.float32)
IN_VMEM = pl.BlockSpec(memory_space=pltpu.VMEM)
ANYWHERE = pl.BlockSpec(memory_space=pl.ANY)


def dot_nt(a, b):
    return lax.dot_general(
        a, b, (((1,), (1,)), ((), ())), precision=EXACT, preferred_element_type=jnp.float32
    )


def dot_nn(a, b):
    return lax.dot_general(
        a, b, (((1,), (0,)), ((), ())), precision=EXACT, preferred_element_type=jnp.float32
    )


def split2(value):
    high = value.astype(jnp.bfloat16)
    low = (value - high.astype(jnp.float32)).astype(jnp.bfloat16)
    return high, low


def split3(value):
    high = value.astype(jnp.bfloat16)
    rest = value - high.astype(jnp.float32)
    middle, low = split2(rest)
    return high, middle, low


def store_parts(ref, value, axis, pattern):
    parts = split3(value)
    for n, k in enumerate(pattern):
        place = slice(n * NB, (n + 1) * NB)
        if axis:
            ref[:, place] = parts[k]
        else:
            ref[place] = parts[k]


LEFT_PARTS = (0, 1, 2, 0, 1, 0)
RIGHT_PARTS = (0, 0, 0, 1, 1, 2)


def pack_kernel(matrix_ref, first_ref, second_ref):
    for n, (i, j) in enumerate(LOWER):
        target, place = (first_ref, n) if n < HALF else (second_ref, n - HALF)
        target[place] = matrix_ref[i * SUB : (i + 1) * SUB, j * SUB : (j + 1) * SUB]


def pack_corner(matrix):
    part = jax.ShapeDtypeStruct((HALF, SUB, SUB), jnp.float32)
    whole = pl.BlockSpec((HALF, SUB, SUB), lambda i: (0, 0, 0))
    return pl.pallas_call(
        pack_kernel,
        grid=(1,),
        out_shape=(part, part),
        in_specs=[pl.BlockSpec((NB, NB), lambda i: (0, 0))],
        out_specs=(whole, whole),
        compiler_params=PARAMS,
        name="pack_corner",
    )(matrix)


def turn_kernel(count, matrix_ref, *refs):
    for t in range(count):
        refs[t][...] = matrix_ref[:, t * NB : (t + 1) * NB].T


def turn_blocks(matrix, count):
    square = pl.BlockSpec((NB, NB), lambda i: (0, 0))
    return pl.pallas_call(
        functools.partial(turn_kernel, count),
        grid=(1,),
        out_shape=(SQUARE,) * count,
        in_specs=[pl.BlockSpec((NB, count * NB), lambda i: (0, 0))],
        out_specs=(square,) * count,
        compiler_params=PARAMS,
        name="turn_blocks",
    )(matrix)


def reciprocal(value):
    guess = pl.reciprocal(value, approx=True)
    guess = guess * (2.0 - value * guess)
    return guess * (2.0 - value * guess)


def small_cholesky(block):
    groups = SUB // LANES
    shape = (LANES, SUB)
    lane = lax.broadcasted_iota(jnp.int32, shape, 1)
    sub = lax.broadcasted_iota(jnp.int32, shape, 0)
    left = [block[g * LANES : (g + 1) * LANES] for g in range(groups)]
    right = [jnp.where(lane == sub + g * LANES, 1.0, 0.0) for g in range(groups)]
    for g0 in range(groups):
        i = g0 * LANES
        head, side = left[g0], right[g0]
        columns = [jnp.broadcast_to(head[:, i + j : i + j + 1], shape) for j in range(LANES)]
        ratios, heads, sides = [], [], []
        for k in range(LANES):
            inverse = reciprocal(columns[k][k : k + 1])
            ratio = {j: columns[j][k : k + 1] * inverse for j in range(k + 1, LANES)}
            scaled_head = head[k : k + 1] * inverse
            scaled_side = side[k : k + 1] * inverse
            ratios.append(ratio)
            heads.append(scaled_head)
            sides.append(scaled_side)
            if k + 1 < LANES:
                below = jnp.where(sub > k, columns[k], 0.0)
                for j in range(k + 1, LANES):
                    columns[j] = columns[j] - below * ratio[j]
                head = head - below * scaled_head
                side = side - below * scaled_side
        left[g0], right[g0] = head, side
        for g in range(g0 + 1, groups):
            own = [jnp.broadcast_to(left[g][:, i + j : i + j + 1], shape) for j in range(LANES)]
            body, tail = left[g], right[g]
            for k in range(LANES):
                for j in range(k + 1, LANES):
                    own[j] = own[j] - own[k] * ratios[k][j]
                body = body - own[k] * heads[k]
                tail = tail - own[k] * sides[k]
            left[g], right[g] = body, tail
    upper, inverse = [], []
    for g in range(groups):
        row = sub + g * LANES
        pivot = jnp.sum(jnp.where(lane == row, left[g], 0.0), axis=1, keepdims=True)
        scale = lax.rsqrt(pivot)
        upper.append(jnp.where(lane >= row, left[g] * scale, 0.0))
        inverse.append(jnp.where(lane <= row, right[g] * scale, 0.0))
    return jnp.concatenate(upper, 0), jnp.concatenate(inverse, 0)


def factor_block(k, work, inv_t):
    start = pl.multiple_of(k * SUB, SUB)
    here = pl.ds(start, SUB)
    upper, inverse = small_cholesky(work[here, here])
    inverse_t = inverse.T
    row = lax.broadcasted_iota(jnp.int32, (NB, SUB), 0)
    panel = jnp.where(row >= start + SUB, dot_nn(work[:, here], inverse_t), 0.0)
    work[...] -= dot_nt(panel, panel)
    work[:, here] = panel
    work[here, here] = upper.T
    column = lax.broadcasted_iota(jnp.int32, (SUB, NB), 1)
    before = jnp.where(column < start, work[here, :], 0.0)
    inv_t[:, here] = -dot_nn(dot_nt(inv_t[...], before), inverse_t)
    inv_t[here, here] = inverse_t


def factor_first_kernel(last, first_ref, second_ref, work, inv_t):
    inv_t[...] = jnp.zeros_like(inv_t)
    work[...] = jnp.zeros_like(work)
    for n, (i, j) in enumerate(LOWER):
        value = first_ref[n] if n < HALF else second_ref[n - HALF]
        work[i * SUB : (i + 1) * SUB, j * SUB : (j + 1) * SUB] = value

    @pl.loop(0, last)
    def _(k):
        factor_block(k, work, inv_t)


def factor_last_kernel(begin, work_in, inv_t_in, factor_ref, inv_ref, inv_t_ref):
    factor_ref[...] = work_in[...]
    inv_t_ref[...] = inv_t_in[...]

    @pl.loop(begin, COUNT)
    def _(k):
        factor_block(k, factor_ref, inv_t_ref)

    inv_ref[...] = inv_t_ref[...].T


FACTOR_COST = pl.CostEstimate(flops=2 * NB**3, bytes_accessed=4 * NB * NB * 4, transcendentals=0)


def factor_first(first, second):
    return pl.pallas_call(
        functools.partial(factor_first_kernel, COUNT // 2),
        out_shape=(SQUARE, SQUARE),
        in_specs=[IN_VMEM] * 2,
        out_specs=(IN_VMEM,) * 2,
        compiler_params=PARAMS,
        cost_estimate=FACTOR_COST,
        name="factor_first",
    )(first, second)


def factor_last(work, inv_t):
    return pl.pallas_call(
        functools.partial(factor_last_kernel, COUNT // 2),
        out_shape=(SQUARE, SQUARE, SQUARE),
        in_specs=[IN_VMEM] * 2,
        out_specs=(IN_VMEM,) * 3,
        compiler_params=PARAMS,
        cost_estimate=FACTOR_COST,
        name="factor_last",
    )(work, inv_t)


def across_kernel(count, info, inv_ref, *refs):
    sources, out_ref, left, right, rows, sem = refs[:count], *refs[count:]
    i = pl.program_id(0)

    @pl.when(i == 0)
    def _():
        for n in range(count):

            @pl.when(info[0] == n)
            def _():
                copy = pltpu.make_async_copy(sources[n].at[pl.ds(0, NB)], rows, sem)
                copy.start()
                copy.wait()

        store_parts(left, inv_ref[...], 1, LEFT_PARTS)

    columns = pl.ds(pl.multiple_of(i * NB, NB), NB)
    store_parts(right, rows[:, columns], 0, RIGHT_PARTS)
    value = jnp.dot(left[...], right[...], preferred_element_type=jnp.float32)
    high, low = split2(value)
    out_ref[:NB] = high
    out_ref[NB : 2 * NB] = high
    out_ref[2 * NB :] = low


def solve_across(info, inv, sources):
    width = sources[0].shape[1]
    count = len(sources)
    return pl.pallas_call(
        functools.partial(across_kernel, count),
        grid_spec=pltpu.PrefetchScalarGridSpec(
            num_scalar_prefetch=1,
            grid=(width // NB,),
            in_specs=[pl.BlockSpec((NB, NB), lambda i, info: (0, 0))] + [ANYWHERE] * count,
            out_specs=pl.BlockSpec((3 * NB, NB), lambda i, info: (0, i)),
            scratch_shapes=[
                pltpu.VMEM((NB, 6 * NB), jnp.bfloat16),
                pltpu.VMEM((6 * NB, NB), jnp.bfloat16),
                pltpu.VMEM((NB, width), jnp.float32),
                pltpu.SemaphoreType.DMA,
            ],
        ),
        out_shape=jax.ShapeDtypeStruct((3 * NB, width), jnp.bfloat16),
        compiler_params=PARAMS,
        cost_estimate=pl.CostEstimate(
            flops=12 * NB * NB * width, bytes_accessed=10 * NB * width, transcendentals=0
        ),
        name="solve_across",
    )(info, inv, *sources)


def update_kernel(count, tile, info, *refs):
    chunks = refs[:count]
    inv_t_ref, factor_ref, across_ref, matrix_ref = refs[count : count + 4]
    out_ref, panel, panel3, left, right = refs[-5:]
    i, j = pl.program_id(0), pl.program_id(1)
    first_row = jnp.logical_and(info[0] == 0, info[2 + i] == 0)
    first_col = jnp.logical_and(info[1] == 0, j == 0)

    @pl.when(jnp.logical_and(i == 0, j == 0))
    def _():
        store_parts(right, inv_t_ref[...], 0, RIGHT_PARTS)

    @pl.when(j == 0)
    def _():
        for n in range(count):

            @pl.when(i == n)
            def _():
                store_parts(left, chunks[n][...], 1, LEFT_PARTS)

        value = jnp.dot(left[...], right[...], preferred_element_type=jnp.float32)
        panel[...] = value
        high, low = split2(value)
        panel3[:, :NB] = high
        panel3[:, NB : 2 * NB] = low
        panel3[:, 2 * NB :] = high

        @pl.when(first_row)
        def _():
            panel[...] = factor_ref[...]

    @pl.when(first_row)
    def _():
        out_ref[...] = jnp.zeros_like(out_ref)

    @pl.when(jnp.logical_not(first_row))
    def _():
        columns = pl.ds(pl.multiple_of(j * tile, tile), tile)
        product = jnp.dot(panel3[...], across_ref[:, columns], preferred_element_type=jnp.float32)
        out_ref[...] = matrix_ref[...] - product

    @pl.when(first_col)
    def _():
        out_ref[:, :NB] = panel[...]


def update(info, chunks, inv_t, factor, across, matrix, base):
    count = len(chunks)
    width = matrix.shape[1]
    tile = 2 * NB if width % (2 * NB) == 0 else NB
    whole = lambda i, j, info: (0, 0)
    moving = lambda i, j, info: (info[2 + i], j)
    square = pl.BlockSpec((NB, NB), whole)
    in_specs = [square] * (count + 2) + [
        pl.BlockSpec((3 * NB, width), whole),
        pl.BlockSpec((NB, tile), moving),
    ]
    operands = [info, *chunks, inv_t, factor, across, matrix]
    aliases = {}
    if base is not None:
        in_specs.append(ANYWHERE)
        operands.append(base)
        aliases = {len(operands) - 1: 0}
    return pl.pallas_call(
        functools.partial(update_kernel, count, tile),
        grid_spec=pltpu.PrefetchScalarGridSpec(
            num_scalar_prefetch=1,
            grid=(count, width // tile),
            in_specs=in_specs,
            out_specs=pl.BlockSpec((NB, tile), moving),
            scratch_shapes=[
                pltpu.VMEM((NB, NB), jnp.float32),
                pltpu.VMEM((NB, 3 * NB), jnp.bfloat16),
                pltpu.VMEM((NB, 6 * NB), jnp.bfloat16),
                pltpu.VMEM((6 * NB, NB), jnp.bfloat16),
            ],
        ),
        out_shape=jax.ShapeDtypeStruct(matrix.shape, jnp.float32),
        input_output_aliases=aliases,
        compiler_params=PARAMS,
        cost_estimate=pl.CostEstimate(
            flops=6 * count * NB * NB * (width + 2 * NB),
            bytes_accessed=8 * count * NB * width,
            transcendentals=0,
        ),
        name="update_rows",
    )(*operands)


def tree_stages(order):
    reached, done, stages = [0], 0, []
    for bit in order:
        stages.append(([(n, n | bit) for n in reached], bit, done))
        reached = reached + [n | bit for n in reached]
        done |= bit
    return stages


def bits_of(size):
    return [1 << n for n in range(size.bit_length() - 1)]


def corner_orders(rows_axis, cols_axis):
    low = bits_of(cols_axis)
    high = [cols_axis * bit for bit in bits_of(rows_axis)]
    core, across = high[:1], high[:0:-1]
    near, far = low[:1], low[:0:-1]
    return across + near + far + core, far + near + across + core


def spread_apart(held, axis, bit):
    return held + [(n | bit, lax.ppermute(v, axis, [(n, n | bit)])) for n, v in held]


def ring_positions(cols_axis):
    half = cols_axis // 2
    return [2 * n for n in range(half)] + [2 * n + 1 for n in reversed(range(half))]


def scatter_pairs(t, rows_axis, cols_axis):
    pairs = []
    for r in range(cols_axis):
        h, target = divmod(r, rows_axis)
        pairs.append((r, target * cols_axis + h * rows_axis + (target ^ t)))
    return pairs


def ring_shifts(cols_axis):
    shifts = [0]
    last = cols_axis // 2 - 1
    for step in range(1, last):
        shifts += [-step, step]
    return shifts + [cols_axis // 2, -last, last]


def place_table(rows_axis, cols_axis, balanced, row_blocks):
    ring = ring_positions(cols_axis)
    groups = cols_axis // rows_axis
    table = []
    for p in range(rows_axis):
        for q in range(cols_axis):
            if balanced:
                places = []
                for shift in ring_shifts(cols_axis):
                    source = ring[(ring.index(q) + shift) % cols_axis]
                    places.append(groups * ((source % rows_axis) ^ p) + source // rows_axis)
            else:
                places = list(range(row_blocks))
            table.append([p, q] + places)
    return np.array(table, np.int32)


def from_root(value, axis, source):
    kept = jnp.where(lax.axis_index(axis) == source, value, 0).astype(value.dtype)
    return lax.psum(kept, axis)


def tie(*values):
    return lax.optimization_barrier(values)


def on_device(matrix):
    rows_axis = lax.axis_size("row")
    cols_axis = lax.axis_size("col")
    both = ("row", "col")
    index = lax.axis_index("row") * cols_axis + lax.axis_index("col")
    row_blocks = matrix.shape[0] // NB
    col_blocks = matrix.shape[1] // NB
    balanced = row_blocks == cols_axis and col_blocks == rows_axis
    table = jnp.asarray(place_table(rows_axis, cols_axis, balanced, row_blocks))
    places = lax.dynamic_slice_in_dim(table, index, 1, 0)[0]

    parts = list(pack_corner(matrix))
    stages = [tree_stages(order) for order in corner_orders(rows_axis, cols_axis)]
    for step in range(len(stages[0])):
        came = [lax.ppermute(parts[n], both, stages[n][step][0]) for n in range(2)]
        for n in range(2):
            _, bit, done = stages[n][step]
            parts[n] = jnp.where((index & ~done) == bit, came[n], parts[n])
        if step == 0 and balanced:
            parts[0], parts[1], *blocks = tie(*parts, *turn_blocks(matrix, col_blocks))
            pieces = [
                lax.ppermute(blocks[t], both, scatter_pairs(t, rows_axis, cols_axis))
                for t in reversed(range(col_blocks))
            ]
        if step == len(stages[0]) - 2 and balanced:
            parts[0], parts[1], *pieces = tie(*parts, *pieces)
    first_bit, *other_bits = bits_of(rows_axis)[::-1]

    if balanced:
        chunk = functools.reduce(jnp.add, pieces)
        ring = ring_positions(cols_axis)
        up = [(ring[n], ring[(n + 1) % cols_axis]) for n in range(cols_axis)]
        down = [(b, a) for a, b in up]
        over = [(ring[n], ring[(n + cols_axis // 2) % cols_axis]) for n in range(cols_axis)]
        going, coming = [chunk], [chunk]

        def advance():
            going.append(lax.ppermute(going[-1], "col", up))
            coming.append(lax.ppermute(coming[-1], "col", down))

        advance()
        head, chunk = tie(matrix[:NB], chunk)
        held = spread_apart([(0, head)], "row", first_bit)
        parts[0], parts[1], chunk = tie(*parts, chunk)
        work, inv_t = factor_first(*parts)
        work, going[-1], coming[-1], chunk = tie(work, going[-1], coming[-1], chunk)
        advance()
        opposite = lax.ppermute(chunk, "col", over)
        factor, inv, inv_t = factor_last(work, inv_t)
        inv, going[-1], coming[-1], *values = tie(inv, going[-1], coming[-1], *[v for _, v in held])
        held = [(n, v) for (n, _), v in zip(held, values)]
        for _ in range(cols_axis // 2 - 4):
            advance()
        chunks = [chunk]
        for a, b in zip(going[1:], coming[1:]):
            chunks += [a, b]
        advance()
        chunks += [opposite, going[-1], coming[-1]]
        early = len(chunks) - 3
    else:
        column = from_root(matrix[:, :NB], "col", 0)
        chunks = [column[s * NB : (s + 1) * NB] for s in range(row_blocks)]
        factor, inv, inv_t = factor_last(*factor_first(*parts))
        early = len(chunks)
        held = spread_apart([(0, matrix[:NB])], "row", first_bit)

    for bit in other_bits:
        held = spread_apart(held, "row", bit)
    sources = [matrix] + [v for _, v in sorted(held, key=lambda entry: entry[0])][1:]
    across = solve_across(places[:2], inv, sources)
    out = None
    for begin, end in ((0, early), (early, len(chunks))):
        if begin < end:
            info = jnp.concatenate([places[:2], places[2 + begin : 2 + end]])
            out = update(info, chunks[begin:end], inv_t, factor, across, matrix, out)
    return out


def solution(mesh):
    in_specs = (P("row", "col"),)
    out_specs = P("row", "col")
    return jax.shard_map(
        on_device, mesh=mesh, in_specs=in_specs, out_specs=out_specs, check_vma=False
    )
```

time: 674 us -> 232 us (0.34)
  the two profiles are of different devices: /device:TPU:0 before, /device:TPU:12 now
where the time goes in v2:
time: 232 us; the launch traced here: 230 us
  Pallas kernels  122 us (53%)
  waiting for transfers between devices  50.3 us (22%)
  starting transfers between devices  42.1 us (18%)
  local copies, waits for them, and re-layouts  8.32 us (4%)
  other arithmetic  7.11 us (3%)
    pallas_call x2, Pallas kernels, update(): pl.pallas_call(functools.partial(update_kernel, count, tile), grid_spec=p...  62.3 us
    ppermute x10, waiting for transfers between devices, on_device(): came = [lax.ppermute(parts[n], both, stages[n][step][0]) for n in range(2)]  29.5 us
    pallas_call x1, Pallas kernels, factor_last(): pl.pallas_call(functools.partial(factor_last_kernel, COUNT // 2), out_sha...  20.7 us
    pallas_call x1, Pallas kernels, factor_first(): pl.pallas_call(functools.partial(factor_first_kernel, COUNT // 2), out_sh...  19.5 us
    ppermute x3, waiting for transfers between devices, advance(): going.append(lax.ppermute(going[-1], 'col', up))  18.1 us
    pallas_call x1, Pallas kernels, solve_across(): pl.pallas_call(functools.partial(across_kernel, count), grid_spec=pltpu.P...  12.9 us
    ppermute x3, starting transfers between devices, spread_apart(): lax.ppermute(v, axis, [(n, n | bit)])  12.8 us
    ppermute x10, starting transfers between devices, on_device(): came = [lax.ppermute(parts[n], both, stages[n][step][0]) for n in range(2)]  10.6 us
  transfers between devices with their start and end apart: 24, of which 6 were waited for; matrix products, arithmetic and copies ran while one was open for 4% of the time, Pallas kernels for 41%

profile of v2, /device:TPU:12, one launch (start us, length us, event | category | flops | bytes accessed | tf_op | source)
XLA Modules:
  0.0 230.2 jit_solution(7402425237425329934)
XLA Ops:
  0.0 2.1 pack_corner.1
  2.1 0.7 collective-permute-start
  2.8 0.7 collective-permute-start.1
  3.5 4.6 %turn_blocks.1 = (f32[512,512]{1,0:T(8,128)}, f32[512,512]{1,0:T(8,128)}, f32[512,512]{1,0:T(8,128)}, f32[512,512]{1,0:T(8,128)}) custom-call(f32[4096,2048]{1,0:T(8,128)} %refs_6_.1), custom_call_target="tpu_custom_call" | custom-call | tf_op jit(solution)/shard_map/turn_blocks/pallas_call | solution.py:91
  8.2 0.7 collective-permute-start.2
  8.9 0.7 collective-permute-start.5
  9.6 0.7 collective-permute-start.3
  10.4 1.3 collective-permute-start.6
  11.7 2.1 collective-permute-start.8
  13.7 1.4 collective-permute-start.9
  15.1 2.3 collective-permute-start.10
  17.4 0.7 copy-done.5
  18.1 2.3 %collective-permute-start.11 = (f32[512,512]{1,0:T(8,128)}, f32[512,512]{1,0:T(8,128)}, u32[]{:S(2)}, u32[]{:S(2)}) collective-permute-start(f32[512,512]{1,0:T(8,128)} %get-tuple-element.53), channel_id=1, source_target_pairs={{0,0},{1,9},{2,18},{3,27},{4,4},{5,13},{6,22},{7,31}} | collective-permute-start | bytes 3145736 | tf_op jit(solution)/shard_map/ppermute | solution.py:453
  20.5 6.7 %collective-permute-done.6 = f32[5,128,128]{2,1,0:T(8,128)S(1)} collective-permute-done((f32[5,128,128]{2,1,0:T(8,128)S(1)}, f32[5,128,128]{2,1,0:T(8,128)S(1)}, u32[]{:S(2)}, u32[]{:S(2)}) %collective-permute-start.6) | collective-permute-done | bytes 327712 | tf_op jit(solution)/shard_map/ppermute | solution.py:446
  27.2 1.3 collective-permute-start.4
  28.5 1.0 broadcast_select_fusion.1
  29.5 22.3 %collective-permute-done.4 = f32[5,128,128]{2,1,0:T(8,128)S(1)} collective-permute-done((f32[5,128,128]{2,1,0:T(8,128)S(1)}, f32[5,128,128]{2,1,0:T(8,128)S(1)}, u32[]{:S(2)}, u32[]{:S(2)}) %collective-permute-start.4) | collective-permute-done | bytes 327712 | tf_op jit(solution)/shard_map/ppermute | solution.py:446
  51.8 2.0 collective-permute-start.7
  53.9 4.7 %slice.27 = f32[512,2048]{1,0:T(8,128)} slice(f32[4096,2048]{1,0:T(8,128)} %refs_6_.1), slice={[0:512], [0:2048]} | slice | bytes 8388608 | tf_op jit(solution)/shard_map/slice | solution.py:473
  58.7 3.0 %add_add_fusion.refs_0_ = f32[512,512]{1,0:T(8,128)} fusion(f32[512,512]{1,0:T(8,128)} %collective-permute-done.11, f32[512,512]{1,0:T(8,128)} %collective-permute-done.10, f32[512,512]{1,0:T(8,128)S(1)} %collective-permute-done.8, f32[512,512]{1,0:T(8,128)S(1)} %collective-permute-done.9), kind=kLoop, calls=%fused_computation | loop fusion | flops 786432 | bytes 5242880 | tf_op jit(solution)/shard_map/add | solution.py:461
  61.7 6.6 %collective-permute-start.19 = (f32[512,2048]{1,0:T(8,128)}, f32[512,2048]{1,0:T(8,128)}, u32[]{:S(2)}, u32[]{:S(2)}) collective-permute-start(f32[512,2048]{1,0:T(8,128)} %slice.27), channel_id=1, source_target_pairs={{0,16},{1,17},{2,18},{3,19},{4,20},{5,21},{6,22},{7,23}} | collective-permute-start | bytes 12582920 | tf_op jit(solution)/shard_map/ppermute | solution.py:382
  68.3 2.0 collective-permute-start.14
  70.4 1.3 collective-permute-start.12
  71.7 1.3 collective-permute-start.13
  73.0 0.8 broadcast_select_fusion.9.first_ref
  73.8 0.4 collective-permute-done.13
  74.2 0.8 broadcast_select_fusion.8.second_ref
  75.0 19.5 %factor_first.1 = (f32[512,512]{1,0:T(8,128)}, f32[512,512]{1,0:T(8,128)}) custom-call(f32[5,128,128]{2,1,0:T(8,128)} %broadcast_select_fusion.9.first_ref, f32[5,128,128]{2,1,0:T(8,128)} %broadcast_select_fusion.8.second_ref), custom_call_target="tpu_custom_call" | custom-call | flops 268435456 | bytes 4194304 | tf_op jit(solution)/shard_map/factor_first/pallas_call | solution.py:197
  94.5 3.4 %collective-permute-start.17 = (f32[512,512]{1,0:T(8,128)}, f32[512,512]{1,0:T(8,128)S(1)}, u32[]{:S(2)}, u32[]{:S(2)}) collective-permute-start(f32[512,512]{1,0:T(8,128)} %collective-permute-done.14.refs_1_), channel_id=1, source_target_pairs={{0,2},{2,4},{4,6},{6,7},{7,5},{5,3},{3,1},{1,0},{8,10},{10,12},{12... | collective-permute-start | bytes 3145736 | tf_op jit(solution)/shard_map/ppermute | solution.py:469
  97.9 20.7 %factor_last.1 = (f32[512,512]{1,0:T(8,128)}, f32[512,512]{1,0:T(8,128)}, f32[512,512]{1,0:T(8,128)}) custom-call(f32[512,512]{1,0:T(8,128)} %get-tuple-element.66.work_in, f32[512,512]{1,0:T(8,128)} %get-tuple-element.67.inv_t_in), custom_call_target="tpu_custom_call" | custom-call | flops 268435456 | bytes 4194304 | tf_op jit(solution)/shard_map/factor_last/pallas_call | solution.py:209
  118.6 2.6 %collective-permute-done.17.refs_3_ = f32[512,512]{1,0:T(8,128)S(1)} collective-permute-done((f32[512,512]{1,0:T(8,128)}, f32[512,512]{1,0:T(8,128)S(1)}, u32[]{:S(2)}, u32[]{:S(2)}) %collective-permute-start.17) | collective-permute-done | bytes 1048608 | tf_op jit(solution)/shard_map/ppermute | solution.py:469
  121.2 2.6 %collective-permute-done.18.refs_4_ = f32[512,512]{1,0:T(8,128)S(1)} collective-permute-done((f32[512,512]{1,0:T(8,128)S(1)}, f32[512,512]{1,0:T(8,128)S(1)}, u32[]{:S(2)}, u32[]{:S(2)}) %collective-permute-start.18) | collective-permute-done | bytes 1048608 | tf_op jit(solution)/shard_map/ppermute | solution.py:470
  123.8 3.5 %collective-permute-start.22 = (f32[512,2048]{1,0:T(8,128)}, f32[512,2048]{1,0:T(8,128)}, u32[]{:S(2)}, u32[]{:S(2)}) collective-permute-start(f32[512,2048]{1,0:T(8,128)} %slice.27), channel_id=1, source_target_pairs={{0,8},{1,9},{2,10},{3,11},{4,12},{5,13},{6,14},{7,15}} | collective-permute-start | bytes 12582920 | tf_op jit(solution)/shard_map/ppermute | solution.py:382
  127.3 2.6 %collective-permute-start.23 = (f32[512,2048]{1,0:T(8,128)}, f32[512,2048]{1,0:T(8,128)}, u32[]{:S(2)}, u32[]{:S(2)}) collective-permute-start(f32[512,2048]{1,0:T(8,128)} %collective-permute-done.19.refs_2_), channel_id=1, source_target_pairs={{16,24},{17,25},{18,26},{19,27},{20,28},{21,29},{22,30},{23,31}} | collective-permute-start | bytes 12582920 | tf_op jit(solution)/shard_map/ppermute | solution.py:382
  130.0 0.7 constant_dynamic-slice_fusion
  130.7 0.1 slice_bitcast_fusion.1
  130.7 0.6 pad_add_fusion.info
  131.3 0.1 slice_bitcast_fusion
  131.4 0.7 pad_add_fusion.1.info
  132.1 3.2 %collective-permute-start.16 = (f32[512,512]{1,0:T(8,128)}, f32[512,512]{1,0:T(8,128)S(1)}, u32[]{:S(2)}, u32[]{:S(2)}) collective-permute-start(f32[512,512]{1,0:T(8,128)} %add_add_fusion.refs_0_), channel_id=1, source_target_pairs={{0,7},{2,5},{4,3},{6,1},{7,0},{5,2},{3,4},{1,6},{8,15},{10,13},{12... | collective-permute-start | bytes 3145736 | tf_op jit(solution)/shard_map/ppermute | solution.py:479
  135.3 1.6 collective-permute-start.20
  136.9 0.5 collective-permute-start.21
  137.4 12.9 %solve_across.1.refs_7_.refs_5_ = bf16[1536,2048]{1,0:T(8,128)(2,1)} custom-call(s32[2]{0:T(128)} %copy-done.7, f32[512,512]{1,0:T(8,128)} %get-tuple-element.76.inv_ref, f32[4096,2048]{1,0:T(8,128)} %refs_6_.1, f32[512,2048]{1,0:T(8,128)} %collective-permute-done.22.refs_1_, f32[512,2048]{1,0:T(8,128)} %collective-permute-done.19.refs_2_, ...), custom_call_target="tpu_custom_call" | custom-call | flops 6442450944 | bytes 10485760 | tf_op jit(solution)/shard_map/solve_across/pallas_call | solution.py:248
  150.3 36.4 %update_rows.2.refs_7_ = f32[4096,2048]{1,0:T(8,128)} custom-call(s32[7]{0:T(128)} %pad_add_fusion.1.info, f32[512,512]{1,0:T(8,128)} %add_add_fusion.refs_0_, f32[512,512]{1,0:T(8,128)} %collective-permute-done.14.refs_1_, f32[512,512]{1,0:T(8,128)} %copy-done.8, f32[512,512]{1,0:T(8,128)} %copy-done.9, f32[512,512]{1,0:T(8,128)} %copy-done.10, ...), custom_call_target="tpu_custom_call" | custom-call | flops 24159191040 | bytes 41943040 | tf_op jit(solution)/shard_map/update_rows/pallas_call | solution.py:334
  186.7 15.5 %collective-permute-done.20.refs_1_ = f32[512,512]{1,0:T(8,128)S(1)} collective-permute-done((f32[512,512]{1,0:T(8,128)}, f32[512,512]{1,0:T(8,128)S(1)}, u32[]{:S(2)}, u32[]{:S(2)}) %collective-permute-start.20) | collective-permute-done | bytes 1048608 | tf_op jit(solution)/shard_map/ppermute | solution.py:469
  202.3 1.0 copy-done.1
  203.2 1.1 copy-done.2
  204.3 25.9 %update_rows.3 = f32[4096,2048]{1,0:T(8,128)} custom-call(s32[5]{0:T(128)} %pad_add_fusion.info, f32[512,512]{1,0:T(8,128)} %copy-done, f32[512,512]{1,0:T(8,128)} %copy-done.1, f32[512,512]{1,0:T(8,128)} %copy-done.2, f32[512,512]{1,0:T(8,128)} %get-tuple-element.74.refs_5_.refs_3_, ...), custom_call_target="tpu_custom_call", output_to_operand_aliasing={{}: (8, {})} | custom-call | flops 14495514624 | bytes 25165824 | tf_op jit(solution)/shard_map/update_rows/pallas_call | solution.py:334
  (47 shorter events, 0.4 us)
Async XLA Ops:
  2.1 6.0 %collective-permute-start = (f32[5,128,128]{2,1,0:T(8,128)}, f32[5,128,128]{2,1,0:T(8,128)S(1)}, u32[]{:S(2)}, u32[]{:S(2)}) collective-permute-start(f32[5,128,128]{2,1,0:T(8,128)} %get-tuple-element.42), channel_id=1, source_target_pairs={{0,16}} | collective-permute-start | bytes 983048 | tf_op jit(solution)/shard_map/ppermute | solution.py:446
  2.8 5.3 %collective-permute-start.1 = (f32[5,128,128]{2,1,0:T(8,128)}, f32[5,128,128]{2,1,0:T(8,128)S(1)}, u32[]{:S(2)}, u32[]{:S(2)}) collective-permute-start(f32[5,128,128]{2,1,0:T(8,128)} %get-tuple-element.43), channel_id=1, source_target_pairs={{0,4}} | collective-permute-start | bytes 983048 | tf_op jit(solution)/shard_map/ppermute | solution.py:446
  3.5 4.6 %copy-start.6 = (f32[5,128,128]{2,1,0:T(8,128)S(1)}, f32[5,128,128]{2,1,0:T(8,128)}, u32[]{:S(2)}) copy-start(f32[5,128,128]{2,1,0:T(8,128)} %get-tuple-element.42) | copy-start | bytes 983044
  3.5 4.6 %copy-start.3 = (f32[5,128,128]{2,1,0:T(8,128)S(1)}, f32[5,128,128]{2,1,0:T(8,128)}, u32[]{:S(2)}) copy-start(f32[5,128,128]{2,1,0:T(8,128)} %get-tuple-element.43) | copy-start | bytes 983044
  8.2 1.4 collective-permute-start.2
  8.9 1.4 collective-permute-start.5
  9.6 7.8 %collective-permute-start.3 = (f32[5,128,128]{2,1,0:T(8,128)S(1)}, f32[5,128,128]{2,1,0:T(8,128)S(1)}, u32[]{:S(2)}, u32[]{:S(2)}) collective-permute-start(f32[5,128,128]{2,1,0:T(8,128)S(1)} %broadcast_select_fusion.5), channel_id=1, source_target_pairs={{0,4},{16,20},{1,5},{17,21}} | collective-permute-start | bytes 983048 | tf_op jit(solution)/shard_map/ppermute | solution.py:446
  10.4 16.8 %collective-permute-start.6 = (f32[5,128,128]{2,1,0:T(8,128)S(1)}, f32[5,128,128]{2,1,0:T(8,128)S(1)}, u32[]{:S(2)}, u32[]{:S(2)}) collective-permute-start(f32[5,128,128]{2,1,0:T(8,128)S(1)} %broadcast_select_fusion), channel_id=1, source_target_pairs={{0,1},{4,5},{2,3},{6,7}} | collective-permute-start | bytes 983048 | tf_op jit(solution)/shard_map/ppermute | solution.py:446
  11.7 47.0 %collective-permute-start.8 = (f32[512,512]{1,0:T(8,128)}, f32[512,512]{1,0:T(8,128)S(1)}, u32[]{:S(2)}, u32[]{:S(2)}) collective-permute-start(f32[512,512]{1,0:T(8,128)} %get-tuple-element.50), channel_id=1, source_target_pairs={{0,3},{1,10},{2,17},{3,24},{4,7},{5,14},{6,21},{7,28}} | collective-permute-start | bytes 3145736 | tf_op jit(solution)/shard_map/ppermute | solution.py:453
  13.7 45.0 %collective-permute-start.9 = (f32[512,512]{1,0:T(8,128)}, f32[512,512]{1,0:T(8,128)S(1)}, u32[]{:S(2)}, u32[]{:S(2)}) collective-permute-start(f32[512,512]{1,0:T(8,128)} %get-tuple-element.51), channel_id=1, source_target_pairs={{0,2},{1,11},{2,16},{3,25},{4,6},{5,15},{6,20},{7,29}} | collective-permute-start | bytes 3145736 | tf_op jit(solution)/shard_map/ppermute | solution.py:453
  15.1 43.6 %collective-permute-start.10 = (f32[512,512]{1,0:T(8,128)}, f32[512,512]{1,0:T(8,128)}, u32[]{:S(2)}, u32[]{:S(2)}) collective-permute-start(f32[512,512]{1,0:T(8,128)} %get-tuple-element.52), channel_id=1, source_target_pairs={{0,1},{1,8},{2,19},{3,26},{4,5},{5,12},{6,23},{7,30}} | collective-permute-start | bytes 3145736 | tf_op jit(solution)/shard_map/ppermute | solution.py:453
  17.4 0.7 copy-start.5
  18.1 40.6 %collective-permute-start.11 = (f32[512,512]{1,0:T(8,128)}, f32[512,512]{1,0:T(8,128)}, u32[]{:S(2)}, u32[]{:S(2)}) collective-permute-start(f32[512,512]{1,0:T(8,128)} %get-tuple-element.53), channel_id=1, source_target_pairs={{0,0},{1,9},{2,18},{3,27},{4,4},{5,13},{6,22},{7,31}} | collective-permute-start | bytes 3145736 | tf_op jit(solution)/shard_map/ppermute | solution.py:453
  27.2 1.3 copy-start.4
  27.2 24.7 %collective-permute-start.4 = (f32[5,128,128]{2,1,0:T(8,128)S(1)}, f32[5,128,128]{2,1,0:T(8,128)S(1)}, u32[]{:S(2)}, u32[]{:S(2)}) collective-permute-start(f32[5,128,128]{2,1,0:T(8,128)S(1)} %broadcast_select_fusion.6), channel_id=1, source_target_pairs={{0,2},{16,18},{1,3},{17,19},{4,6},{20,22},{5,7},{21,23}} | collective-permute-start | bytes 983048 | tf_op jit(solution)/shard_map/ppermute | solution.py:446
  51.8 6.8 %collective-permute-start.7 = (f32[5,128,128]{2,1,0:T(8,128)S(1)}, f32[5,128,128]{2,1,0:T(8,128)}, u32[]{:S(2)}, u32[]{:S(2)}) collective-permute-start(f32[5,128,128]{2,1,0:T(8,128)S(1)} %broadcast_select_fusion.1), channel_id=1, source_target_pairs={{0,16},{4,20},{2,18},{6,22},{1,17},{5,21},{3,19},{7,23}} | collective-permute-start | bytes 983048 | tf_op jit(solution)/shard_map/ppermute | solution.py:446
  61.7 62.1 %collective-permute-start.19 = (f32[512,2048]{1,0:T(8,128)}, f32[512,2048]{1,0:T(8,128)}, u32[]{:S(2)}, u32[]{:S(2)}) collective-permute-start(f32[512,2048]{1,0:T(8,128)} %slice.27), channel_id=1, source_target_pairs={{0,16},{1,17},{2,18},{3,19},{4,20},{5,21},{6,22},{7,23}} | collective-permute-start | bytes 12582920 | tf_op jit(solution)/shard_map/ppermute | solution.py:382
  68.3 26.2 %collective-permute-start.15 = (f32[512,512]{1,0:T(8,128)}, f32[512,512]{1,0:T(8,128)S(1)}, u32[]{:S(2)}, u32[]{:S(2)}) collective-permute-start(f32[512,512]{1,0:T(8,128)} %add_add_fusion.refs_0_), channel_id=1, source_target_pairs={{2,0},{4,2},{6,4},{7,6},{5,7},{3,5},{1,3},{0,1},{10,8},{12,10},{14... | collective-permute-start | bytes 3145736 | tf_op jit(solution)/shard_map/ppermute | solution.py:470
  68.3 26.2 %collective-permute-start.14 = (f32[512,512]{1,0:T(8,128)}, f32[512,512]{1,0:T(8,128)}, u32[]{:S(2)}, u32[]{:S(2)}) collective-permute-start(f32[512,512]{1,0:T(8,128)} %add_add_fusion.refs_0_), channel_id=1, source_target_pairs={{0,2},{2,4},{4,6},{6,7},{7,5},{5,3},{3,1},{1,0},{8,10},{10,12},{12... | collective-permute-start | bytes 3145736 | tf_op jit(solution)/shard_map/ppermute | solution.py:469
  70.4 2.6 %collective-permute-start.12 = (f32[5,128,128]{2,1,0:T(8,128)S(1)}, f32[5,128,128]{2,1,0:T(8,128)S(1)}, u32[]{:S(2)}, u32[]{:S(2)}) collective-permute-start(f32[5,128,128]{2,1,0:T(8,128)S(1)} %broadcast_select_fusion.7), channel_id=1, source_target_pairs={{0,8},{16,24},{1,9},{17,25},{4,12},{20,28},{5,13},{21,29},{2,10},{... | collective-permute-start | bytes 983048 | tf_op jit(solution)/shard_map/ppermute | solution.py:446
  71.7 2.5 %collective-permute-start.13 = (f32[5,128,128]{2,1,0:T(8,128)S(1)}, f32[5,128,128]{2,1,0:T(8,128)S(1)}, u32[]{:S(2)}, u32[]{:S(2)}) collective-permute-start(f32[5,128,128]{2,1,0:T(8,128)S(1)} %broadcast_select_fusion.2), channel_id=1, source_target_pairs={{0,8},{4,12},{2,10},{6,14},{1,9},{5,13},{3,11},{7,15},{16,24},{20,... | collective-permute-start | bytes 983048 | tf_op jit(solution)/shard_map/ppermute | solution.py:446
  94.5 37.6 %copy-start.8 = (f32[512,512]{1,0:T(8,128)}, f32[512,512]{1,0:T(8,128)S(1)}, u32[]{:S(2)}) copy-start(f32[512,512]{1,0:T(8,128)S(1)} %collective-permute-done.15.refs_2_) | copy-start | bytes 3145732
  94.5 26.6 %collective-permute-start.17 = (f32[512,512]{1,0:T(8,128)}, f32[512,512]{1,0:T(8,128)S(1)}, u32[]{:S(2)}, u32[]{:S(2)}) collective-permute-start(f32[512,512]{1,0:T(8,128)} %collective-permute-done.14.refs_1_), channel_id=1, source_target_pairs={{0,2},{2,4},{4,6},{6,7},{7,5},{5,3},{3,1},{1,0},{8,10},{10,12},{12... | collective-permute-start | bytes 3145736 | tf_op jit(solution)/shard_map/ppermute | solution.py:469
  97.9 25.9 %collective-permute-start.18 = (f32[512,512]{1,0:T(8,128)S(1)}, f32[512,512]{1,0:T(8,128)S(1)}, u32[]{:S(2)}, u32[]{:S(2)}) collective-permute-start(f32[512,512]{1,0:T(8,128)S(1)} %collective-permute-done.15.refs_2_), channel_id=1, source_target_pairs={{2,0},{4,2},{6,4},{7,6},{5,7},{3,5},{1,3},{0,1},{10,8},{12,10},{14... | collective-permute-start | bytes 3145736 | tf_op jit(solution)/shard_map/ppermute | solution.py:470
  121.2 2.6 %copy-start.9 = (f32[512,512]{1,0:T(8,128)}, f32[512,512]{1,0:T(8,128)S(1)}, u32[]{:S(2)}) copy-start(f32[512,512]{1,0:T(8,128)S(1)} %collective-permute-done.17.refs_3_) | copy-start | bytes 3145732
  123.8 6.2 %copy-start.10 = (f32[512,512]{1,0:T(8,128)}, f32[512,512]{1,0:T(8,128)S(1)}, u32[]{:S(2)}) copy-start(f32[512,512]{1,0:T(8,128)S(1)} %collective-permute-done.18.refs_4_) | copy-start | bytes 3145732
  123.8 13.6 %collective-permute-start.22 = (f32[512,2048]{1,0:T(8,128)}, f32[512,2048]{1,0:T(8,128)}, u32[]{:S(2)}, u32[]{:S(2)}) collective-permute-start(f32[512,2048]{1,0:T(8,128)} %slice.27), channel_id=1, source_target_pairs={{0,8},{1,9},{2,10},{3,11},{4,12},{5,13},{6,14},{7,15}} | collective-permute-start | bytes 12582920 | tf_op jit(solution)/shard_map/ppermute | solution.py:382
  127.3 10.0 %collective-permute-start.23 = (f32[512,2048]{1,0:T(8,128)}, f32[512,2048]{1,0:T(8,128)}, u32[]{:S(2)}, u32[]{:S(2)}) collective-permute-start(f32[512,2048]{1,0:T(8,128)} %collective-permute-done.19.refs_2_), channel_id=1, source_target_pairs={{16,24},{17,25},{18,26},{19,27},{20,28},{21,29},{22,30},{23,31}} | collective-permute-start | bytes 12582920 | tf_op jit(solution)/shard_map/ppermute | solution.py:382
  130.7 6.7 %copy-start.7 = (s32[2]{0:T(128)}, s32[2]{0:T(128)S(1)}, u32[]{:S(2)}) copy-start(s32[2]{0:T(128)S(1)} %slice_bitcast_fusion.2.info) | copy-start | bytes 28
  132.1 54.6 %collective-permute-start.16 = (f32[512,512]{1,0:T(8,128)}, f32[512,512]{1,0:T(8,128)S(1)}, u32[]{:S(2)}, u32[]{:S(2)}) collective-permute-start(f32[512,512]{1,0:T(8,128)} %add_add_fusion.refs_0_), channel_id=1, source_target_pairs={{0,7},{2,5},{4,3},{6,1},{7,0},{5,2},{3,4},{1,6},{8,15},{10,13},{12... | collective-permute-start | bytes 3145736 | tf_op jit(solution)/shard_map/ppermute | solution.py:479
  135.3 67.0 %collective-permute-start.20 = (f32[512,512]{1,0:T(8,128)}, f32[512,512]{1,0:T(8,128)S(1)}, u32[]{:S(2)}, u32[]{:S(2)}) collective-permute-start(f32[512,512]{1,0:T(8,128)} %copy-done.9), channel_id=1, source_target_pairs={{0,2},{2,4},{4,6},{6,7},{7,5},{5,3},{3,1},{1,0},{8,10},{10,12},{12... | collective-permute-start | bytes 3145736 | tf_op jit(solution)/shard_map/ppermute | solution.py:469
  136.9 65.4 %collective-permute-start.21 = (f32[512,512]{1,0:T(8,128)}, f32[512,512]{1,0:T(8,128)S(1)}, u32[]{:S(2)}, u32[]{:S(2)}) collective-permute-start(f32[512,512]{1,0:T(8,128)} %copy-done.10), channel_id=1, source_target_pairs={{2,0},{4,2},{6,4},{7,6},{5,7},{3,5},{1,3},{0,1},{10,8},{12,10},{14... | collective-permute-start | bytes 3145736 | tf_op jit(solution)/shard_map/ppermute | solution.py:470
  186.7 15.6 %copy-start = (f32[512,512]{1,0:T(8,128)}, f32[512,512]{1,0:T(8,128)S(1)}, u32[]{:S(2)}) copy-start(f32[512,512]{1,0:T(8,128)S(1)} %collective-permute-done.16.refs_0_) | copy-start | bytes 3145732
  202.3 1.0 copy-start.1
  203.2 1.1 copy-start.2

commit v3 on v2

--- a/solution.py
+++ b/solution.py
@@ -49,16 +49,19 @@
 
 def store_parts(ref, value, axis, pattern):
     parts = split3(value)
-    for n, k in enumerate(pattern):
-        place = slice(n * NB, (n + 1) * NB)
-        if axis:
-            ref[:, place] = parts[k]
-        else:
-            ref[place] = parts[k]
+    half = NB // 2
+    for h in range(2):
+        for n, k in enumerate(pattern):
+            begin = (h * len(pattern) + n) * half
+            if axis:
+                ref[:, begin : begin + half] = parts[k][:, h * half : (h + 1) * half]
+            else:
+                ref[begin : begin + half] = parts[k][h * half : (h + 1) * half]
 
 
 LEFT_PARTS = (0, 1, 2, 0, 1, 0)
 RIGHT_PARTS = (0, 0, 0, 1, 1, 2)
+DEPTH = len(LEFT_PARTS) * NB
 
 
 def pack_kernel(matrix_ref, first_ref, second_ref):
@@ -84,6 +87,7 @@
 def turn_kernel(count, matrix_ref, *refs):
     for t in range(count):
         refs[t][...] = matrix_ref[:, t * NB : (t + 1) * NB].T
+    refs[count][...] = matrix_ref[...]
 
 
 def turn_blocks(matrix, count):
@@ -91,9 +95,9 @@
     return pl.pallas_call(
         functools.partial(turn_kernel, count),
         grid=(1,),
-        out_shape=(SQUARE,) * count,
+        out_shape=(SQUARE,) * count + (jax.ShapeDtypeStruct((NB, count * NB), jnp.float32),),
         in_specs=[pl.BlockSpec((NB, count * NB), lambda i: (0, 0))],
-        out_specs=(square,) * count,
+        out_specs=(square,) * count + (pl.BlockSpec((NB, count * NB), lambda i: (0, 0)),),
         compiler_params=PARAMS,
         name="turn_blocks",
     )(matrix)
@@ -217,139 +221,179 @@
     )(work, inv_t)
 
 
-def across_kernel(count, info, inv_ref, *refs):
-    sources, out_ref, left, right, rows, sem = refs[:count], *refs[count:]
-    i = pl.program_id(0)
-
-    @pl.when(i == 0)
+def update_kernel(count, ahead, offset, tile, source_count, info, *refs):
+    factor_ref, inv_ref, inv_t_ref, matrix_ref = refs[:4]
+    chunks = refs[4 : 4 + count]
+    sources = refs[4 + count : 4 + count + source_count]
+    out_ref = refs[-12 - ahead]
+    across, rows, arrived, panel, panel3, left, right = refs[-11:-4]
+    chunk_sems, row_sems, across_sem, out_sem = refs[-4:]
+    i, j = pl.program_id(0), pl.program_id(1)
+    tiles = across.shape[1] // tile
+    half, deep = NB // 2, DEPTH // 2
+    first_row = jnp.logical_and(info[0] == 0, info[2 + offset + jnp.maximum(i - ahead, 0)] == 0)
+    first_col = jnp.logical_and(info[1] == 0, j == 0)
+
+    def chunk_copy(n):
+        return pltpu.make_async_copy(chunks[n], arrived.at[n], chunk_sems.at[n])
+
+    def row_copy(n, t):
+        place = pl.ds(t * tile, tile)
+        return pltpu.make_async_copy(
+            sources[n].at[pl.ds(0, NB), place], rows.at[:, place], row_sems.at[t]
+        )
+
+    @pl.when(jnp.logical_and(i == 0, j == 0))
+    def _():
+        if ahead:
+            for n in range(source_count):
+
+                @pl.when(info[0] == n)
+                def _():
+                    for t in range(tiles):
+                        row_copy(n, t).start()
+
+        for n in range(count):
+            chunk_copy(n).start()
+        if ahead:
+            store_parts(left, inv_ref[...], 1, LEFT_PARTS)
+        else:
+            pltpu.make_async_copy(sources[0], across, across_sem).start()
+
+    if ahead:
+
+        @pl.when(i == 0)
+        def _():
+            for t in range(tiles):
+
+                @pl.when(j == t)
+                def _():
+                    row_copy(0, t).wait()
+                    for c in range(t * tile, (t + 1) * tile, NB):
+                        store_parts(right, rows[:, c : c + NB], 0, RIGHT_PARTS)
+                        for h in range(2):
+                            part = slice(h * half, (h + 1) * half)
+                            value = jnp.dot(
+                                left[part, : (h + 1) * deep],
+                                right[: (h + 1) * deep],
+                                preferred_element_type=jnp.float32,
+                            )
+                            high, low = split2(value)
+                            across[h * half : (h + 1) * half, c : c + NB] = high
+                            across[NB + h * half : NB + (h + 1) * half, c : c + NB] = high
+                            across[2 * NB + h * half : 2 * NB + (h + 1) * half, c : c + NB] = low
+
+        handed = pltpu.make_async_copy(across, refs[-12], out_sem)
+
+        @pl.when(jnp.logical_and(i == 1, j == 0))
+        def _():
+            handed.start()
+
+        @pl.when(jnp.logical_and(i == count, j == tiles - 1))
+        def _():
+            handed.wait()
+
+    @pl.when(jnp.logical_and(i == ahead, j == 0))
+    def _():
+        store_parts(right, inv_t_ref[...], 0, RIGHT_PARTS)
+
+    @pl.when(jnp.logical_and(i >= ahead, j == 0))
     def _():
         for n in range(count):
 
-            @pl.when(info[0] == n)
+            @pl.when(i == n + ahead)
             def _():
-                copy = pltpu.make_async_copy(sources[n].at[pl.ds(0, NB)], rows, sem)
-                copy.start()
-                copy.wait()
-
-        store_parts(left, inv_ref[...], 1, LEFT_PARTS)
-
-    columns = pl.ds(pl.multiple_of(i * NB, NB), NB)
-    store_parts(right, rows[:, columns], 0, RIGHT_PARTS)
-    value = jnp.dot(left[...], right[...], preferred_element_type=jnp.float32)
-    high, low = split2(value)
-    out_ref[:NB] = high
-    out_ref[NB : 2 * NB] = high
-    out_ref[2 * NB :] = low
-
-
-def solve_across(info, inv, sources):
-    width = sources[0].shape[1]
-    count = len(sources)
-    return pl.pallas_call(
-        functools.partial(across_kernel, count),
-        grid_spec=pltpu.PrefetchScalarGridSpec(
-            num_scalar_prefetch=1,
-            grid=(width // NB,),
-            in_specs=[pl.BlockSpec((NB, NB), lambda i, info: (0, 0))] + [ANYWHERE] * count,
-            out_specs=pl.BlockSpec((3 * NB, NB), lambda i, info: (0, i)),
-            scratch_shapes=[
-                pltpu.VMEM((NB, 6 * NB), jnp.bfloat16),
-                pltpu.VMEM((6 * NB, NB), jnp.bfloat16),
-                pltpu.VMEM((NB, width), jnp.float32),
-                pltpu.SemaphoreType.DMA,
-            ],
-        ),
-        out_shape=jax.ShapeDtypeStruct((3 * NB, width), jnp.bfloat16),
-        compiler_params=PARAMS,
-        cost_estimate=pl.CostEstimate(
-            flops=12 * NB * NB * width, bytes_accessed=10 * NB * width, transcendentals=0
-        ),
-        name="solve_across",
-    )(info, inv, *sources)
-
-
-def update_kernel(count, tile, info, *refs):
-    chunks = refs[:count]
-    inv_t_ref, factor_ref, across_ref, matrix_ref = refs[count : count + 4]
-    out_ref, panel, panel3, left, right = refs[-5:]
-    i, j = pl.program_id(0), pl.program_id(1)
-    first_row = jnp.logical_and(info[0] == 0, info[2 + i] == 0)
-    first_col = jnp.logical_and(info[1] == 0, j == 0)
-
-    @pl.when(jnp.logical_and(i == 0, j == 0))
-    def _():
-        store_parts(right, inv_t_ref[...], 0, RIGHT_PARTS)
-
-    @pl.when(j == 0)
-    def _():
-        for n in range(count):
-
-            @pl.when(i == n)
-            def _():
-                store_parts(left, chunks[n][...], 1, LEFT_PARTS)
-
-        value = jnp.dot(left[...], right[...], preferred_element_type=jnp.float32)
-        panel[...] = value
-        high, low = split2(value)
-        panel3[:, :NB] = high
-        panel3[:, NB : 2 * NB] = low
-        panel3[:, 2 * NB :] = high
+                chunk_copy(n).wait()
+                store_parts(left, arrived[n], 1, LEFT_PARTS)
+
+        for h in range(2):
+            part = slice(h * half, (h + 1) * half)
+            value = jnp.dot(
+                left[:, : (h + 1) * deep],
+                right[: (h + 1) * deep, part],
+                preferred_element_type=jnp.float32,
+            )
+            panel[:, part] = value
+            high, low = split2(value)
+            panel3[:, h * half : (h + 1) * half] = high
+            panel3[:, NB + h * half : NB + (h + 1) * half] = low
+            panel3[:, 2 * NB + h * half : 2 * NB + (h + 1) * half] = high
 
         @pl.when(first_row)
         def _():
             panel[...] = factor_ref[...]
 
-    @pl.when(first_row)
+    if not ahead:
+
+        @pl.when(jnp.logical_and(i == 0, j == 0))
+        def _():
+            pltpu.make_async_copy(sources[0], across, across_sem).wait()
+
+    @pl.when(jnp.logical_and(i >= ahead, first_row))
     def _():
         out_ref[...] = jnp.zeros_like(out_ref)
 
-    @pl.when(jnp.logical_not(first_row))
+    @pl.when(jnp.logical_and(i >= ahead, jnp.logical_not(first_row)))
     def _():
         columns = pl.ds(pl.multiple_of(j * tile, tile), tile)
-        product = jnp.dot(panel3[...], across_ref[:, columns], preferred_element_type=jnp.float32)
+        product = jnp.dot(panel3[...], across[:, columns], preferred_element_type=jnp.float32)
         out_ref[...] = matrix_ref[...] - product
 
-    @pl.when(first_col)
+    @pl.when(jnp.logical_and(i >= ahead, first_col))
     def _():
         out_ref[:, :NB] = panel[...]
 
 
-def update(info, chunks, inv_t, factor, across, matrix, base):
+def update(info, offset, chunks, factor, inv, inv_t, matrix, sources, base):
     count = len(chunks)
+    ahead = 1 if base is None else 0
     width = matrix.shape[1]
     tile = 2 * NB if width % (2 * NB) == 0 else NB
     whole = lambda i, j, info: (0, 0)
-    moving = lambda i, j, info: (info[2 + i], j)
+
+    def moving(i, j, info):
+        n = i - ahead
+        return info[2 + offset + jnp.maximum(n, 0)], jnp.where(n < 0, 0, j)
+
     square = pl.BlockSpec((NB, NB), whole)
-    in_specs = [square] * (count + 2) + [
-        pl.BlockSpec((3 * NB, width), whole),
-        pl.BlockSpec((NB, tile), moving),
-    ]
-    operands = [info, *chunks, inv_t, factor, across, matrix]
-    aliases = {}
-    if base is not None:
+    block = pl.BlockSpec((NB, tile), moving)
+    across = jax.ShapeDtypeStruct((3 * NB, width), jnp.bfloat16)
+    in_specs = [square] * 3 + [block] + [ANYWHERE] * (count + len(sources))
+    operands = [info, factor, inv, inv_t, matrix, *chunks, *sources]
+    out_shape, out_specs, aliases = [jax.ShapeDtypeStruct(matrix.shape, jnp.float32)], [block], {}
+    if ahead:
+        out_shape.append(across)
+        out_specs.append(ANYWHERE)
+    else:
         in_specs.append(ANYWHERE)
         operands.append(base)
         aliases = {len(operands) - 1: 0}
     return pl.pallas_call(
-        functools.partial(update_kernel, count, tile),
+        functools.partial(update_kernel, count, ahead, offset, tile, len(sources)),
         grid_spec=pltpu.PrefetchScalarGridSpec(
             num_scalar_prefetch=1,
-            grid=(count, width // tile),
+            grid=(count + ahead, width // tile),
             in_specs=in_specs,
-            out_specs=pl.BlockSpec((NB, tile), moving),
+            out_specs=out_specs,
             scratch_shapes=[
+                pltpu.VMEM(across.shape, jnp.bfloat16),
+                pltpu.VMEM((NB, width) if ahead else (8, 128), jnp.float32),
+                pltpu.VMEM((count, NB, NB), jnp.float32),
                 pltpu.VMEM((NB, NB), jnp.float32),
                 pltpu.VMEM((NB, 3 * NB), jnp.bfloat16),
-                pltpu.VMEM((NB, 6 * NB), jnp.bfloat16),
-                pltpu.VMEM((6 * NB, NB), jnp.bfloat16),
+                pltpu.VMEM((NB, DEPTH), jnp.bfloat16),
+                pltpu.VMEM((DEPTH, NB), jnp.bfloat16),
+                pltpu.SemaphoreType.DMA((count,)),
+                pltpu.SemaphoreType.DMA((width // tile,)),
+                pltpu.SemaphoreType.DMA,
+                pltpu.SemaphoreType.DMA,
             ],
         ),
-        out_shape=jax.ShapeDtypeStruct(matrix.shape, jnp.float32),
+        out_shape=out_shape,
         input_output_aliases=aliases,
         compiler_params=PARAMS,
         cost_estimate=pl.CostEstimate(
-            flops=6 * count * NB * NB * (width + 2 * NB),
+            flops=6 * (count + ahead) * NB * NB * (width + 2 * NB),
             bytes_accessed=8 * count * NB * width,
             transcendentals=0,
         ),
@@ -442,19 +486,20 @@
 
     parts = list(pack_corner(matrix))
     stages = [tree_stages(order) for order in corner_orders(rows_axis, cols_axis)]
+    *blocks, head = turn_blocks(matrix, col_blocks)
+    pieces = []
+    if balanced:
+        pieces = [
+            lax.ppermute(blocks[t], both, scatter_pairs(t, rows_axis, cols_axis))
+            for t in reversed(range(col_blocks))
+        ]
     for step in range(len(stages[0])):
+        if step == len(stages[0]) - 1:
+            parts[0], parts[1], *pieces = tie(*parts, *pieces)
         came = [lax.ppermute(parts[n], both, stages[n][step][0]) for n in range(2)]
         for n in range(2):
             _, bit, done = stages[n][step]
             parts[n] = jnp.where((index & ~done) == bit, came[n], parts[n])
-        if step == 0 and balanced:
-            parts[0], parts[1], *blocks = tie(*parts, *turn_blocks(matrix, col_blocks))
-            pieces = [
-                lax.ppermute(blocks[t], both, scatter_pairs(t, rows_axis, cols_axis))
-                for t in reversed(range(col_blocks))
-            ]
-        if step == len(stages[0]) - 2 and balanced:
-            parts[0], parts[1], *pieces = tie(*parts, *pieces)
     first_bit, *other_bits = bits_of(rows_axis)[::-1]
 
     if balanced:
@@ -470,16 +515,23 @@
             coming.append(lax.ppermute(coming[-1], "col", down))
 
         advance()
-        head, chunk = tie(matrix[:NB], chunk)
+        head, chunk = tie(head, chunk)
         held = spread_apart([(0, head)], "row", first_bit)
+        own = [(n, head) for n in (0,)]
+        for bit in other_bits:
+            own = spread_apart(own, "row", bit)
         parts[0], parts[1], chunk = tie(*parts, chunk)
         work, inv_t = factor_first(*parts)
         work, going[-1], coming[-1], chunk = tie(work, going[-1], coming[-1], chunk)
         advance()
         opposite = lax.ppermute(chunk, "col", over)
         factor, inv, inv_t = factor_last(work, inv_t)
-        inv, going[-1], coming[-1], *values = tie(inv, going[-1], coming[-1], *[v for _, v in held])
-        held = [(n, v) for (n, _), v in zip(held, values)]
+        far, value = held[1]
+        inv, going[-1], coming[-1], value, opposite = tie(inv, going[-1], coming[-1], value, opposite)
+        far = [(far, value)]
+        for bit in other_bits:
+            far = spread_apart(far, "row", bit)
+        held = own + far
         for _ in range(cols_axis // 2 - 4):
             advance()
         chunks = [chunk]
@@ -493,17 +545,14 @@
         chunks = [column[s * NB : (s + 1) * NB] for s in range(row_blocks)]
         factor, inv, inv_t = factor_last(*factor_first(*parts))
         early = len(chunks)
-        held = spread_apart([(0, matrix[:NB])], "row", first_bit)
-
-    for bit in other_bits:
-        held = spread_apart(held, "row", bit)
+        held = [(0, head)]
+        for bit in [first_bit, *other_bits]:
+            held = spread_apart(held, "row", bit)
+
     sources = [matrix] + [v for _, v in sorted(held, key=lambda entry: entry[0])][1:]
-    across = solve_across(places[:2], inv, sources)
-    out = None
-    for begin, end in ((0, early), (early, len(chunks))):
-        if begin < end:
-            info = jnp.concatenate([places[:2], places[2 + begin : 2 + end]])
-            out = update(info, chunks[begin:end], inv_t, factor, across, matrix, out)
+    out, across = update(places, 0, chunks[:early], factor, inv, inv_t, matrix, sources, None)
+    if early < len(chunks):
+        (out,) = update(places, early, chunks[early:], factor, inv, inv_t, matrix, [across], out)
     return out
 
 

time: 232 us -> 249 us (1.073)
  the two profiles are of different devices: /device:TPU:12 before, /device:TPU:0 now
where the time goes in v3:
time: 249 us; the launch traced here: 246 us
  Pallas kernels  113 us (45%)
  starting transfers between devices  79.1 us (32%)
  waiting for transfers between devices  44.3 us (18%)
  other arithmetic  6.12 us (2%)
  local copies, waits for them, and re-layouts  2.63 us (1%)
    pallas_call x2, Pallas kernels, update(): pl.pallas_call(functools.partial(update_kernel, count, ahead, offset, til...  65.3 us
    ppermute x3, starting transfers between devices, advance(): going.append(lax.ppermute(going[-1], 'col', up))  25.9 us
    ppermute x10, waiting for transfers between devices, on_device(): came = [lax.ppermute(parts[n], both, stages[n][step][0]) for n in range(2)]  24.3 us
    pallas_call x1, Pallas kernels, factor_last(): pl.pallas_call(functools.partial(factor_last_kernel, COUNT // 2), out_sha...  20.6 us
    ppermute x1, waiting for transfers between devices, on_device(): opposite = lax.ppermute(chunk, 'col', over)  20 us
    pallas_call x1, Pallas kernels, factor_first(): pl.pallas_call(functools.partial(factor_first_kernel, COUNT // 2), out_sh...  19.5 us
    ppermute x10, starting transfers between devices, on_device(): came = [lax.ppermute(parts[n], both, stages[n][step][0]) for n in range(2)]  19.4 us
    ppermute x4, starting transfers between devices, on_device(): lax.ppermute(blocks[t], both, scatter_pairs(t, rows_axis, cols_axis))  17.6 us
  transfers between devices with their start and end apart: 24, of which 7 were waited for; matrix products, arithmetic and copies ran while one was open for 2% of the time, Pallas kernels for 35%

profile of v3, /device:TPU:0, one launch (start us, length us, event | category | flops | bytes accessed | tf_op | source)
XLA Modules:
  0.0 246.1 jit_solution(11758053597979074088)
XLA Ops:
  0.0 2.1 pack_corner.1
  2.1 4.8 %collective-permute-start = (f32[5,128,128]{2,1,0:T(8,128)}, f32[5,128,128]{2,1,0:T(8,128)S(1)}, u32[]{:S(2)}, u32[]{:S(2)}) collective-permute-start(f32[5,128,128]{2,1,0:T(8,128)} %get-tuple-element.39), channel_id=1, source_target_pairs={{0,16}} | collective-permute-start | bytes 983048 | tf_op jit(solution)/shard_map/ppermute | solution.py:499
  6.9 1.8 collective-permute-start.4
  8.7 3.1 %collective-permute-done = f32[5,128,128]{2,1,0:T(8,128)S(1)} collective-permute-done((f32[5,128,128]{2,1,0:T(8,128)}, f32[5,128,128]{2,1,0:T(8,128)S(1)}, u32[]{:S(2)}, u32[]{:S(2)}) %collective-permute-start) | collective-permute-done | bytes 327712 | tf_op jit(solution)/shard_map/ppermute | solution.py:499
  11.8 1.0 broadcast_select_fusion.4
  12.8 1.3 collective-permute-start.1
  14.1 0.0 collective-permute-done.4
  14.2 1.0 broadcast_select_fusion
  15.2 1.3 collective-permute-start.5
  16.5 2.2 collective-permute-done.1
  18.7 1.5 collective-permute-start.2
  20.2 0.8 collective-permute-done.5
  21.1 3.4 %collective-permute-start.6 = (f32[5,128,128]{2,1,0:T(8,128)S(1)}, f32[5,128,128]{2,1,0:T(8,128)S(1)}, u32[]{:S(2)}, u32[]{:S(2)}) collective-permute-start(f32[5,128,128]{2,1,0:T(8,128)S(1)} %broadcast_select_fusion.1), channel_id=1, source_target_pairs={{0,1},{4,5},{2,3},{6,7}} | collective-permute-start | bytes 983048 | tf_op jit(solution)/shard_map/ppermute | solution.py:499
  24.5 5.9 %turn_blocks.1 = (f32[512,512]{1,0:T(8,128)}, f32[512,512]{1,0:T(8,128)}, f32[512,512]{1,0:T(8,128)}, f32[512,512]{1,0:T(8,128)}, f32[512,2048]{1,0:T(8,128)}) custom-call(f32[4096,2048]{1,0:T(8,128)} %refs_3_.3), custom_call_target="tpu_custom_call" | custom-call | tf_op jit(solution)/shard_map/turn_blocks/pallas_call | solution.py:95
  30.5 1.3 collective-permute-start.8
  31.8 4.5 %collective-permute-start.9 = (f32[512,512]{1,0:T(8,128)}, f32[512,512]{1,0:T(8,128)}, u32[]{:S(2)}, u32[]{:S(2)}) collective-permute-start(f32[512,512]{1,0:T(8,128)} %get-tuple-element.42), channel_id=1, source_target_pairs={{0,2},{1,11},{2,16},{3,25},{4,6},{5,15},{6,20},{7,29}} | collective-permute-start | bytes 3145736 | tf_op jit(solution)/shard_map/ppermute | solution.py:493
  36.3 2.3 collective-permute-start.10
  38.6 0.0 collective-permute-done.2
  38.6 9.5 %collective-permute-start.11 = (f32[512,512]{1,0:T(8,128)}, f32[512,512]{1,0:T(8,128)}, u32[]{:S(2)}, u32[]{:S(2)}) collective-permute-start(f32[512,512]{1,0:T(8,128)} %get-tuple-element.44), channel_id=1, source_target_pairs={{0,0},{1,9},{2,18},{3,27},{4,4},{5,13},{6,22},{7,31}} | collective-permute-start | bytes 3145736 | tf_op jit(solution)/shard_map/ppermute | solution.py:493
  48.1 0.0 collective-permute-done.6
  48.2 1.3 collective-permute-start.3
  49.5 13.2 %collective-permute-done.3 = f32[5,128,128]{2,1,0:T(8,128)S(1)} collective-permute-done((f32[5,128,128]{2,1,0:T(8,128)S(1)}, f32[5,128,128]{2,1,0:T(8,128)S(1)}, u32[]{:S(2)}, u32[]{:S(2)}) %collective-permute-start.3) | collective-permute-done | bytes 327712 | tf_op jit(solution)/shard_map/ppermute | solution.py:499
  62.8 1.3 collective-permute-start.7
  64.1 4.5 %collective-permute-done.7 = f32[5,128,128]{2,1,0:T(8,128)S(1)} collective-permute-done((f32[5,128,128]{2,1,0:T(8,128)S(1)}, f32[5,128,128]{2,1,0:T(8,128)S(1)}, u32[]{:S(2)}, u32[]{:S(2)}) %collective-permute-start.7) | collective-permute-done | bytes 327712 | tf_op jit(solution)/shard_map/ppermute | solution.py:499
  68.7 0.0 collective-permute-done.10
  68.7 0.0 collective-permute-done.11
  68.7 2.3 add_add_fusion.refs_4_
  71.0 6.4 %collective-permute-start.18 = (f32[512,2048]{1,0:T(8,128)}, f32[512,2048]{1,0:T(8,128)}, u32[]{:S(2)}, u32[]{:S(2)}) collective-permute-start(f32[512,2048]{1,0:T(8,128)} %get-tuple-element.63), channel_id=1, source_target_pairs={{0,16},{1,17},{2,18},{3,19},{4,20},{5,21},{6,22},{7,23}} | collective-permute-start | bytes 12582920 | tf_op jit(solution)/shard_map/ppermute | solution.py:426
  77.5 2.5 %collective-permute-start.14 = (f32[512,512]{1,0:T(8,128)S(1)}, f32[512,512]{1,0:T(8,128)}, u32[]{:S(2)}, u32[]{:S(2)}) collective-permute-start(f32[512,512]{1,0:T(8,128)S(1)} %add_add_fusion.refs_4_), channel_id=1, source_target_pairs={{0,2},{2,4},{4,6},{6,7},{7,5},{5,3},{3,1},{1,0},{8,10},{10,12},{12... | collective-permute-start | bytes 3145736 | tf_op jit(solution)/shard_map/ppermute | solution.py:514
  80.0 1.3 collective-permute-start.12
  81.3 1.3 collective-permute-start.13
  82.6 0.8 broadcast_select_fusion.9.first_ref
  83.4 0.4 collective-permute-done.13
  83.8 0.8 broadcast_select_fusion.8.second_ref
  84.6 19.5 %factor_first.1 = (f32[512,512]{1,0:T(8,128)}, f32[512,512]{1,0:T(8,128)}) custom-call(f32[5,128,128]{2,1,0:T(8,128)} %broadcast_select_fusion.9.first_ref, f32[5,128,128]{2,1,0:T(8,128)} %broadcast_select_fusion.8.second_ref), custom_call_target="tpu_custom_call" | custom-call | flops 268435456 | bytes 4194304 | tf_op jit(solution)/shard_map/factor_first/pallas_call | solution.py:201
  104.1 2.1 collective-permute-start.16
  106.2 3.3 %collective-permute-start.19 = (f32[512,512]{1,0:T(8,128)S(1)}, f32[512,512]{1,0:T(8,128)S(1)}, u32[]{:S(2)}, u32[]{:S(2)}) collective-permute-start(f32[512,512]{1,0:T(8,128)S(1)} %add_add_fusion.refs_4_), channel_id=1, source_target_pairs={{0,7},{2,5},{4,3},{6,1},{7,0},{5,2},{3,4},{1,6},{8,15},{10,13},{12... | collective-permute-start | bytes 3145736 | tf_op jit(solution)/shard_map/ppermute | solution.py:527
  109.6 3.7 %collective-permute-start.22 = (f32[512,2048]{1,0:T(8,128)}, f32[512,2048]{1,0:T(8,128)}, u32[]{:S(2)}, u32[]{:S(2)}) collective-permute-start(f32[512,2048]{1,0:T(8,128)} %get-tuple-element.63), channel_id=1, source_target_pairs={{0,8},{1,9},{2,10},{3,11},{4,12},{5,13},{6,14},{7,15}} | collective-permute-start | bytes 12582920 | tf_op jit(solution)/shard_map/ppermute | solution.py:426
  113.3 20.6 %factor_last.1 = (f32[512,512]{1,0:T(8,128)}, f32[512,512]{1,0:T(8,128)}, f32[512,512]{1,0:T(8,128)}) custom-call(f32[512,512]{1,0:T(8,128)} %get-tuple-element.57.work_in, f32[512,512]{1,0:T(8,128)} %get-tuple-element.58.inv_t_in), custom_call_target="tpu_custom_call" | custom-call | flops 268435456 | bytes 4194304 | tf_op jit(solution)/shard_map/factor_last/pallas_call | solution.py:213
  134.0 20.0 %collective-permute-done.19.refs_4_ = f32[512,512]{1,0:T(8,128)S(1)} collective-permute-done((f32[512,512]{1,0:T(8,128)S(1)}, f32[512,512]{1,0:T(8,128)S(1)}, u32[]{:S(2)}, u32[]{:S(2)}) %collective-permute-start.19) | collective-permute-done | bytes 1048608 | tf_op jit(solution)/shard_map/ppermute | solution.py:527
  154.0 2.6 %collective-permute-start.23 = (f32[512,2048]{1,0:T(8,128)}, f32[512,2048]{1,0:T(8,128)}, u32[]{:S(2)}, u32[]{:S(2)}) collective-permute-start(f32[512,2048]{1,0:T(8,128)} %collective-permute-done.18.refs_11_), channel_id=1, source_target_pairs={{16,24},{17,25},{18,26},{19,27},{20,28},{21,29},{22,30},{23,31}} | collective-permute-start | bytes 12582920 | tf_op jit(solution)/shard_map/ppermute | solution.py:426
  156.6 1.2 dynamic-slice_bitcast_fusion.info
  157.8 21.3 %collective-permute-start.20 = (f32[512,512]{1,0:T(8,128)}, f32[512,512]{1,0:T(8,128)S(1)}, u32[]{:S(2)}, u32[]{:S(2)}) collective-permute-start(f32[512,512]{1,0:T(8,128)} %collective-permute-done.16.refs_7_), channel_id=1, source_target_pairs={{0,2},{2,4},{4,6},{6,7},{7,5},{5,3},{3,1},{1,0},{8,10},{10,12},{12... | collective-permute-start | bytes 3145736 | tf_op jit(solution)/shard_map/ppermute | solution.py:514
  179.1 0.0 collective-permute-start.21
  179.1 41.3 %update_rows.2 = (f32[4096,2048]{1,0:T(8,128)}, bf16[1536,2048]{1,0:T(8,128)(2,1)}) custom-call(s32[10]{0:T(128)} %dynamic-slice_bitcast_fusion.info, f32[512,512]{1,0:T(8,128)} %get-tuple-element.59.refs_0_, f32[512,512]{1,0:T(8,128)} %get-tuple-element.65.refs_1_, f32[512,512]{1,0:T(8,128)} %get-tuple-element.66.refs_2_, f32[4096,2048]{1,0:T(8,128)} %refs_3_.3, ...), custom_call_target="tpu_custom_call" | custom-call | flops 28991029248 | bytes 41943040 | tf_op jit(solution)/shard_map/update_rows/pallas_call | solution.py:371
  220.5 1.0 copy-done.1
  221.5 0.4 copy-done.2
  221.9 24.0 %update_rows.3 = f32[4096,2048]{1,0:T(8,128)} custom-call(s32[10]{0:T(128)} %dynamic-slice_bitcast_fusion.info, f32[512,512]{1,0:T(8,128)} %get-tuple-element.59.refs_0_, f32[512,512]{1,0:T(8,128)} %get-tuple-element.65.refs_1_, f32[512,512]{1,0:T(8,128)} %get-tuple-element.66.refs_2_, f32[4096,2048]{1,0:T(8,128)} %refs_3_.3, ...), custom_call_target="tpu_custom_call", output_to_operand_aliasing={{}: (9, {})} | custom-call | flops 14495514624 | bytes 25165824 | tf_op jit(solution)/shard_map/update_rows/pallas_call | solution.py:371
  (28 shorter events, 0.3 us)
Async XLA Ops:
  2.1 9.7 %collective-permute-start = (f32[5,128,128]{2,1,0:T(8,128)}, f32[5,128,128]{2,1,0:T(8,128)S(1)}, u32[]{:S(2)}, u32[]{:S(2)}) collective-permute-start(f32[5,128,128]{2,1,0:T(8,128)} %get-tuple-element.39), channel_id=1, source_target_pairs={{0,16}} | collective-permute-start | bytes 983048 | tf_op jit(solution)/shard_map/ppermute | solution.py:499
  6.9 7.2 %collective-permute-start.4 = (f32[5,128,128]{2,1,0:T(8,128)}, f32[5,128,128]{2,1,0:T(8,128)S(1)}, u32[]{:S(2)}, u32[]{:S(2)}) collective-permute-start(f32[5,128,128]{2,1,0:T(8,128)} %get-tuple-element.40), channel_id=1, source_target_pairs={{0,4}} | collective-permute-start | bytes 983048 | tf_op jit(solution)/shard_map/ppermute | solution.py:499
  12.8 5.9 %collective-permute-start.1 = (f32[5,128,128]{2,1,0:T(8,128)S(1)}, f32[5,128,128]{2,1,0:T(8,128)S(1)}, u32[]{:S(2)}, u32[]{:S(2)}) collective-permute-start(f32[5,128,128]{2,1,0:T(8,128)S(1)} %broadcast_select_fusion.4), channel_id=1, source_target_pairs={{0,1},{16,17}} | collective-permute-start | bytes 983048 | tf_op jit(solution)/shard_map/ppermute | solution.py:499
  15.2 5.9 %collective-permute-start.5 = (f32[5,128,128]{2,1,0:T(8,128)S(1)}, f32[5,128,128]{2,1,0:T(8,128)S(1)}, u32[]{:S(2)}, u32[]{:S(2)}) collective-permute-start(f32[5,128,128]{2,1,0:T(8,128)S(1)} %broadcast_select_fusion), channel_id=1, source_target_pairs={{0,2},{4,6}} | collective-permute-start | bytes 983048 | tf_op jit(solution)/shard_map/ppermute | solution.py:499
  18.7 19.9 %collective-permute-start.2 = (f32[5,128,128]{2,1,0:T(8,128)S(1)}, f32[5,128,128]{2,1,0:T(8,128)S(1)}, u32[]{:S(2)}, u32[]{:S(2)}) collective-permute-start(f32[5,128,128]{2,1,0:T(8,128)S(1)} %broadcast_select_fusion.5), channel_id=1, source_target_pairs={{0,4},{16,20},{1,5},{17,21}} | collective-permute-start | bytes 983048 | tf_op jit(solution)/shard_map/ppermute | solution.py:499
  21.1 27.1 %collective-permute-start.6 = (f32[5,128,128]{2,1,0:T(8,128)S(1)}, f32[5,128,128]{2,1,0:T(8,128)S(1)}, u32[]{:S(2)}, u32[]{:S(2)}) collective-permute-start(f32[5,128,128]{2,1,0:T(8,128)S(1)} %broadcast_select_fusion.1), channel_id=1, source_target_pairs={{0,1},{4,5},{2,3},{6,7}} | collective-permute-start | bytes 983048 | tf_op jit(solution)/shard_map/ppermute | solution.py:499
  30.5 38.2 %collective-permute-start.8 = (f32[512,512]{1,0:T(8,128)}, f32[512,512]{1,0:T(8,128)S(1)}, u32[]{:S(2)}, u32[]{:S(2)}) collective-permute-start(f32[512,512]{1,0:T(8,128)} %get-tuple-element.41), channel_id=1, source_target_pairs={{0,3},{1,10},{2,17},{3,24},{4,7},{5,14},{6,21},{7,28}} | collective-permute-start | bytes 3145736 | tf_op jit(solution)/shard_map/ppermute | solution.py:493
  31.8 36.9 %collective-permute-start.9 = (f32[512,512]{1,0:T(8,128)}, f32[512,512]{1,0:T(8,128)}, u32[]{:S(2)}, u32[]{:S(2)}) collective-permute-start(f32[512,512]{1,0:T(8,128)} %get-tuple-element.42), channel_id=1, source_target_pairs={{0,2},{1,11},{2,16},{3,25},{4,6},{5,15},{6,20},{7,29}} | collective-permute-start | bytes 3145736 | tf_op jit(solution)/shard_map/ppermute | solution.py:493
  36.3 32.3 %collective-permute-start.10 = (f32[512,512]{1,0:T(8,128)}, f32[512,512]{1,0:T(8,128)}, u32[]{:S(2)}, u32[]{:S(2)}) collective-permute-start(f32[512,512]{1,0:T(8,128)} %get-tuple-element.43), channel_id=1, source_target_pairs={{0,1},{1,8},{2,19},{3,26},{4,5},{5,12},{6,23},{7,30}} | collective-permute-start | bytes 3145736 | tf_op jit(solution)/shard_map/ppermute | solution.py:493
  38.6 30.0 %collective-permute-start.11 = (f32[512,512]{1,0:T(8,128)}, f32[512,512]{1,0:T(8,128)}, u32[]{:S(2)}, u32[]{:S(2)}) collective-permute-start(f32[512,512]{1,0:T(8,128)} %get-tuple-element.44), channel_id=1, source_target_pairs={{0,0},{1,9},{2,18},{3,27},{4,4},{5,13},{6,22},{7,31}} | collective-permute-start | bytes 3145736 | tf_op jit(solution)/shard_map/ppermute | solution.py:493
  48.2 14.6 %collective-permute-start.3 = (f32[5,128,128]{2,1,0:T(8,128)S(1)}, f32[5,128,128]{2,1,0:T(8,128)S(1)}, u32[]{:S(2)}, u32[]{:S(2)}) collective-permute-start(f32[5,128,128]{2,1,0:T(8,128)S(1)} %broadcast_select_fusion.6), channel_id=1, source_target_pairs={{0,2},{16,18},{1,3},{17,19},{4,6},{20,22},{5,7},{21,23}} | collective-permute-start | bytes 983048 | tf_op jit(solution)/shard_map/ppermute | solution.py:499
  62.8 5.9 %collective-permute-start.7 = (f32[5,128,128]{2,1,0:T(8,128)S(1)}, f32[5,128,128]{2,1,0:T(8,128)S(1)}, u32[]{:S(2)}, u32[]{:S(2)}) collective-permute-start(f32[5,128,128]{2,1,0:T(8,128)S(1)} %broadcast_select_fusion.2), channel_id=1, source_target_pairs={{0,16},{4,20},{2,18},{6,22},{1,17},{5,21},{3,19},{7,23}} | collective-permute-start | bytes 983048 | tf_op jit(solution)/shard_map/ppermute | solution.py:499
  71.0 85.6 %copy-start.3 = (f32[512,512]{1,0:T(8,128)}, f32[512,512]{1,0:T(8,128)S(1)}, u32[]{:S(2)}) copy-start(f32[512,512]{1,0:T(8,128)S(1)} %add_add_fusion.refs_4_) | copy-start | bytes 3145732
  71.0 82.9 %collective-permute-start.18 = (f32[512,2048]{1,0:T(8,128)}, f32[512,2048]{1,0:T(8,128)}, u32[]{:S(2)}, u32[]{:S(2)}) collective-permute-start(f32[512,2048]{1,0:T(8,128)} %get-tuple-element.63), channel_id=1, source_target_pairs={{0,16},{1,17},{2,18},{3,19},{4,20},{5,21},{6,22},{7,23}} | collective-permute-start | bytes 12582920 | tf_op jit(solution)/shard_map/ppermute | solution.py:426
  77.5 26.6 %collective-permute-start.15 = (f32[512,512]{1,0:T(8,128)S(1)}, f32[512,512]{1,0:T(8,128)S(1)}, u32[]{:S(2)}, u32[]{:S(2)}) collective-permute-start(f32[512,512]{1,0:T(8,128)S(1)} %add_add_fusion.refs_4_), channel_id=1, source_target_pairs={{2,0},{4,2},{6,4},{7,6},{5,7},{3,5},{1,3},{0,1},{10,8},{12,10},{14... | collective-permute-start | bytes 3145736 | tf_op jit(solution)/shard_map/ppermute | solution.py:515
  77.5 26.6 %collective-permute-start.14 = (f32[512,512]{1,0:T(8,128)S(1)}, f32[512,512]{1,0:T(8,128)}, u32[]{:S(2)}, u32[]{:S(2)}) collective-permute-start(f32[512,512]{1,0:T(8,128)S(1)} %add_add_fusion.refs_4_), channel_id=1, source_target_pairs={{0,2},{2,4},{4,6},{6,7},{7,5},{5,3},{3,1},{1,0},{8,10},{10,12},{12... | collective-permute-start | bytes 3145736 | tf_op jit(solution)/shard_map/ppermute | solution.py:514
  80.0 2.6 %collective-permute-start.12 = (f32[5,128,128]{2,1,0:T(8,128)S(1)}, f32[5,128,128]{2,1,0:T(8,128)S(1)}, u32[]{:S(2)}, u32[]{:S(2)}) collective-permute-start(f32[5,128,128]{2,1,0:T(8,128)S(1)} %broadcast_select_fusion.7), channel_id=1, source_target_pairs={{0,8},{16,24},{1,9},{17,25},{4,12},{20,28},{5,13},{21,29},{2,10},{... | collective-permute-start | bytes 983048 | tf_op jit(solution)/shard_map/ppermute | solution.py:499
  81.3 2.5 %collective-permute-start.13 = (f32[5,128,128]{2,1,0:T(8,128)S(1)}, f32[5,128,128]{2,1,0:T(8,128)S(1)}, u32[]{:S(2)}, u32[]{:S(2)}) collective-permute-start(f32[5,128,128]{2,1,0:T(8,128)S(1)} %broadcast_select_fusion.3), channel_id=1, source_target_pairs={{0,8},{4,12},{2,10},{6,14},{1,9},{5,13},{3,11},{7,15},{16,24},{20,... | collective-permute-start | bytes 983048 | tf_op jit(solution)/shard_map/ppermute | solution.py:499
  104.1 53.7 %copy-start.4 = (f32[512,512]{1,0:T(8,128)}, f32[512,512]{1,0:T(8,128)S(1)}, u32[]{:S(2)}) copy-start(f32[512,512]{1,0:T(8,128)S(1)} %collective-permute-done.15.refs_6_) | copy-start | bytes 3145732
  104.1 29.8 %collective-permute-start.16 = (f32[512,512]{1,0:T(8,128)}, f32[512,512]{1,0:T(8,128)}, u32[]{:S(2)}, u32[]{:S(2)}) collective-permute-start(f32[512,512]{1,0:T(8,128)} %collective-permute-done.14.refs_5_), channel_id=1, source_target_pairs={{0,2},{2,4},{4,6},{6,7},{7,5},{5,3},{3,1},{1,0},{8,10},{10,12},{12... | collective-permute-start | bytes 3145736 | tf_op jit(solution)/shard_map/ppermute | solution.py:514
  106.2 27.7 %collective-permute-start.17 = (f32[512,512]{1,0:T(8,128)S(1)}, f32[512,512]{1,0:T(8,128)}, u32[]{:S(2)}, u32[]{:S(2)}) collective-permute-start(f32[512,512]{1,0:T(8,128)S(1)} %collective-permute-done.15.refs_6_), channel_id=1, source_target_pairs={{2,0},{4,2},{6,4},{7,6},{5,7},{3,5},{1,3},{0,1},{10,8},{12,10},{14... | collective-permute-start | bytes 3145736 | tf_op jit(solution)/shard_map/ppermute | solution.py:515
  106.2 47.7 %collective-permute-start.19 = (f32[512,512]{1,0:T(8,128)S(1)}, f32[512,512]{1,0:T(8,128)S(1)}, u32[]{:S(2)}, u32[]{:S(2)}) collective-permute-start(f32[512,512]{1,0:T(8,128)S(1)} %add_add_fusion.refs_4_), channel_id=1, source_target_pairs={{0,7},{2,5},{4,3},{6,1},{7,0},{5,2},{3,4},{1,6},{8,15},{10,13},{12... | collective-permute-start | bytes 3145736 | tf_op jit(solution)/shard_map/ppermute | solution.py:527
  109.6 69.6 %collective-permute-start.22 = (f32[512,2048]{1,0:T(8,128)}, f32[512,2048]{1,0:T(8,128)}, u32[]{:S(2)}, u32[]{:S(2)}) collective-permute-start(f32[512,2048]{1,0:T(8,128)} %get-tuple-element.63), channel_id=1, source_target_pairs={{0,8},{1,9},{2,10},{3,11},{4,12},{5,13},{6,14},{7,15}} | collective-permute-start | bytes 12582920 | tf_op jit(solution)/shard_map/ppermute | solution.py:426
  154.0 66.5 %copy-start = (f32[512,512]{1,0:T(8,128)}, f32[512,512]{1,0:T(8,128)S(1)}, u32[]{:S(2)}) copy-start(f32[512,512]{1,0:T(8,128)S(1)} %collective-permute-done.19.refs_4_) | copy-start | bytes 3145732
  154.0 25.2 %collective-permute-start.23 = (f32[512,2048]{1,0:T(8,128)}, f32[512,2048]{1,0:T(8,128)}, u32[]{:S(2)}, u32[]{:S(2)}) collective-permute-start(f32[512,2048]{1,0:T(8,128)} %collective-permute-done.18.refs_11_), channel_id=1, source_target_pairs={{16,24},{17,25},{18,26},{19,27},{20,28},{21,29},{22,30},{23,31}} | collective-permute-start | bytes 12582920 | tf_op jit(solution)/shard_map/ppermute | solution.py:426
  157.8 62.6 %collective-permute-start.20 = (f32[512,512]{1,0:T(8,128)}, f32[512,512]{1,0:T(8,128)S(1)}, u32[]{:S(2)}, u32[]{:S(2)}) collective-permute-start(f32[512,512]{1,0:T(8,128)} %collective-permute-done.16.refs_7_), channel_id=1, source_target_pairs={{0,2},{2,4},{4,6},{6,7},{7,5},{5,3},{3,1},{1,0},{8,10},{10,12},{12... | collective-permute-start | bytes 3145736 | tf_op jit(solution)/shard_map/ppermute | solution.py:514
  179.1 41.3 %collective-permute-start.21 = (f32[512,512]{1,0:T(8,128)}, f32[512,512]{1,0:T(8,128)S(1)}, u32[]{:S(2)}, u32[]{:S(2)}) collective-permute-start(f32[512,512]{1,0:T(8,128)} %collective-permute-done.17.refs_8_), channel_id=1, source_target_pairs={{2,0},{4,2},{6,4},{7,6},{5,7},{3,5},{1,3},{0,1},{10,8},{12,10},{14... | collective-permute-start | bytes 3145736 | tf_op jit(solution)/shard_map/ppermute | solution.py:515
  220.4 1.0 copy-start.1
  220.5 1.4 copy-start.2

commit v4 on v3

--- a/solution.py
+++ b/solution.py
@@ -105,7 +105,6 @@
 
 def reciprocal(value):
     guess = pl.reciprocal(value, approx=True)
-    guess = guess * (2.0 - value * guess)
     return guess * (2.0 - value * guess)
 
 
@@ -444,7 +443,7 @@
     last = cols_axis // 2 - 1
     for step in range(1, last):
         shifts += [-step, step]
-    return shifts + [cols_axis // 2, -last, last]
+    return shifts + [-last, last, cols_axis // 2]
 
 
 def place_table(rows_axis, cols_axis, balanced, row_blocks):
@@ -487,72 +486,80 @@
     parts = list(pack_corner(matrix))
     stages = [tree_stages(order) for order in corner_orders(rows_axis, cols_axis)]
     *blocks, head = turn_blocks(matrix, col_blocks)
-    pieces = []
-    if balanced:
-        pieces = [
-            lax.ppermute(blocks[t], both, scatter_pairs(t, rows_axis, cols_axis))
-            for t in reversed(range(col_blocks))
-        ]
+    first_bit, *other_bits = bits_of(rows_axis)[::-1]
+    far = None
     for step in range(len(stages[0])):
-        if step == len(stages[0]) - 1:
-            parts[0], parts[1], *pieces = tie(*parts, *pieces)
+        if step == len(stages[0]) - 1 and balanced and False:
+            parts[0], parts[1], far = tie(*parts, far)
         came = [lax.ppermute(parts[n], both, stages[n][step][0]) for n in range(2)]
         for n in range(2):
             _, bit, done = stages[n][step]
             parts[n] = jnp.where((index & ~done) == bit, came[n], parts[n])
-    first_bit, *other_bits = bits_of(rows_axis)[::-1]
+        if step == 0:
+            parts[0], parts[1], head, *blocks = tie(*parts, head, *blocks)
+        if step == 0 and balanced:
+            _, far = spread_apart([(0, head)], "row", first_bit)[1]
+        if step == len(stages[0]) - 2 and balanced:
+            parts[0], parts[1], *blocks = tie(*parts, *blocks)
+            pieces = [
+                lax.ppermute(blocks[t], both, scatter_pairs(t, rows_axis, cols_axis))
+                for t in reversed(range(col_blocks))
+            ]
 
     if balanced:
-        chunk = functools.reduce(jnp.add, pieces)
         ring = ring_positions(cols_axis)
         up = [(ring[n], ring[(n + 1) % cols_axis]) for n in range(cols_axis)]
         down = [(b, a) for a, b in up]
-        over = [(ring[n], ring[(n + cols_axis // 2) % cols_axis]) for n in range(cols_axis)]
-        going, coming = [chunk], [chunk]
-
-        def advance():
-            going.append(lax.ppermute(going[-1], "col", up))
-            coming.append(lax.ppermute(coming[-1], "col", down))
-
-        advance()
-        head, chunk = tie(head, chunk)
-        held = spread_apart([(0, head)], "row", first_bit)
-        own = [(n, head) for n in (0,)]
+
+        def advance(going, coming):
+            return lax.ppermute(going, "col", up), lax.ppermute(coming, "col", down)
+
+        own = [(0, head)]
         for bit in other_bits:
             own = spread_apart(own, "row", bit)
-        parts[0], parts[1], chunk = tie(*parts, chunk)
         work, inv_t = factor_first(*parts)
-        work, going[-1], coming[-1], chunk = tie(work, going[-1], coming[-1], chunk)
-        advance()
-        opposite = lax.ppermute(chunk, "col", over)
-        factor, inv, inv_t = factor_last(work, inv_t)
-        far, value = held[1]
-        inv, going[-1], coming[-1], value, opposite = tie(inv, going[-1], coming[-1], value, opposite)
-        far = [(far, value)]
+        work, far, *pieces = tie(work, far, *pieces)
+        far = [(first_bit, far)]
         for bit in other_bits:
             far = spread_apart(far, "row", bit)
         held = own + far
-        for _ in range(cols_axis // 2 - 4):
-            advance()
-        chunks = [chunk]
-        for a, b in zip(going[1:], coming[1:]):
-            chunks += [a, b]
-        advance()
-        chunks += [opposite, going[-1], coming[-1]]
-        early = len(chunks) - 3
+        chunk = functools.reduce(jnp.add, pieces)
+        chunks = [[chunk]]
+        going, coming = advance(chunk, chunk)
+        work, chunk = tie(work, chunk)
+        factor, inv, inv_t = factor_last(work, inv_t)
+        inv, going, coming = tie(inv, going, coming)
+        chunks.append([going, coming])
+        going, coming = advance(going, coming)
     else:
         column = from_root(matrix[:, :NB], "col", 0)
-        chunks = [column[s * NB : (s + 1) * NB] for s in range(row_blocks)]
+        chunks = [[column[s * NB : (s + 1) * NB] for s in range(row_blocks)]]
         factor, inv, inv_t = factor_last(*factor_first(*parts))
-        early = len(chunks)
         held = [(0, head)]
         for bit in [first_bit, *other_bits]:
             held = spread_apart(held, "row", bit)
 
     sources = [matrix] + [v for _, v in sorted(held, key=lambda entry: entry[0])][1:]
-    out, across = update(places, 0, chunks[:early], factor, inv, inv_t, matrix, sources, None)
-    if early < len(chunks):
-        (out,) = update(places, early, chunks[early:], factor, inv, inv_t, matrix, [across], out)
+    place = len(chunks[0])
+    out, across = update(places, 0, chunks[0], factor, inv, inv_t, matrix, sources, None)
+
+    def more(out, part, place):
+        return update(places, place, part, factor, inv, inv_t, matrix, [across], out)[0]
+
+    if balanced:
+        waiting = chunks[1]
+        for step in range(2, cols_axis // 2):
+            out, going, coming = tie(out, going, coming)
+            waiting = waiting + [going, coming]
+            if step < cols_axis // 2 - 1:
+                going, coming = advance(going, coming)
+            else:
+                top = lax.ppermute(going[: NB // 2], "col", up)
+                bottom = lax.ppermute(coming[NB // 2 :], "col", down)
+            out = more(out, waiting, place)
+            place += len(waiting)
+            waiting = []
+        out = more(out, [jnp.concatenate([top, bottom], 0)], place)
     return out
 
 

time: 249 us -> 235 us (0.944)
  starting transfers between devices: 79.1 us -> 57.4 us
  Pallas kernels: 113 us -> 121 us
  waiting for transfers between devices: 44.3 us -> 47.2 us
    ppermute x7 -> x8, starting transfers between devices: 29.2 us -> 8.71 us  [the longest x6 6.63 us: advance(): return (lax.ppermute(going, 'col', up), lax.ppermute(coming, 'col', down))]
    ppermute x10, waiting for transfers between devices: 24.3 us -> 36.2 us  [on_device(): came = [lax.ppermute(parts[n], both, stages[n][step][0]) for n in range(2)]]
    pallas_call x2 -> x4, Pallas kernels: 65.3 us -> 75 us  [update(): pl.pallas_call(functools.partial(update_kernel, count, ahead, offset, til...]
    ppermute x7 -> x8, waiting for transfers between devices: 20 us -> 11 us  [the longest x6 11 us: advance(): return (lax.ppermute(going, 'col', up), lax.ppermute(coming, 'col', down))]
    ppermute x3, starting transfers between devices: 12.8 us -> 9.48 us  [spread_apart(): lax.ppermute(v, axis, [(n, n | bit)])]
  transfers between devices with their start and end apart: 24 -> 25, of which waited for: 7 -> 9; matrix products, arithmetic and copies ran while one was open for 2% -> 2% of each run, Pallas kernels for 35% -> 46%
where the time goes in v4:
time: 235 us; the launch traced here: 233 us
  Pallas kernels  121 us (51%)
  starting transfers between devices  57.4 us (24%)
  waiting for transfers between devices  47.2 us (20%)
  other arithmetic  5.91 us (3%)
    pallas_call x4, Pallas kernels, update(): pl.pallas_call(functools.partial(update_kernel, count, ahead, offset, til...  75 us
    ppermute x10, waiting for transfers between devices, on_device(): came = [lax.ppermute(parts[n], both, stages[n][step][0]) for n in range(2)]  36.2 us
    ppermute x10, starting transfers between devices, on_device(): came = [lax.ppermute(parts[n], both, stages[n][step][0]) for n in range(2)]  20.6 us
    pallas_call x1, Pallas kernels, factor_last(): pl.pallas_call(functools.partial(factor_last_kernel, COUNT // 2), out_sha...  19.5 us
    ppermute x4, starting transfers between devices, on_device(): lax.ppermute(blocks[t], both, scatter_pairs(t, rows_axis, cols_axis))  18.7 us
    pallas_call x1, Pallas kernels, factor_first(): pl.pallas_call(functools.partial(factor_first_kernel, COUNT // 2), out_sh...  18.4 us
    ppermute x6, waiting for transfers between devices, advance(): return (lax.ppermute(going, 'col', up), lax.ppermute(coming, 'col', down))  11 us
    ppermute x3, starting transfers between devices, spread_apart(): lax.ppermute(v, axis, [(n, n | bit)])  9.48 us
  transfers between devices with their start and end apart: 25, of which 9 were waited for; matrix products, arithmetic and copies ran while one was open for 2% of the time, Pallas kernels for 46%

profile of v4, /device:TPU:0, one launch (start us, length us, event | category | flops | bytes accessed | tf_op | source)
XLA Modules:
  0.0 233.4 jit_solution(2153749900640444799)
XLA Ops:
  0.0 2.1 pack_corner.1
  2.1 5.0 %collective-permute-start = (f32[5,128,128]{2,1,0:T(8,128)}, f32[5,128,128]{2,1,0:T(8,128)S(1)}, u32[]{:S(2)}, u32[]{:S(2)}) collective-permute-start(f32[5,128,128]{2,1,0:T(8,128)} %get-tuple-element.48), channel_id=1, source_target_pairs={{0,16}} | collective-permute-start | bytes 983048 | tf_op jit(solution)/shard_map/ppermute | solution.py:494
  7.1 1.8 collective-permute-start.1
  8.9 5.9 %turn_blocks.1 = (f32[512,512]{1,0:T(8,128)}, f32[512,512]{1,0:T(8,128)}, f32[512,512]{1,0:T(8,128)}, f32[512,512]{1,0:T(8,128)}, f32[512,2048]{1,0:T(8,128)}) custom-call(f32[4096,2048]{1,0:T(8,128)} %refs_3_.7), custom_call_target="tpu_custom_call" | custom-call | tf_op jit(solution)/shard_map/turn_blocks/pallas_call | solution.py:95
  14.9 3.5 %collective-permute-start.10 = (f32[512,2048]{1,0:T(8,128)}, f32[512,2048]{1,0:T(8,128)}, u32[]{:S(2)}, u32[]{:S(2)}) collective-permute-start(f32[512,2048]{1,0:T(8,128)} %get-tuple-element.64), channel_id=1, source_target_pairs={{0,16},{1,17},{2,18},{3,19},{4,20},{5,21},{6,22},{7,23}} | collective-permute-start | bytes 12582920 | tf_op jit(solution)/shard_map/ppermute | solution.py:425
  18.4 1.6 collective-permute-start.2
  20.0 1.3 collective-permute-start.5
  21.3 3.2 %collective-permute-done.2 = f32[5,128,128]{2,1,0:T(8,128)S(1)} collective-permute-done((f32[5,128,128]{2,1,0:T(8,128)S(1)}, f32[5,128,128]{2,1,0:T(8,128)S(1)}, u32[]{:S(2)}, u32[]{:S(2)}) %collective-permute-start.2) | collective-permute-done | bytes 327712 | tf_op jit(solution)/shard_map/ppermute | solution.py:494
  24.6 1.3 collective-permute-start.3
  26.0 4.4 %collective-permute-start.6 = (f32[5,128,128]{2,1,0:T(8,128)S(1)}, f32[5,128,128]{2,1,0:T(8,128)S(1)}, u32[]{:S(2)}, u32[]{:S(2)}) collective-permute-start(f32[5,128,128]{2,1,0:T(8,128)S(1)} %broadcast_select_fusion), channel_id=1, source_target_pairs={{0,1},{4,5},{2,3},{6,7}} | collective-permute-start | bytes 983048 | tf_op jit(solution)/shard_map/ppermute | solution.py:494
  30.4 0.1 collective-permute-done.3
  30.5 1.3 collective-permute-start.4
  31.8 3.1 %collective-permute-done.6 = f32[5,128,128]{2,1,0:T(8,128)S(1)} collective-permute-done((f32[5,128,128]{2,1,0:T(8,128)S(1)}, f32[5,128,128]{2,1,0:T(8,128)S(1)}, u32[]{:S(2)}, u32[]{:S(2)}) %collective-permute-start.6) | collective-permute-done | bytes 327712 | tf_op jit(solution)/shard_map/ppermute | solution.py:494
  35.0 1.3 collective-permute-start.7
  36.3 0.1 collective-permute-done.4
  36.4 29.7 %collective-permute-done.7 = f32[5,128,128]{2,1,0:T(8,128)S(1)} collective-permute-done((f32[5,128,128]{2,1,0:T(8,128)S(1)}, f32[5,128,128]{2,1,0:T(8,128)S(1)}, u32[]{:S(2)}, u32[]{:S(2)}) %collective-permute-start.7) | collective-permute-done | bytes 327712 | tf_op jit(solution)/shard_map/ppermute | solution.py:494
  66.1 1.3 collective-permute-start.8
  67.4 1.3 collective-permute-start.9
  68.8 2.6 %collective-permute-start.11 = (f32[512,512]{1,0:T(8,128)}, f32[512,512]{1,0:T(8,128)S(1)}, u32[]{:S(2)}, u32[]{:S(2)}) collective-permute-start(f32[512,512]{1,0:T(8,128)} %get-tuple-element.65), channel_id=1, source_target_pairs={{0,3},{1,10},{2,17},{3,24},{4,7},{5,14},{6,21},{7,28}} | collective-permute-start | bytes 3145736 | tf_op jit(solution)/shard_map/ppermute | solution.py:505
  71.4 4.3 %collective-permute-start.12 = (f32[512,512]{1,0:T(8,128)}, f32[512,512]{1,0:T(8,128)S(1)}, u32[]{:S(2)}, u32[]{:S(2)}) collective-permute-start(f32[512,512]{1,0:T(8,128)} %get-tuple-element.66), channel_id=1, source_target_pairs={{0,2},{1,11},{2,16},{3,25},{4,6},{5,15},{6,20},{7,29}} | collective-permute-start | bytes 3145736 | tf_op jit(solution)/shard_map/ppermute | solution.py:505
  75.7 0.0 collective-permute-done.8
  75.8 2.3 collective-permute-start.13
  78.0 9.4 %collective-permute-start.14 = (f32[512,512]{1,0:T(8,128)}, f32[512,512]{1,0:T(8,128)}, u32[]{:S(2)}, u32[]{:S(2)}) collective-permute-start(f32[512,512]{1,0:T(8,128)} %get-tuple-element.68), channel_id=1, source_target_pairs={{0,0},{1,9},{2,18},{3,27},{4,4},{5,13},{6,22},{7,31}} | collective-permute-start | bytes 3145736 | tf_op jit(solution)/shard_map/ppermute | solution.py:505
  87.5 0.8 broadcast_select_fusion.9.first_ref
  88.2 0.8 broadcast_select_fusion.8.second_ref
  89.0 18.4 %factor_first.1 = (f32[512,512]{1,0:T(8,128)}, f32[512,512]{1,0:T(8,128)}) custom-call(f32[5,128,128]{2,1,0:T(8,128)} %broadcast_select_fusion.9.first_ref, f32[5,128,128]{2,1,0:T(8,128)} %broadcast_select_fusion.8.second_ref), custom_call_target="tpu_custom_call" | custom-call | flops 268435456 | bytes 4194304 | tf_op jit(solution)/shard_map/factor_first/pallas_call | solution.py:200
  107.4 3.3 %collective-permute-start.17 = (f32[512,2048]{1,0:T(8,128)}, f32[512,2048]{1,0:T(8,128)}, u32[]{:S(2)}, u32[]{:S(2)}) collective-permute-start(f32[512,2048]{1,0:T(8,128)} %get-tuple-element.64), channel_id=1, source_target_pairs={{0,8},{1,9},{2,10},{3,11},{4,12},{5,13},{6,14},{7,15}} | collective-permute-start | bytes 12582920 | tf_op jit(solution)/shard_map/ppermute | solution.py:425
  110.7 2.6 %collective-permute-start.18 = (f32[512,2048]{1,0:T(8,128)}, f32[512,2048]{1,0:T(8,128)}, u32[]{:S(2)}, u32[]{:S(2)}) collective-permute-start(f32[512,2048]{1,0:T(8,128)} %collective-permute-done.10.refs_7_), channel_id=1, source_target_pairs={{16,24},{17,25},{18,26},{19,27},{20,28},{21,29},{22,30},{23,31}} | collective-permute-start | bytes 12582920 | tf_op jit(solution)/shard_map/ppermute | solution.py:425
  113.4 2.0 add_add_fusion.refs_4_
  115.4 0.1 collective-permute-start.16
  115.5 2.0 collective-permute-start.15
  117.5 19.5 %factor_last.1 = (f32[512,512]{1,0:T(8,128)}, f32[512,512]{1,0:T(8,128)}, f32[512,512]{1,0:T(8,128)}) custom-call(f32[512,512]{1,0:T(8,128)} %get-tuple-element.74.work_in, f32[512,512]{1,0:T(8,128)} %get-tuple-element.75.inv_t_in), custom_call_target="tpu_custom_call" | custom-call | flops 268435456 | bytes 4194304 | tf_op jit(solution)/shard_map/factor_last/pallas_call | solution.py:212
  137.0 1.0 collective-permute-done.16.refs_5_
  138.0 1.1 collective-permute-done.15.refs_4_
  139.2 2.5 %collective-permute-start.19 = (f32[512,512]{1,0:T(8,128)}, f32[512,512]{1,0:T(8,128)}, u32[]{:S(2)}, u32[]{:S(2)}) collective-permute-start(f32[512,512]{1,0:T(8,128)} %collective-permute-done.15.refs_4_), channel_id=1, source_target_pairs={{0,2},{2,4},{4,6},{6,7},{7,5},{5,3},{3,1},{1,0},{8,10},{10,12},{12... | collective-permute-start | bytes 3145736 | tf_op jit(solution)/shard_map/ppermute | solution.py:515
  141.7 0.0 collective-permute-start.20
  141.7 1.2 dynamic-slice_bitcast_fusion.info
  142.9 15.4 %update_rows.4 = (f32[4096,2048]{1,0:T(8,128)}, bf16[1536,2048]{1,0:T(8,128)(2,1)}) custom-call(s32[10]{0:T(128)} %dynamic-slice_bitcast_fusion.info, f32[512,512]{1,0:T(8,128)} %get-tuple-element.76.refs_0_, f32[512,512]{1,0:T(8,128)} %get-tuple-element.78.refs_1_, f32[512,512]{1,0:T(8,128)} %get-tuple-element.79.refs_2_, f32[4096,2048]{1,0:T(8,128)} %refs_3_.7, ...), custom_call_target="tpu_custom_call" | custom-call | flops 9663676416 | bytes 8388608 | tf_op jit(solution)/shard_map/update_rows/pallas_call | solution.py:370
  158.3 6.5 %collective-permute-done.19.refs_6_ = f32[512,512]{1,0:T(8,128)} collective-permute-done((f32[512,512]{1,0:T(8,128)}, f32[512,512]{1,0:T(8,128)}, u32[]{:S(2)}, u32[]{:S(2)}) %collective-permute-start.19) | collective-permute-done | bytes 1048608 | tf_op jit(solution)/shard_map/ppermute | solution.py:515
  164.8 2.4 %collective-permute-done.20.refs_7_ = f32[512,512]{1,0:T(8,128)} collective-permute-done((f32[512,512]{1,0:T(8,128)S(1)}, f32[512,512]{1,0:T(8,128)}, u32[]{:S(2)}, u32[]{:S(2)}) %collective-permute-start.20) | collective-permute-done | bytes 1048608 | tf_op jit(solution)/shard_map/ppermute | solution.py:515
  167.2 1.0 collective-permute-start.21
  168.2 1.0 collective-permute-start.22
  169.2 30.4 %update_rows.5.refs_7_ = f32[4096,2048]{1,0:T(8,128)} custom-call(s32[10]{0:T(128)} %dynamic-slice_bitcast_fusion.info, f32[512,512]{1,0:T(8,128)} %get-tuple-element.76.refs_0_, f32[512,512]{1,0:T(8,128)} %get-tuple-element.78.refs_1_, f32[512,512]{1,0:T(8,128)} %get-tuple-element.79.refs_2_, ...), custom_call_target="tpu_custom_call", output_to_operand_aliasing={{}: (10, {})} | custom-call | flops 19327352832 | bytes 33554432 | tf_op jit(solution)/shard_map/update_rows/pallas_call | solution.py:370
  199.7 0.1 collective-permute-start.23
  199.8 2.0 collective-permute-start.24
  201.8 17.8 %update_rows.6.refs_6_ = f32[4096,2048]{1,0:T(8,128)} custom-call(s32[10]{0:T(128)} %dynamic-slice_bitcast_fusion.info, f32[512,512]{1,0:T(8,128)} %get-tuple-element.76.refs_0_, f32[512,512]{1,0:T(8,128)} %get-tuple-element.78.refs_1_, f32[512,512]{1,0:T(8,128)} %get-tuple-element.79.refs_2_, f32[4096,2048]{1,0:T(8,128)} %refs_3_.7, ...), custom_call_target="tpu_custom_call", output_to_operand_aliasing={{}: (8, {})} | custom-call | flops 9663676416 | bytes 16777216 | tf_op jit(solution)/shard_map/update_rows/pallas_call | solution.py:370
  219.6 2.1 pad_maximum_fusion.refs_4_
  221.7 11.5 %update_rows.7 = f32[4096,2048]{1,0:T(8,128)} custom-call(s32[10]{0:T(128)} %dynamic-slice_bitcast_fusion.info, f32[512,512]{1,0:T(8,128)} %get-tuple-element.76.refs_0_, f32[512,512]{1,0:T(8,128)} %get-tuple-element.78.refs_1_, f32[512,512]{1,0:T(8,128)} %get-tuple-element.79.refs_2_, f32[4096,2048]{1,0:T(8,128)} %refs_3_.7, ...), custom_call_target="tpu_custom_call", output_to_operand_aliasing={{}: (7, {})} | custom-call | flops 4831838208 | bytes 8388608 | tf_op jit(solution)/shard_map/update_rows/pallas_call | solution.py:370
  (37 shorter events, 0.4 us)
Async XLA Ops:
  2.1 12.7 %copy-start.5 = (f32[5,128,128]{2,1,0:T(8,128)S(1)}, f32[5,128,128]{2,1,0:T(8,128)}, u32[]{:S(2)}) copy-start(f32[5,128,128]{2,1,0:T(8,128)} %get-tuple-element.48) | copy-start | bytes 983044
  2.1 12.8 %copy-start.4 = (f32[5,128,128]{2,1,0:T(8,128)S(1)}, f32[5,128,128]{2,1,0:T(8,128)}, u32[]{:S(2)}) copy-start(f32[5,128,128]{2,1,0:T(8,128)} %get-tuple-element.49) | copy-start | bytes 983044
  2.1 12.7 %collective-permute-start = (f32[5,128,128]{2,1,0:T(8,128)}, f32[5,128,128]{2,1,0:T(8,128)S(1)}, u32[]{:S(2)}, u32[]{:S(2)}) collective-permute-start(f32[5,128,128]{2,1,0:T(8,128)} %get-tuple-element.48), channel_id=1, source_target_pairs={{0,16}} | collective-permute-start | bytes 983048 | tf_op jit(solution)/shard_map/ppermute | solution.py:494
  7.1 7.8 %collective-permute-start.1 = (f32[5,128,128]{2,1,0:T(8,128)}, f32[5,128,128]{2,1,0:T(8,128)S(1)}, u32[]{:S(2)}, u32[]{:S(2)}) collective-permute-start(f32[5,128,128]{2,1,0:T(8,128)} %get-tuple-element.49), channel_id=1, source_target_pairs={{0,4}} | collective-permute-start | bytes 983048 | tf_op jit(solution)/shard_map/ppermute | solution.py:494
  14.9 95.8 %collective-permute-start.10 = (f32[512,2048]{1,0:T(8,128)}, f32[512,2048]{1,0:T(8,128)}, u32[]{:S(2)}, u32[]{:S(2)}) collective-permute-start(f32[512,2048]{1,0:T(8,128)} %get-tuple-element.64), channel_id=1, source_target_pairs={{0,16},{1,17},{2,18},{3,19},{4,20},{5,21},{6,22},{7,23}} | collective-permute-start | bytes 12582920 | tf_op jit(solution)/shard_map/ppermute | solution.py:425
  18.4 6.1 %collective-permute-start.2 = (f32[5,128,128]{2,1,0:T(8,128)S(1)}, f32[5,128,128]{2,1,0:T(8,128)S(1)}, u32[]{:S(2)}, u32[]{:S(2)}) collective-permute-start(f32[5,128,128]{2,1,0:T(8,128)S(1)} %broadcast_select_fusion.4), channel_id=1, source_target_pairs={{0,1},{16,17}} | collective-permute-start | bytes 983048 | tf_op jit(solution)/shard_map/ppermute | solution.py:494
  20.0 5.9 %collective-permute-start.5 = (f32[5,128,128]{2,1,0:T(8,128)S(1)}, f32[5,128,128]{2,1,0:T(8,128)S(1)}, u32[]{:S(2)}, u32[]{:S(2)}) collective-permute-start(f32[5,128,128]{2,1,0:T(8,128)S(1)} %broadcast_select_fusion.3), channel_id=1, source_target_pairs={{0,2},{4,6}} | collective-permute-start | bytes 983048 | tf_op jit(solution)/shard_map/ppermute | solution.py:494
  24.6 5.9 %collective-permute-start.3 = (f32[5,128,128]{2,1,0:T(8,128)S(1)}, f32[5,128,128]{2,1,0:T(8,128)S(1)}, u32[]{:S(2)}, u32[]{:S(2)}) collective-permute-start(f32[5,128,128]{2,1,0:T(8,128)S(1)} %broadcast_select_fusion.5), channel_id=1, source_target_pairs={{0,4},{16,20},{1,5},{17,21}} | collective-permute-start | bytes 983048 | tf_op jit(solution)/shard_map/ppermute | solution.py:494
  26.0 9.0 %collective-permute-start.6 = (f32[5,128,128]{2,1,0:T(8,128)S(1)}, f32[5,128,128]{2,1,0:T(8,128)S(1)}, u32[]{:S(2)}, u32[]{:S(2)}) collective-permute-start(f32[5,128,128]{2,1,0:T(8,128)S(1)} %broadcast_select_fusion), channel_id=1, source_target_pairs={{0,1},{4,5},{2,3},{6,7}} | collective-permute-start | bytes 983048 | tf_op jit(solution)/shard_map/ppermute | solution.py:494
  30.5 5.9 %collective-permute-start.4 = (f32[5,128,128]{2,1,0:T(8,128)S(1)}, f32[5,128,128]{2,1,0:T(8,128)S(1)}, u32[]{:S(2)}, u32[]{:S(2)}) collective-permute-start(f32[5,128,128]{2,1,0:T(8,128)S(1)} %broadcast_select_fusion.6), channel_id=1, source_target_pairs={{0,2},{16,18},{1,3},{17,19},{4,6},{20,22},{5,7},{21,23}} | collective-permute-start | bytes 983048 | tf_op jit(solution)/shard_map/ppermute | solution.py:494
  35.0 31.1 %collective-permute-start.7 = (f32[5,128,128]{2,1,0:T(8,128)S(1)}, f32[5,128,128]{2,1,0:T(8,128)S(1)}, u32[]{:S(2)}, u32[]{:S(2)}) collective-permute-start(f32[5,128,128]{2,1,0:T(8,128)S(1)} %broadcast_select_fusion.1), channel_id=1, source_target_pairs={{0,16},{4,20},{2,18},{6,22},{1,17},{5,21},{3,19},{7,23}} | collective-permute-start | bytes 983048 | tf_op jit(solution)/shard_map/ppermute | solution.py:494
  66.1 9.6 %collective-permute-start.8 = (f32[5,128,128]{2,1,0:T(8,128)S(1)}, f32[5,128,128]{2,1,0:T(8,128)S(1)}, u32[]{:S(2)}, u32[]{:S(2)}) collective-permute-start(f32[5,128,128]{2,1,0:T(8,128)S(1)} %broadcast_select_fusion.7), channel_id=1, source_target_pairs={{0,8},{16,24},{1,9},{17,25},{4,12},{20,28},{5,13},{21,29},{2,10},{... | collective-permute-start | bytes 983048 | tf_op jit(solution)/shard_map/ppermute | solution.py:494
  67.4 10.6 %collective-permute-start.9 = (f32[5,128,128]{2,1,0:T(8,128)S(1)}, f32[5,128,128]{2,1,0:T(8,128)S(1)}, u32[]{:S(2)}, u32[]{:S(2)}) collective-permute-start(f32[5,128,128]{2,1,0:T(8,128)S(1)} %broadcast_select_fusion.2), channel_id=1, source_target_pairs={{0,8},{4,12},{2,10},{6,14},{1,9},{5,13},{3,11},{7,15},{16,24},{20,... | collective-permute-start | bytes 983048 | tf_op jit(solution)/shard_map/ppermute | solution.py:494
  68.8 38.6 %collective-permute-start.11 = (f32[512,512]{1,0:T(8,128)}, f32[512,512]{1,0:T(8,128)S(1)}, u32[]{:S(2)}, u32[]{:S(2)}) collective-permute-start(f32[512,512]{1,0:T(8,128)} %get-tuple-element.65), channel_id=1, source_target_pairs={{0,3},{1,10},{2,17},{3,24},{4,7},{5,14},{6,21},{7,28}} | collective-permute-start | bytes 3145736 | tf_op jit(solution)/shard_map/ppermute | solution.py:505
  71.4 39.3 %collective-permute-start.12 = (f32[512,512]{1,0:T(8,128)}, f32[512,512]{1,0:T(8,128)S(1)}, u32[]{:S(2)}, u32[]{:S(2)}) collective-permute-start(f32[512,512]{1,0:T(8,128)} %get-tuple-element.66), channel_id=1, source_target_pairs={{0,2},{1,11},{2,16},{3,25},{4,6},{5,15},{6,20},{7,29}} | collective-permute-start | bytes 3145736 | tf_op jit(solution)/shard_map/ppermute | solution.py:505
  75.8 35.0 %collective-permute-start.13 = (f32[512,512]{1,0:T(8,128)}, f32[512,512]{1,0:T(8,128)}, u32[]{:S(2)}, u32[]{:S(2)}) collective-permute-start(f32[512,512]{1,0:T(8,128)} %get-tuple-element.67), channel_id=1, source_target_pairs={{0,1},{1,8},{2,19},{3,26},{4,5},{5,12},{6,23},{7,30}} | collective-permute-start | bytes 3145736 | tf_op jit(solution)/shard_map/ppermute | solution.py:505
  78.0 32.7 %collective-permute-start.14 = (f32[512,512]{1,0:T(8,128)}, f32[512,512]{1,0:T(8,128)}, u32[]{:S(2)}, u32[]{:S(2)}) collective-permute-start(f32[512,512]{1,0:T(8,128)} %get-tuple-element.68), channel_id=1, source_target_pairs={{0,0},{1,9},{2,18},{3,27},{4,4},{5,13},{6,22},{7,31}} | collective-permute-start | bytes 3145736 | tf_op jit(solution)/shard_map/ppermute | solution.py:505
  107.4 35.6 %collective-permute-start.17 = (f32[512,2048]{1,0:T(8,128)}, f32[512,2048]{1,0:T(8,128)}, u32[]{:S(2)}, u32[]{:S(2)}) collective-permute-start(f32[512,2048]{1,0:T(8,128)} %get-tuple-element.64), channel_id=1, source_target_pairs={{0,8},{1,9},{2,10},{3,11},{4,12},{5,13},{6,14},{7,15}} | collective-permute-start | bytes 12582920 | tf_op jit(solution)/shard_map/ppermute | solution.py:425
  110.7 32.2 %collective-permute-start.18 = (f32[512,2048]{1,0:T(8,128)}, f32[512,2048]{1,0:T(8,128)}, u32[]{:S(2)}, u32[]{:S(2)}) collective-permute-start(f32[512,2048]{1,0:T(8,128)} %collective-permute-done.10.refs_7_), channel_id=1, source_target_pairs={{16,24},{17,25},{18,26},{19,27},{20,28},{21,29},{22,30},{23,31}} | collective-permute-start | bytes 12582920 | tf_op jit(solution)/shard_map/ppermute | solution.py:425
  115.4 27.5 %copy-start = (f32[512,512]{1,0:T(8,128)}, f32[512,512]{1,0:T(8,128)S(1)}, u32[]{:S(2)}) copy-start(f32[512,512]{1,0:T(8,128)S(1)} %add_add_fusion.refs_4_) | copy-start | bytes 3145732
  115.4 22.6 %collective-permute-start.16 = (f32[512,512]{1,0:T(8,128)S(1)}, f32[512,512]{1,0:T(8,128)S(1)}, u32[]{:S(2)}, u32[]{:S(2)}) collective-permute-start(f32[512,512]{1,0:T(8,128)S(1)} %add_add_fusion.refs_4_), channel_id=1, source_target_pairs={{2,0},{4,2},{6,4},{7,6},{5,7},{3,5},{1,3},{0,1},{10,8},{12,10},{14... | collective-permute-start | bytes 3145736 | tf_op jit(solution)/shard_map/ppermute | solution.py:515
  115.5 23.7 %collective-permute-start.15 = (f32[512,512]{1,0:T(8,128)S(1)}, f32[512,512]{1,0:T(8,128)}, u32[]{:S(2)}, u32[]{:S(2)}) collective-permute-start(f32[512,512]{1,0:T(8,128)S(1)} %add_add_fusion.refs_4_), channel_id=1, source_target_pairs={{0,2},{2,4},{4,6},{6,7},{7,5},{5,3},{3,1},{1,0},{8,10},{10,12},{12... | collective-permute-start | bytes 3145736 | tf_op jit(solution)/shard_map/ppermute | solution.py:515
  138.0 20.3 %copy-start.3 = (f32[512,512]{1,0:T(8,128)}, f32[512,512]{1,0:T(8,128)S(1)}, u32[]{:S(2)}) copy-start(f32[512,512]{1,0:T(8,128)S(1)} %collective-permute-done.16.refs_5_) | copy-start | bytes 3145732
  139.2 25.6 %collective-permute-start.19 = (f32[512,512]{1,0:T(8,128)}, f32[512,512]{1,0:T(8,128)}, u32[]{:S(2)}, u32[]{:S(2)}) collective-permute-start(f32[512,512]{1,0:T(8,128)} %collective-permute-done.15.refs_4_), channel_id=1, source_target_pairs={{0,2},{2,4},{4,6},{6,7},{7,5},{5,3},{3,1},{1,0},{8,10},{10,12},{12... | collective-permute-start | bytes 3145736 | tf_op jit(solution)/shard_map/ppermute | solution.py:515
  141.7 25.5 %collective-permute-start.20 = (f32[512,512]{1,0:T(8,128)S(1)}, f32[512,512]{1,0:T(8,128)}, u32[]{:S(2)}, u32[]{:S(2)}) collective-permute-start(f32[512,512]{1,0:T(8,128)S(1)} %collective-permute-done.16.refs_5_), channel_id=1, source_target_pairs={{2,0},{4,2},{6,4},{7,6},{5,7},{3,5},{1,3},{0,1},{10,8},{12,10},{14... | collective-permute-start | bytes 3145736 | tf_op jit(solution)/shard_map/ppermute | solution.py:515
  167.2 32.4 %collective-permute-start.21 = (f32[512,512]{1,0:T(8,128)}, f32[512,512]{1,0:T(8,128)S(1)}, u32[]{:S(2)}, u32[]{:S(2)}) collective-permute-start(f32[512,512]{1,0:T(8,128)} %collective-permute-done.19.refs_6_), channel_id=1, source_target_pairs={{0,2},{2,4},{4,6},{6,7},{7,5},{5,3},{3,1},{1,0},{8,10},{10,12},{12... | collective-permute-start | bytes 3145736 | tf_op jit(solution)/shard_map/ppermute | solution.py:515
  168.2 31.4 %collective-permute-start.22 = (f32[512,512]{1,0:T(8,128)}, f32[512,512]{1,0:T(8,128)S(1)}, u32[]{:S(2)}, u32[]{:S(2)}) collective-permute-start(f32[512,512]{1,0:T(8,128)} %collective-permute-done.20.refs_7_), channel_id=1, source_target_pairs={{2,0},{4,2},{6,4},{7,6},{5,7},{3,5},{1,3},{0,1},{10,8},{12,10},{14... | collective-permute-start | bytes 3145736 | tf_op jit(solution)/shard_map/ppermute | solution.py:515
  199.6 2.2 copy-start.1
  199.6 2.2 copy-start.2
  199.7 19.9 %collective-permute-start.23 = (f32[256,512]{1,0:T(8,128)S(1)}, f32[256,512]{1,0:T(8,128)S(1)}, u32[]{:S(2)}, u32[]{:S(2)}) collective-permute-start(f32[256,512]{1,0:T(8,128)S(1)} %slice.6), channel_id=1, source_target_pairs={{0,2},{2,4},{4,6},{6,7},{7,5},{5,3},{3,1},{1,0},{8,10},{10,12},{12... | collective-permute-start | bytes 1572872 | tf_op jit(solution)/shard_map/ppermute | solution.py:557
  199.8 19.8 %collective-permute-start.24 = (f32[256,512]{1,0:T(8,128)S(1)}, f32[256,512]{1,0:T(8,128)}, u32[]{:S(2)}, u32[]{:S(2)}) collective-permute-start(f32[256,512]{1,0:T(8,128)S(1)} %slice.7), channel_id=1, source_target_pairs={{2,0},{4,2},{6,4},{7,6},{5,7},{3,5},{1,3},{0,1},{10,8},{12,10},{14... | collective-permute-start | bytes 1572872 | tf_op jit(solution)/shard_map/ppermute | solution.py:558

commit v5 on v4

--- a/solution.py
+++ b/solution.py
@@ -221,9 +221,11 @@
 
 
 def update_kernel(count, ahead, offset, tile, source_count, info, *refs):
-    factor_ref, inv_ref, inv_t_ref, matrix_ref = refs[:4]
-    chunks = refs[4 : 4 + count]
-    sources = refs[4 + count : 4 + count + source_count]
+    inv_t_ref, matrix_ref = refs[:2]
+    chunks = refs[2 : 2 + count]
+    sources = refs[2 + count : 2 + count + source_count]
+    if ahead:
+        factor_ref, inv_ref = refs[2 + count + source_count : 4 + count + source_count]
     out_ref = refs[-12 - ahead]
     across, rows, arrived, panel, panel3, left, right = refs[-11:-4]
     chunk_sems, row_sems, across_sem, out_sem = refs[-4:]
@@ -318,9 +320,11 @@
             panel3[:, NB + h * half : NB + (h + 1) * half] = low
             panel3[:, 2 * NB + h * half : 2 * NB + (h + 1) * half] = high
 
-        @pl.when(first_row)
-        def _():
-            panel[...] = factor_ref[...]
+        if ahead:
+
+            @pl.when(first_row)
+            def _():
+                panel[...] = factor_ref[...]
 
     if not ahead:
 
@@ -357,10 +361,12 @@
     square = pl.BlockSpec((NB, NB), whole)
     block = pl.BlockSpec((NB, tile), moving)
     across = jax.ShapeDtypeStruct((3 * NB, width), jnp.bfloat16)
-    in_specs = [square] * 3 + [block] + [ANYWHERE] * (count + len(sources))
-    operands = [info, factor, inv, inv_t, matrix, *chunks, *sources]
+    in_specs = [square, block] + [ANYWHERE] * (count + len(sources))
+    operands = [info, inv_t, matrix, *chunks, *sources]
     out_shape, out_specs, aliases = [jax.ShapeDtypeStruct(matrix.shape, jnp.float32)], [block], {}
     if ahead:
+        in_specs += [square] * 2
+        operands += [factor, inv]
         out_shape.append(across)
         out_specs.append(ANYWHERE)
     else:
@@ -418,7 +424,7 @@
     high = [cols_axis * bit for bit in bits_of(rows_axis)]
     core, across = high[:1], high[:0:-1]
     near, far = low[:1], low[:0:-1]
-    return across + near + far + core, far + near + across + core
+    return across + near + far + core, across + far + near + core
 
 
 def spread_apart(held, axis, bit):
@@ -435,7 +441,7 @@
     for r in range(cols_axis):
         h, target = divmod(r, rows_axis)
         pairs.append((r, target * cols_axis + h * rows_axis + (target ^ t)))
-    return pairs
+    return [(a, b) for a, b in pairs if a != b]
 
 
 def ring_shifts(cols_axis):
@@ -523,7 +529,8 @@
         for bit in other_bits:
             far = spread_apart(far, "row", bit)
         held = own + far
-        chunk = functools.reduce(jnp.add, pieces)
+        own_block = jnp.logical_and(index < cols_axis, index % rows_axis == 0)
+        chunk = jnp.where(own_block, blocks[0], functools.reduce(jnp.add, pieces))
         chunks = [[chunk]]
         going, coming = advance(chunk, chunk)
         work, chunk = tie(work, chunk)

time: 235 us -> 208 us (0.89)
  waiting for transfers between devices: 47.2 us -> 30.2 us
  starting transfers between devices: 57.4 us -> 49.5 us
    ppermute x10, waiting for transfers between devices: 36.2 us -> 14.2 us  [on_device(): came = [lax.ppermute(parts[n], both, stages[n][step][0]) for n in range(2)]]
    ppermute x4, starting transfers between devices: 18.7 us -> 10.7 us  [on_device(): lax.ppermute(blocks[t], both, scatter_pairs(t, rows_axis, cols_axis))]
    ppermute x3, waiting for transfers between devices: 0.01 us -> 7.93 us  [spread_apart(): lax.ppermute(v, axis, [(n, n | bit)])]
    ppermute x10, starting transfers between devices: 20.6 us -> 17.7 us  [on_device(): came = [lax.ppermute(parts[n], both, stages[n][step][0]) for n in range(2)]]
    ppermute x6, waiting for transfers between devices: 11 us -> 8.11 us  [advance(): return (lax.ppermute(going, 'col', up), lax.ppermute(coming, 'col', down))]
    ppermute x3, starting transfers between devices: 9.48 us -> 12.3 us  [spread_apart(): lax.ppermute(v, axis, [(n, n | bit)])]
    select_n x0 -> x1, other arithmetic: none -> 2.48 us  [on_device(): chunk = jnp.where(own_block, blocks[0], functools.reduce(jnp.add, pieces))]
  transfers between devices with their start and end apart: 25 -> 25, of which waited for: 9 -> 10; matrix products, arithmetic and copies ran while one was open for 2% -> 3% of each run, Pallas kernels for 46% -> 51%
where the time goes in v5:
time: 208 us; the launch traced here: 207 us
  Pallas kernels  119 us (57%)
  starting transfers between devices  49.5 us (24%)
  waiting for transfers between devices  30.2 us (15%)
  other arithmetic  6.36 us (3%)
    pallas_call x4, Pallas kernels, update(): pl.pallas_call(functools.partial(update_kernel, count, ahead, offset, til...  73.1 us
    pallas_call x1, Pallas kernels, factor_last(): pl.pallas_call(functools.partial(factor_last_kernel, COUNT // 2), out_sha...  19.5 us
    pallas_call x1, Pallas kernels, factor_first(): pl.pallas_call(functools.partial(factor_first_kernel, COUNT // 2), out_sh...  18.4 us
    ppermute x10, starting transfers between devices, on_device(): came = [lax.ppermute(parts[n], both, stages[n][step][0]) for n in range(2)]  17.7 us
    ppermute x10, waiting for transfers between devices, on_device(): came = [lax.ppermute(parts[n], both, stages[n][step][0]) for n in range(2)]  14.2 us
    ppermute x3, starting transfers between devices, spread_apart(): lax.ppermute(v, axis, [(n, n | bit)])  12.3 us
    ppermute x4, starting transfers between devices, on_device(): lax.ppermute(blocks[t], both, scatter_pairs(t, rows_axis, cols_axis))  10.7 us
    ppermute x6, waiting for transfers between devices, advance(): return (lax.ppermute(going, 'col', up), lax.ppermute(coming, 'col', down))  8.11 us
  transfers between devices with their start and end apart: 25, of which 10 were waited for; matrix products, arithmetic and copies ran while one was open for 3% of the time, Pallas kernels for 51%

profile of v5, /device:TPU:0, one launch (start us, length us, event | category | flops | bytes accessed | tf_op | source)
XLA Modules:
  0.0 207.0 jit_solution(7276402105133582256)
XLA Ops:
  0.0 2.1 %pack_corner.1 = (f32[5,128,128]{2,1,0:T(8,128)}, f32[5,128,128]{2,1,0:T(8,128)}) custom-call(f32[4096,2048]{1,0:T(8,128)} %refs_1_.7), custom_call_target="tpu_custom_call" | custom-call | tf_op jit(solution)/shard_map/pack_corner/pallas_call | solution.py:76
  2.1 5.0 %collective-permute-start = (f32[5,128,128]{2,1,0:T(8,128)}, f32[5,128,128]{2,1,0:T(8,128)S(1)}, u32[]{:S(2)}, u32[]{:S(2)}) collective-permute-start(f32[5,128,128]{2,1,0:T(8,128)} %get-tuple-element.48), channel_id=1, source_target_pairs={{0,16}} | collective-permute-start | bytes 983048 | tf_op jit(solution)/shard_map/ppermute | solution.py:500
  7.1 1.3 collective-permute-start.1
  8.4 5.9 %turn_blocks.1 = (f32[512,512]{1,0:T(8,128)}, f32[512,512]{1,0:T(8,128)}, f32[512,512]{1,0:T(8,128)}, f32[512,512]{1,0:T(8,128)}, f32[512,2048]{1,0:T(8,128)}) custom-call(f32[4096,2048]{1,0:T(8,128)} %refs_1_.7), custom_call_target="tpu_custom_call" | custom-call | tf_op jit(solution)/shard_map/turn_blocks/pallas_call | solution.py:95
  14.4 1.1 collective-permute-done.1
  15.5 6.3 %collective-permute-start.10 = (f32[512,2048]{1,0:T(8,128)}, f32[512,2048]{1,0:T(8,128)}, u32[]{:S(2)}, u32[]{:S(2)}) collective-permute-start(f32[512,2048]{1,0:T(8,128)} %get-tuple-element.64), channel_id=1, source_target_pairs={{0,16},{1,17},{2,18},{3,19},{4,20},{5,21},{6,22},{7,23}} | collective-permute-start | bytes 12582920 | tf_op jit(solution)/shard_map/ppermute | solution.py:431
  21.9 1.3 collective-permute-start.2
  23.2 1.3 collective-permute-start.5
  24.5 3.2 %collective-permute-done.2 = f32[5,128,128]{2,1,0:T(8,128)S(1)} collective-permute-done((f32[5,128,128]{2,1,0:T(8,128)S(1)}, f32[5,128,128]{2,1,0:T(8,128)S(1)}, u32[]{:S(2)}, u32[]{:S(2)}) %collective-permute-start.2) | collective-permute-done | bytes 327712 | tf_op jit(solution)/shard_map/ppermute | solution.py:500
  27.8 1.3 collective-permute-start.3
  29.1 1.3 collective-permute-start.6
  30.5 3.2 %collective-permute-done.3 = f32[5,128,128]{2,1,0:T(8,128)S(1)} collective-permute-done((f32[5,128,128]{2,1,0:T(8,128)S(1)}, f32[5,128,128]{2,1,0:T(8,128)S(1)}, u32[]{:S(2)}, u32[]{:S(2)}) %collective-permute-start.3) | collective-permute-done | bytes 327712 | tf_op jit(solution)/shard_map/ppermute | solution.py:500
  33.7 1.3 collective-permute-start.4
  35.0 2.2 %collective-permute-done.6 = f32[5,128,128]{2,1,0:T(8,128)S(1)} collective-permute-done((f32[5,128,128]{2,1,0:T(8,128)S(1)}, f32[5,128,128]{2,1,0:T(8,128)S(1)}, u32[]{:S(2)}, u32[]{:S(2)}) %collective-permute-start.6) | collective-permute-done | bytes 327712 | tf_op jit(solution)/shard_map/ppermute | solution.py:500
  37.2 2.3 %collective-permute-start.7 = (f32[5,128,128]{2,1,0:T(8,128)S(1)}, f32[5,128,128]{2,1,0:T(8,128)S(1)}, u32[]{:S(2)}, u32[]{:S(2)}) collective-permute-start(f32[5,128,128]{2,1,0:T(8,128)S(1)} %broadcast_select_fusion.1), channel_id=1, source_target_pairs={{0,1},{16,17},{4,5},{20,21},{2,3},{18,19},{6,7},{22,23}} | collective-permute-start | bytes 983048 | tf_op jit(solution)/shard_map/ppermute | solution.py:500
  39.5 1.2 collective-permute-done.4
  40.7 3.3 %collective-permute-done.7 = f32[5,128,128]{2,1,0:T(8,128)S(1)} collective-permute-done((f32[5,128,128]{2,1,0:T(8,128)S(1)}, f32[5,128,128]{2,1,0:T(8,128)S(1)}, u32[]{:S(2)}, u32[]{:S(2)}) %collective-permute-start.7) | collective-permute-done | bytes 327712 | tf_op jit(solution)/shard_map/ppermute | solution.py:500
  44.1 1.3 collective-permute-start.8
  45.4 1.3 collective-permute-start.9
  46.7 5.4 %collective-permute-start.11 = (f32[512,512]{1,0:T(8,128)}, f32[512,512]{1,0:T(8,128)S(1)}, u32[]{:S(2)}, u32[]{:S(2)}) collective-permute-start(f32[512,512]{1,0:T(8,128)} %get-tuple-element.65), channel_id=1, source_target_pairs={{0,3},{1,10},{2,17},{3,24},{4,7},{5,14},{6,21},{7,28}} | collective-permute-start | bytes 3145736 | tf_op jit(solution)/shard_map/ppermute | solution.py:511
  52.1 1.4 collective-permute-start.12
  53.5 2.3 %collective-permute-start.13 = (f32[512,512]{1,0:T(8,128)}, f32[512,512]{1,0:T(8,128)}, u32[]{:S(2)}, u32[]{:S(2)}) collective-permute-start(f32[512,512]{1,0:T(8,128)} %get-tuple-element.67), channel_id=1, source_target_pairs={{0,1},{1,8},{2,19},{3,26},{4,5},{5,12},{6,23},{7,30}} | collective-permute-start | bytes 3145736 | tf_op jit(solution)/shard_map/ppermute | solution.py:511
  55.8 1.7 collective-permute-start.14
  57.4 0.8 broadcast_select_fusion.9.first_ref
  58.2 0.8 broadcast_select_fusion.8.second_ref
  58.9 18.4 %factor_first.1 = (f32[512,512]{1,0:T(8,128)}, f32[512,512]{1,0:T(8,128)}) custom-call(f32[5,128,128]{2,1,0:T(8,128)} %broadcast_select_fusion.9.first_ref, f32[5,128,128]{2,1,0:T(8,128)} %broadcast_select_fusion.8.second_ref), custom_call_target="tpu_custom_call" | custom-call | flops 268435456 | bytes 4194304 | tf_op jit(solution)/shard_map/factor_first/pallas_call | solution.py:200
  77.3 3.3 %collective-permute-start.17 = (f32[512,2048]{1,0:T(8,128)}, f32[512,2048]{1,0:T(8,128)}, u32[]{:S(2)}, u32[]{:S(2)}) collective-permute-start(f32[512,2048]{1,0:T(8,128)} %get-tuple-element.64), channel_id=1, source_target_pairs={{0,8},{1,9},{2,10},{3,11},{4,12},{5,13},{6,14},{7,15}} | collective-permute-start | bytes 12582920 | tf_op jit(solution)/shard_map/ppermute | solution.py:431
  80.7 7.9 %collective-permute-done.10.refs_5_ = f32[512,2048]{1,0:T(8,128)} collective-permute-done((f32[512,2048]{1,0:T(8,128)}, f32[512,2048]{1,0:T(8,128)}, u32[]{:S(2)}, u32[]{:S(2)}) %collective-permute-start.10) | collective-permute-done | bytes 4194336 | tf_op jit(solution)/shard_map/ppermute | solution.py:431
  88.6 2.6 %collective-permute-start.18 = (f32[512,2048]{1,0:T(8,128)}, f32[512,2048]{1,0:T(8,128)}, u32[]{:S(2)}, u32[]{:S(2)}) collective-permute-start(f32[512,2048]{1,0:T(8,128)} %collective-permute-done.10.refs_5_), channel_id=1, source_target_pairs={{16,24},{17,25},{18,26},{19,27},{20,28},{21,29},{22,30},{23,31}} | collective-permute-start | bytes 12582920 | tf_op jit(solution)/shard_map/ppermute | solution.py:431
  91.2 2.5 %add_select_fusion.refs_2_ = f32[512,512]{1,0:T(8,128)S(1)} fusion(f32[512,512]{1,0:T(8,128)} %get-tuple-element.68, f32[512,512]{1,0:T(8,128)} %collective-permute-done.14, f32[512,512]{1,0:T(8,128)} %collective-permute-done.13, f32[512,512]{1,0:T(8,128)S(1)} %collective-permute-done.11, f32[512,512]{1,0:T(8,128)S(1)} %collective-permute-done.12, pred[]{:T(512)S(6)} %and.37), kind=kLoop, calls=%fused_computation.1 | loop fusion | flops 1048576 | bytes 6291457 | tf_op jit(solution)/shard_map/jit(_where)/select_n | solution.py:533
  93.7 0.1 collective-permute-start.16
  93.8 2.0 collective-permute-start.15
  95.8 19.5 %factor_last.1 = (f32[512,512]{1,0:T(8,128)}, f32[512,512]{1,0:T(8,128)}, f32[512,512]{1,0:T(8,128)}) custom-call(f32[512,512]{1,0:T(8,128)} %get-tuple-element.74.work_in, f32[512,512]{1,0:T(8,128)} %get-tuple-element.75.inv_t_in), custom_call_target="tpu_custom_call" | custom-call | flops 268435456 | bytes 4194304 | tf_op jit(solution)/shard_map/factor_last/pallas_call | solution.py:212
  115.3 1.0 collective-permute-done.15.refs_2_
  116.3 2.6 %collective-permute-start.19 = (f32[512,512]{1,0:T(8,128)}, f32[512,512]{1,0:T(8,128)}, u32[]{:S(2)}, u32[]{:S(2)}) collective-permute-start(f32[512,512]{1,0:T(8,128)} %collective-permute-done.15.refs_2_), channel_id=1, source_target_pairs={{0,2},{2,4},{4,6},{6,7},{7,5},{5,3},{3,1},{1,0},{8,10},{10,12},{12... | collective-permute-start | bytes 3145736 | tf_op jit(solution)/shard_map/ppermute | solution.py:521
  118.9 0.0 collective-permute-start.20
  118.9 1.2 dynamic-slice_bitcast_fusion.info
  120.1 15.4 %update_rows.4 = (f32[4096,2048]{1,0:T(8,128)}, bf16[1536,2048]{1,0:T(8,128)(2,1)}) custom-call(s32[10]{0:T(128)} %dynamic-slice_bitcast_fusion.info, f32[512,512]{1,0:T(8,128)} %get-tuple-element.76.refs_0_, f32[4096,2048]{1,0:T(8,128)} %refs_1_.7, f32[512,512]{1,0:T(8,128)} %copy-done, f32[4096,2048]{1,0:T(8,128)} %refs_1_.7, ...), custom_call_target="tpu_custom_call" | custom-call | flops 9663676416 | bytes 8388608 | tf_op jit(solution)/shard_map/update_rows/pallas_call | solution.py:376
  135.5 5.3 %collective-permute-done.19.refs_4_ = f32[512,512]{1,0:T(8,128)} collective-permute-done((f32[512,512]{1,0:T(8,128)}, f32[512,512]{1,0:T(8,128)}, u32[]{:S(2)}, u32[]{:S(2)}) %collective-permute-start.19) | collective-permute-done | bytes 1048608 | tf_op jit(solution)/shard_map/ppermute | solution.py:521
  140.7 1.9 collective-permute-done.20.refs_5_
  142.6 0.6 collective-permute-start.21
  143.2 1.4 collective-permute-start.22
  144.7 29.7 %update_rows.5.refs_5_ = f32[4096,2048]{1,0:T(8,128)} custom-call(s32[10]{0:T(128)} %dynamic-slice_bitcast_fusion.info, f32[512,512]{1,0:T(8,128)} %get-tuple-element.76.refs_0_, f32[4096,2048]{1,0:T(8,128)} %refs_1_.7, f32[512,512]{1,0:T(8,128)} %collective-permute-done.15.refs_2_, f32[512,512]{1,0:T(8,128)} %copy-done.3, ...), custom_call_target="tpu_custom_call", output_to_operand_aliasing={{}: (8, {})} | custom-call | flops 19327352832 | bytes 33554432 | tf_op jit(solution)/shard_map/update_rows/pallas_call | solution.py:376
  174.5 0.1 collective-permute-start.23
  174.6 2.0 collective-permute-start.24
  176.6 17.2 %update_rows.6.refs_4_ = f32[4096,2048]{1,0:T(8,128)} custom-call(s32[10]{0:T(128)} %dynamic-slice_bitcast_fusion.info, f32[512,512]{1,0:T(8,128)} %get-tuple-element.76.refs_0_, f32[4096,2048]{1,0:T(8,128)} %refs_1_.7, f32[512,512]{1,0:T(8,128)} %copy-done.1, f32[512,512]{1,0:T(8,128)} %copy-done.2, ...), custom_call_target="tpu_custom_call", output_to_operand_aliasing={{}: (6, {})} | custom-call | flops 9663676416 | bytes 16777216 | tf_op jit(solution)/shard_map/update_rows/pallas_call | solution.py:376
  193.8 2.1 %pad_maximum_fusion.refs_2_ = f32[512,512]{1,0:T(8,128)} fusion(f32[256,512]{1,0:T(8,128)} %collective-permute-done.24, f32[256,512]{1,0:T(8,128)S(1)} %collective-permute-done.23), kind=kLoop, calls=%fused_computation | loop fusion | flops 262144 | bytes 2097152 | tf_op jit(solution)/shard_map/concatenate | solution.py:569
  195.9 10.9 %update_rows.7 = f32[4096,2048]{1,0:T(8,128)} custom-call(s32[10]{0:T(128)} %dynamic-slice_bitcast_fusion.info, f32[512,512]{1,0:T(8,128)} %get-tuple-element.76.refs_0_, f32[4096,2048]{1,0:T(8,128)} %refs_1_.7, f32[512,512]{1,0:T(8,128)} %pad_maximum_fusion.refs_2_, ...), custom_call_target="tpu_custom_call", output_to_operand_aliasing={{}: (5, {})} | custom-call | flops 4831838208 | bytes 8388608 | tf_op jit(solution)/shard_map/update_rows/pallas_call | solution.py:376
  (37 shorter events, 0.4 us)
Async XLA Ops:
  2.1 12.2 %copy-start.5 = (f32[5,128,128]{2,1,0:T(8,128)S(1)}, f32[5,128,128]{2,1,0:T(8,128)}, u32[]{:S(2)}) copy-start(f32[5,128,128]{2,1,0:T(8,128)} %get-tuple-element.48) | copy-start | bytes 983044
  2.1 13.4 %copy-start.4 = (f32[5,128,128]{2,1,0:T(8,128)S(1)}, f32[5,128,128]{2,1,0:T(8,128)}, u32[]{:S(2)}) copy-start(f32[5,128,128]{2,1,0:T(8,128)} %get-tuple-element.49) | copy-start | bytes 983044
  2.1 12.2 %collective-permute-start = (f32[5,128,128]{2,1,0:T(8,128)}, f32[5,128,128]{2,1,0:T(8,128)S(1)}, u32[]{:S(2)}, u32[]{:S(2)}) collective-permute-start(f32[5,128,128]{2,1,0:T(8,128)} %get-tuple-element.48), channel_id=1, source_target_pairs={{0,16}} | collective-permute-start | bytes 983048 | tf_op jit(solution)/shard_map/ppermute | solution.py:500
  7.1 8.4 %collective-permute-start.1 = (f32[5,128,128]{2,1,0:T(8,128)}, f32[5,128,128]{2,1,0:T(8,128)S(1)}, u32[]{:S(2)}, u32[]{:S(2)}) collective-permute-start(f32[5,128,128]{2,1,0:T(8,128)} %get-tuple-element.49), channel_id=1, source_target_pairs={{0,16}} | collective-permute-start | bytes 983048 | tf_op jit(solution)/shard_map/ppermute | solution.py:500
  15.5 73.1 %collective-permute-start.10 = (f32[512,2048]{1,0:T(8,128)}, f32[512,2048]{1,0:T(8,128)}, u32[]{:S(2)}, u32[]{:S(2)}) collective-permute-start(f32[512,2048]{1,0:T(8,128)} %get-tuple-element.64), channel_id=1, source_target_pairs={{0,16},{1,17},{2,18},{3,19},{4,20},{5,21},{6,22},{7,23}} | collective-permute-start | bytes 12582920 | tf_op jit(solution)/shard_map/ppermute | solution.py:431
  21.9 5.9 %collective-permute-start.2 = (f32[5,128,128]{2,1,0:T(8,128)S(1)}, f32[5,128,128]{2,1,0:T(8,128)S(1)}, u32[]{:S(2)}, u32[]{:S(2)}) collective-permute-start(f32[5,128,128]{2,1,0:T(8,128)S(1)} %broadcast_select_fusion.4), channel_id=1, source_target_pairs={{0,1},{16,17}} | collective-permute-start | bytes 983048 | tf_op jit(solution)/shard_map/ppermute | solution.py:500
  23.2 5.9 %collective-permute-start.5 = (f32[5,128,128]{2,1,0:T(8,128)S(1)}, f32[5,128,128]{2,1,0:T(8,128)S(1)}, u32[]{:S(2)}, u32[]{:S(2)}) collective-permute-start(f32[5,128,128]{2,1,0:T(8,128)S(1)} %broadcast_select_fusion.3), channel_id=1, source_target_pairs={{0,4},{16,20}} | collective-permute-start | bytes 983048 | tf_op jit(solution)/shard_map/ppermute | solution.py:500
  27.8 5.9 %collective-permute-start.3 = (f32[5,128,128]{2,1,0:T(8,128)S(1)}, f32[5,128,128]{2,1,0:T(8,128)S(1)}, u32[]{:S(2)}, u32[]{:S(2)}) collective-permute-start(f32[5,128,128]{2,1,0:T(8,128)S(1)} %broadcast_select_fusion.5), channel_id=1, source_target_pairs={{0,4},{16,20},{1,5},{17,21}} | collective-permute-start | bytes 983048 | tf_op jit(solution)/shard_map/ppermute | solution.py:500
  29.1 8.0 %collective-permute-start.6 = (f32[5,128,128]{2,1,0:T(8,128)S(1)}, f32[5,128,128]{2,1,0:T(8,128)S(1)}, u32[]{:S(2)}, u32[]{:S(2)}) collective-permute-start(f32[5,128,128]{2,1,0:T(8,128)S(1)} %broadcast_select_fusion), channel_id=1, source_target_pairs={{0,2},{16,18},{4,6},{20,22}} | collective-permute-start | bytes 983048 | tf_op jit(solution)/shard_map/ppermute | solution.py:500
  33.7 7.0 %collective-permute-start.4 = (f32[5,128,128]{2,1,0:T(8,128)S(1)}, f32[5,128,128]{2,1,0:T(8,128)S(1)}, u32[]{:S(2)}, u32[]{:S(2)}) collective-permute-start(f32[5,128,128]{2,1,0:T(8,128)S(1)} %broadcast_select_fusion.6), channel_id=1, source_target_pairs={{0,2},{16,18},{1,3},{17,19},{4,6},{20,22},{5,7},{21,23}} | collective-permute-start | bytes 983048 | tf_op jit(solution)/shard_map/ppermute | solution.py:500
  37.2 6.8 %collective-permute-start.7 = (f32[5,128,128]{2,1,0:T(8,128)S(1)}, f32[5,128,128]{2,1,0:T(8,128)S(1)}, u32[]{:S(2)}, u32[]{:S(2)}) collective-permute-start(f32[5,128,128]{2,1,0:T(8,128)S(1)} %broadcast_select_fusion.1), channel_id=1, source_target_pairs={{0,1},{16,17},{4,5},{20,21},{2,3},{18,19},{6,7},{22,23}} | collective-permute-start | bytes 983048 | tf_op jit(solution)/shard_map/ppermute | solution.py:500
  44.1 9.4 %collective-permute-start.8 = (f32[5,128,128]{2,1,0:T(8,128)S(1)}, f32[5,128,128]{2,1,0:T(8,128)S(1)}, u32[]{:S(2)}, u32[]{:S(2)}) collective-permute-start(f32[5,128,128]{2,1,0:T(8,128)S(1)} %broadcast_select_fusion.7), channel_id=1, source_target_pairs={{0,8},{16,24},{1,9},{17,25},{4,12},{20,28},{5,13},{21,29},{2,10},{... | collective-permute-start | bytes 983048 | tf_op jit(solution)/shard_map/ppermute | solution.py:500
  45.4 10.4 %collective-permute-start.9 = (f32[5,128,128]{2,1,0:T(8,128)S(1)}, f32[5,128,128]{2,1,0:T(8,128)S(1)}, u32[]{:S(2)}, u32[]{:S(2)}) collective-permute-start(f32[5,128,128]{2,1,0:T(8,128)S(1)} %broadcast_select_fusion.2), channel_id=1, source_target_pairs={{0,8},{16,24},{4,12},{20,28},{2,10},{18,26},{6,14},{22,30},{1,9},{... | collective-permute-start | bytes 983048 | tf_op jit(solution)/shard_map/ppermute | solution.py:500
  46.7 30.6 %collective-permute-start.11 = (f32[512,512]{1,0:T(8,128)}, f32[512,512]{1,0:T(8,128)S(1)}, u32[]{:S(2)}, u32[]{:S(2)}) collective-permute-start(f32[512,512]{1,0:T(8,128)} %get-tuple-element.65), channel_id=1, source_target_pairs={{0,3},{1,10},{2,17},{3,24},{4,7},{5,14},{6,21},{7,28}} | collective-permute-start | bytes 3145736 | tf_op jit(solution)/shard_map/ppermute | solution.py:511
  52.1 28.5 %collective-permute-start.12 = (f32[512,512]{1,0:T(8,128)}, f32[512,512]{1,0:T(8,128)S(1)}, u32[]{:S(2)}, u32[]{:S(2)}) collective-permute-start(f32[512,512]{1,0:T(8,128)} %get-tuple-element.66), channel_id=1, source_target_pairs={{0,2},{1,11},{2,16},{3,25},{4,6},{5,15},{6,20},{7,29}} | collective-permute-start | bytes 3145736 | tf_op jit(solution)/shard_map/ppermute | solution.py:511
  53.5 27.2 %collective-permute-start.13 = (f32[512,512]{1,0:T(8,128)}, f32[512,512]{1,0:T(8,128)}, u32[]{:S(2)}, u32[]{:S(2)}) collective-permute-start(f32[512,512]{1,0:T(8,128)} %get-tuple-element.67), channel_id=1, source_target_pairs={{0,1},{1,8},{2,19},{3,26},{4,5},{5,12},{6,23},{7,30}} | collective-permute-start | bytes 3145736 | tf_op jit(solution)/shard_map/ppermute | solution.py:511
  55.8 24.9 %collective-permute-start.14 = (f32[512,512]{1,0:T(8,128)}, f32[512,512]{1,0:T(8,128)}, u32[]{:S(2)}, u32[]{:S(2)}) collective-permute-start(f32[512,512]{1,0:T(8,128)} %get-tuple-element.68), channel_id=1, source_target_pairs={{1,9},{2,18},{3,27},{5,13},{6,22},{7,31}} | collective-permute-start | bytes 3145736 | tf_op jit(solution)/shard_map/ppermute | solution.py:511
  77.3 42.8 %collective-permute-start.17 = (f32[512,2048]{1,0:T(8,128)}, f32[512,2048]{1,0:T(8,128)}, u32[]{:S(2)}, u32[]{:S(2)}) collective-permute-start(f32[512,2048]{1,0:T(8,128)} %get-tuple-element.64), channel_id=1, source_target_pairs={{0,8},{1,9},{2,10},{3,11},{4,12},{5,13},{6,14},{7,15}} | collective-permute-start | bytes 12582920 | tf_op jit(solution)/shard_map/ppermute | solution.py:431
  88.6 31.5 %collective-permute-start.18 = (f32[512,2048]{1,0:T(8,128)}, f32[512,2048]{1,0:T(8,128)}, u32[]{:S(2)}, u32[]{:S(2)}) collective-permute-start(f32[512,2048]{1,0:T(8,128)} %collective-permute-done.10.refs_5_), channel_id=1, source_target_pairs={{16,24},{17,25},{18,26},{19,27},{20,28},{21,29},{22,30},{23,31}} | collective-permute-start | bytes 12582920 | tf_op jit(solution)/shard_map/ppermute | solution.py:431
  93.7 26.4 %copy-start = (f32[512,512]{1,0:T(8,128)}, f32[512,512]{1,0:T(8,128)S(1)}, u32[]{:S(2)}) copy-start(f32[512,512]{1,0:T(8,128)S(1)} %add_select_fusion.refs_2_) | copy-start | bytes 3145732
  93.7 21.6 %collective-permute-start.16 = (f32[512,512]{1,0:T(8,128)S(1)}, f32[512,512]{1,0:T(8,128)S(1)}, u32[]{:S(2)}, u32[]{:S(2)}) collective-permute-start(f32[512,512]{1,0:T(8,128)S(1)} %add_select_fusion.refs_2_), channel_id=1, source_target_pairs={{2,0},{4,2},{6,4},{7,6},{5,7},{3,5},{1,3},{0,1},{10,8},{12,10},{14... | collective-permute-start | bytes 3145736 | tf_op jit(solution)/shard_map/ppermute | solution.py:521
  93.8 22.5 %collective-permute-start.15 = (f32[512,512]{1,0:T(8,128)S(1)}, f32[512,512]{1,0:T(8,128)}, u32[]{:S(2)}, u32[]{:S(2)}) collective-permute-start(f32[512,512]{1,0:T(8,128)S(1)} %add_select_fusion.refs_2_), channel_id=1, source_target_pairs={{0,2},{2,4},{4,6},{6,7},{7,5},{5,3},{3,1},{1,0},{8,10},{10,12},{12... | collective-permute-start | bytes 3145736 | tf_op jit(solution)/shard_map/ppermute | solution.py:521
  115.3 20.2 %copy-start.3 = (f32[512,512]{1,0:T(8,128)}, f32[512,512]{1,0:T(8,128)S(1)}, u32[]{:S(2)}) copy-start(f32[512,512]{1,0:T(8,128)S(1)} %collective-permute-done.16.refs_3_) | copy-start | bytes 3145732
  116.3 24.5 %collective-permute-start.19 = (f32[512,512]{1,0:T(8,128)}, f32[512,512]{1,0:T(8,128)}, u32[]{:S(2)}, u32[]{:S(2)}) collective-permute-start(f32[512,512]{1,0:T(8,128)} %collective-permute-done.15.refs_2_), channel_id=1, source_target_pairs={{0,2},{2,4},{4,6},{6,7},{7,5},{5,3},{3,1},{1,0},{8,10},{10,12},{12... | collective-permute-start | bytes 3145736 | tf_op jit(solution)/shard_map/ppermute | solution.py:521
  118.9 23.8 %collective-permute-start.20 = (f32[512,512]{1,0:T(8,128)S(1)}, f32[512,512]{1,0:T(8,128)}, u32[]{:S(2)}, u32[]{:S(2)}) collective-permute-start(f32[512,512]{1,0:T(8,128)S(1)} %collective-permute-done.16.refs_3_), channel_id=1, source_target_pairs={{2,0},{4,2},{6,4},{7,6},{5,7},{3,5},{1,3},{0,1},{10,8},{12,10},{14... | collective-permute-start | bytes 3145736 | tf_op jit(solution)/shard_map/ppermute | solution.py:521
  142.6 31.8 %collective-permute-start.21 = (f32[512,512]{1,0:T(8,128)}, f32[512,512]{1,0:T(8,128)S(1)}, u32[]{:S(2)}, u32[]{:S(2)}) collective-permute-start(f32[512,512]{1,0:T(8,128)} %collective-permute-done.19.refs_4_), channel_id=1, source_target_pairs={{0,2},{2,4},{4,6},{6,7},{7,5},{5,3},{3,1},{1,0},{8,10},{10,12},{12... | collective-permute-start | bytes 3145736 | tf_op jit(solution)/shard_map/ppermute | solution.py:521
  143.2 31.2 %collective-permute-start.22 = (f32[512,512]{1,0:T(8,128)}, f32[512,512]{1,0:T(8,128)S(1)}, u32[]{:S(2)}, u32[]{:S(2)}) collective-permute-start(f32[512,512]{1,0:T(8,128)} %collective-permute-done.20.refs_5_), channel_id=1, source_target_pairs={{2,0},{4,2},{6,4},{7,6},{5,7},{3,5},{1,3},{0,1},{10,8},{12,10},{14... | collective-permute-start | bytes 3145736 | tf_op jit(solution)/shard_map/ppermute | solution.py:521
  174.4 2.2 %copy-start.1 = (f32[512,512]{1,0:T(8,128)}, f32[512,512]{1,0:T(8,128)S(1)}, u32[]{:S(2)}) copy-start(f32[512,512]{1,0:T(8,128)S(1)} %collective-permute-done.21.refs_2_) | copy-start | bytes 3145732
  174.4 2.2 %copy-start.2 = (f32[512,512]{1,0:T(8,128)}, f32[512,512]{1,0:T(8,128)S(1)}, u32[]{:S(2)}) copy-start(f32[512,512]{1,0:T(8,128)S(1)} %collective-permute-done.22.refs_3_) | copy-start | bytes 3145732
  174.5 19.3 %collective-permute-start.23 = (f32[256,512]{1,0:T(8,128)S(1)}, f32[256,512]{1,0:T(8,128)S(1)}, u32[]{:S(2)}, u32[]{:S(2)}) collective-permute-start(f32[256,512]{1,0:T(8,128)S(1)} %slice.6), channel_id=1, source_target_pairs={{0,2},{2,4},{4,6},{6,7},{7,5},{5,3},{3,1},{1,0},{8,10},{10,12},{12... | collective-permute-start | bytes 1572872 | tf_op jit(solution)/shard_map/ppermute | solution.py:564
  174.6 19.2 %collective-permute-start.24 = (f32[256,512]{1,0:T(8,128)S(1)}, f32[256,512]{1,0:T(8,128)}, u32[]{:S(2)}, u32[]{:S(2)}) collective-permute-start(f32[256,512]{1,0:T(8,128)S(1)} %slice.7), channel_id=1, source_target_pairs={{2,0},{4,2},{6,4},{7,6},{5,7},{3,5},{1,3},{0,1},{10,8},{12,10},{14... | collective-permute-start | bytes 1572872 | tf_op jit(solution)/shard_map/ppermute | solution.py:565
